TPU v7x, 32 devices: a whole 2x2x4 slice. The times are simulated.
32 devices in a mesh: seq: 8 (over z, y), head: 4 (over x, core).
Axes of the slice: x: 2, y: 2, z: 4, core: 2. Of those that a mesh axis runs over, the one named last changes fastest.
Arguments:
- block_input: bfloat16 [4096, 2048], P('seq'), may hold values from -6 to 6
- cotangent: bfloat16 [4096, 2048], P('seq'), may hold values from -6 to 6
- lengths: int32 [2], replicated, may hold values from 1536 to 2560, as said below
- proj_master: float32 [4, 2048, 2048], P(None, 'seq', 'head'), may hold values from -0.125 to 0.125
- proj_first: float32 [4, 2048, 2048], P(None, 'seq', 'head'), as said below
- proj_second: float32 [4, 2048, 2048], P(None, 'seq', 'head'), as said below
- beta_master: float32 [2048, 16], P('seq', 'head'), may hold values from -0.125 to 0.125
- beta_first: float32 [2048, 16], P('seq', 'head'), may hold values from -224 to 224
- beta_second: float32 [2048, 16], P('seq', 'head'), may hold values from 5386.24 to 21544.96
- conv_master: float32 [3, 4, 2048], P(None, None, ('head', 'seq')), may hold values from -3 to 3
- conv_first: float32 [3, 4, 2048], P(None, None, ('head', 'seq')), as said below
- conv_second: float32 [3, 4, 2048], P(None, None, ('head', 'seq')), as said below
- out_master: float32 [2048, 2048], P('head', 'seq'), may hold values from -0.125 to 0.125
- out_first: float32 [2048, 2048], P('head', 'seq'), may hold values from -28 to 28
- out_second: float32 [2048, 2048], P('head', 'seq'), may hold values from 105.6768 to 421.888
- mlp_master: float32 [2, 2048, 5632], P(None, 'seq', 'head'), may hold values from -0.125 to 0.125
- mlp_first: float32 [2, 2048, 5632], P(None, 'seq', 'head'), may hold values from -12 to 12
- mlp_second: float32 [2, 2048, 5632], P(None, 'seq', 'head'), may hold values from 19.37408 to 77.4144
- down_master: float32 [5632, 2048], P('head', 'seq'), may hold values from -0.078125 to 0.078125
- down_first: float32 [5632, 2048], P('head', 'seq'), may hold values from -24 to 24
- down_second: float32 [5632, 2048], P('head', 'seq'), may hold values from 77.4144 to 310.0672
- gains_master: float32 [4224], P('seq'), may hold values from 0.5 to 1.5
- gains_first: float32 [4224], P('seq'), as said below
- gains_second: float32 [4224], P('seq'), as said below
Outputs:
- result: float32 [4096, 2048], P('seq')
- input_grad: float32 [4096, 2048], P('seq')
- proj_new: float32 [4, 2048, 2048], P(None, 'seq', 'head')
- proj_first_new: float32 [4, 2048, 2048], P(None, 'seq', 'head')
- proj_second_new: float32 [4, 2048, 2048], P(None, 'seq', 'head')
- proj_copy: bfloat16 [4, 2048, 2048], P(None, 'seq', 'head')
- beta_new: float32 [2048, 16], P('seq', 'head')
- beta_first_new: float32 [2048, 16], P('seq', 'head')
- beta_second_new: float32 [2048, 16], P('seq', 'head')
- beta_copy: bfloat16 [2048, 16], P('seq', 'head')
- conv_new: float32 [3, 4, 2048], P(None, None, ('head', 'seq'))
- conv_first_new: float32 [3, 4, 2048], P(None, None, ('head', 'seq'))
- conv_second_new: float32 [3, 4, 2048], P(None, None, ('head', 'seq'))
- conv_copy: bfloat16 [3, 4, 2048], P(None, None, ('head', 'seq'))
- out_new: float32 [2048, 2048], P('head', 'seq')
- out_first_new: float32 [2048, 2048], P('head', 'seq')
- out_second_new: float32 [2048, 2048], P('head', 'seq')
- out_copy: bfloat16 [2048, 2048], P('head', 'seq')
- mlp_new: float32 [2, 2048, 5632], P(None, 'seq', 'head')
- mlp_first_new: float32 [2, 2048, 5632], P(None, 'seq', 'head')
- mlp_second_new: float32 [2, 2048, 5632], P(None, 'seq', 'head')
- mlp_copy: bfloat16 [2, 2048, 5632], P(None, 'seq', 'head')
- down_new: float32 [5632, 2048], P('head', 'seq')
- down_first_new: float32 [5632, 2048], P('head', 'seq')
- down_second_new: float32 [5632, 2048], P('head', 'seq')
- down_copy: bfloat16 [5632, 2048], P('head', 'seq')
- gains_new: float32 [4224], P('seq')
- gains_first_new: float32 [4224], P('seq')
- gains_second_new: float32 [4224], P('seq')
Inputs may be any that keep to these rules, and one draw needn't show every extreme that they name: lengths of sequence 0 and sequence 1 in order; both are multiples of 64 and they sum to 4096. `proj_first`: an optimizer state of both signs. `proj_second`: an optimizer state, positive. `conv_first`: an optimizer state of both signs. `conv_second`: an optimizer state, positive. `gains_first`: an optimizer state of both signs. `gains_second`: an optimizer state, positive.
All inputs are finite; a program needn't handle non-finite values.
Results may differ from a plain program's by a relative error of at most 0.024.
Values may be sent and summed in bfloat16 or wider, within the bound.
No kernel may reach another device: no remote copies, remote signals or barrier semaphores. Data moves between devices by JAX's collectives and lax.ppermute only.
A program may use at most 320 MiB of HBM per device.

v0:
```python
from functools import partial

import jax
import jax.numpy as jnp
from jax import lax
from jax.sharding import PartitionSpec as P

D = 2048
DK = 128
CONV = 4
SPAN = 64
STEP = 10


HIGHEST_PREC = lax.Precision.HIGHEST
eps_norm = 1e-05
eps_unit = 1e-06
beta_one = 0.9
beta_two = 0.95
eps_adam = 1e-08
rate_matrix = 0.04
rate_beta = 0.12
rate_down = 0.03
rate_conv = 0.3
rate_gains = 0.4
decay_matrix = 0.1


def passed_along(value, axis, steps):
    count = lax.axis_size(axis)
    leading, last = (max(0, -steps), min(count, count - steps))
    return lax.ppermute(value, axis, [(source, source + steps) for source in range(leading, last)])


def rms_norm(tensor, scale_gain):
    return (
        tensor
        * lax.rsqrt(jnp.mean(tensor * tensor, axis=-1, keepdims=True) + eps_norm)
        * scale_gain
    )


def gated(out_rows, gate_rows, gain_o):
    row_count, width_all = out_rows.shape
    per_head = out_rows.reshape(row_count, width_all // DK, DK)
    scaled = per_head * lax.rsqrt(jnp.mean(per_head * per_head, axis=-1, keepdims=True) + eps_norm)
    gating = jax.nn.silu(gate_rows.reshape(row_count, width_all // DK, DK))
    return (scaled * gain_o * gating).reshape(row_count, width_all)


def unit_heads(tensor):
    row_count, width_all = tensor.shape
    per_head = tensor.reshape(row_count, width_all // DK, DK)
    return per_head * lax.rsqrt(jnp.sum(per_head * per_head, axis=-1, keepdims=True) + eps_unit)


def mixing(valid, extended, conv_taps, logits):
    row_count = logits.shape[0]
    summed = jnp.zeros((3, row_count, extended.shape[2]), jnp.float32)
    for offset in range(CONV):
        summed = (
            summed
            + conv_taps[:, offset][:, None, :]
            * extended[:, offset : offset + row_count]
            * valid[None, :, offset : offset + 1]
        )
    activated = jax.nn.silu(summed)
    return (
        unit_heads(activated[0]),
        unit_heads(activated[1]),
        activated[2].reshape(row_count, -1, DK),
        jax.nn.sigmoid(logits),
    )


def swiglu(gate_up):
    return jax.nn.silu(gate_up[0]) * gate_up[1]


def to_spans(rows_in, span_count):
    return jnp.transpose(rows_in.reshape((span_count, SPAN) + rows_in.shape[1:]), (2, 0, 1, 3))


def from_spans(spanned):
    heads_loc, span_count, size_c, depth = spanned.shape
    return jnp.transpose(spanned, (1, 2, 0, 3)).reshape(span_count * size_c, heads_loc, depth)


def prepare(resets, key_c, value_c, beta_c):
    size_c = key_c.shape[2]
    heads_loc = key_c.shape[0]
    gram = jnp.einsum("hncd,hned->hnce", key_c, key_c, precision=HIGHEST_PREC)
    strict = jnp.tril(jnp.ones((size_c, size_c), jnp.float32), -1)
    system = jnp.eye(size_c, dtype=jnp.float32) + strict * beta_c[..., :, None] * gram
    w_key = lax.linalg.triangular_solve(
        system, beta_c[..., None] * key_c, left_side=True, lower=True
    )
    w_val = lax.linalg.triangular_solve(
        system, beta_c[..., None] * value_c, left_side=True, lower=True
    )
    transit = jnp.eye(DK, dtype=jnp.float32) - jnp.einsum(
        "hncd,hnce->hnde", w_key, key_c, precision=HIGHEST_PREC
    )
    adding = jnp.einsum("hncv,hnck->hnvk", w_val, key_c, precision=HIGHEST_PREC)

    def advance(carried, element):
        product, offset_map = carried
        step_t, step_b, reset_flag = element
        keep_flag = 1.0 - reset_flag
        product = product * keep_flag
        offset_map = offset_map * keep_flag
        moved = (
            jnp.matmul(product, step_t, precision=HIGHEST_PREC),
            jnp.matmul(offset_map, step_t, precision=HIGHEST_PREC) + step_b,
        )
        return (moved, (product, offset_map))

    initial = (
        jnp.broadcast_to(jnp.eye(DK, dtype=jnp.float32), (heads_loc, DK, DK)),
        jnp.zeros((heads_loc, DK, DK), jnp.float32),
    )
    ends, entering = lax.scan(
        advance,
        initial,
        (jnp.transpose(transit, (1, 0, 2, 3)), jnp.transpose(adding, (1, 0, 2, 3)), resets),
    )
    return (w_key, w_val, entering[0], entering[1], ends[0], ends[1])


def apply_state(query_c, key_c, w_key, w_val, p_span, b_span, p_dev, b_dev, state_in):
    size_c = query_c.shape[2]
    states = jnp.einsum("hvk,nhkj->hnvj", state_in, p_span, precision=HIGHEST_PREC) + jnp.transpose(
        b_span, (1, 0, 2, 3)
    )
    fixed_u = w_val - jnp.einsum("hnck,hnvk->hncv", w_key, states, precision=HIGHEST_PREC)
    inclusive = jnp.tril(jnp.ones((size_c, size_c), jnp.float32))
    scores = jnp.einsum("hncd,hned->hnce", query_c, key_c, precision=HIGHEST_PREC) * inclusive
    outputs = jnp.einsum("hnck,hnvk->hncv", query_c, states, precision=HIGHEST_PREC) + jnp.einsum(
        "hnce,hnev->hncv", scores, fixed_u, precision=HIGHEST_PREC
    )
    state_out = jnp.matmul(state_in, p_dev, precision=HIGHEST_PREC) + b_dev
    return (outputs, state_out)


def adam_update(master, first_m, second_m, gradient, step_rate, decay_rate):
    first_new = beta_one * first_m + (1.0 - beta_one) * gradient
    second_new = beta_two * second_m + (1.0 - beta_two) * gradient * gradient
    first_hat = first_new / (1.0 - beta_one**STEP)
    second_hat = second_new / (1.0 - beta_two**STEP)
    master_new = master - step_rate * (
        first_hat / (jnp.sqrt(second_hat) + eps_adam) + decay_rate * master
    )
    return (master_new, first_new, second_new)


def per_device(
    block_input,
    cotangent,
    lengths,
    proj_master,
    proj_first,
    proj_second,
    beta_master,
    beta_first,
    beta_second,
    conv_master,
    conv_first,
    conv_second,
    out_master,
    out_first,
    out_second,
    mlp_master,
    mlp_first,
    mlp_second,
    down_master,
    down_first,
    down_second,
    gains_master,
    gains_first,
    gains_second,
):
    w_proj, w_beta, w_conv, w_out, w_mlp, w_down, w_gains = (
        lax.all_gather(proj_master.astype(jnp.bfloat16), "seq", axis=1, tiled=True),
        lax.all_gather(beta_master.astype(jnp.bfloat16), "seq", axis=0, tiled=True),
        lax.all_gather(conv_master.astype(jnp.bfloat16), "seq", axis=2, tiled=True),
        lax.all_gather(out_master.astype(jnp.bfloat16), "seq", axis=1, tiled=True),
        lax.all_gather(mlp_master.astype(jnp.bfloat16), "seq", axis=1, tiled=True),
        lax.all_gather(down_master.astype(jnp.bfloat16), "seq", axis=1, tiled=True),
        lax.all_gather(gains_master.astype(jnp.bfloat16), "seq", axis=0, tiled=True),
    )
    gain_all = w_gains.astype(jnp.float32)
    gain_a = gain_all[:D]
    gain_m = gain_all[D : 2 * D]
    gain_o = gain_all[2 * D :]
    seq_index = lax.axis_index("seq")
    row_count = block_input.shape[0]
    span_count = row_count // SPAN
    width_loc = w_proj.shape[2]
    first_len = lengths[0]
    token_pos = seq_index * row_count + jnp.arange(row_count, dtype=jnp.int32)
    position = token_pos - first_len * (token_pos >= first_len).astype(jnp.int32)
    reach = CONV - 1 - jnp.arange(CONV, dtype=jnp.int32)
    valid = (position[:, None] >= reach[None, :]).astype(jnp.float32)
    span_pos = seq_index * row_count + SPAN * jnp.arange(span_count, dtype=jnp.int32)
    resets = ((span_pos == 0) | (span_pos == first_len)).astype(jnp.float32)
    x_full = block_input.astype(jnp.float32)
    hidden, norm_back = jax.vjp(rms_norm, x_full, gain_a)
    hidden_low = hidden.astype(jnp.bfloat16)
    projected = jnp.einsum("td,cde->cte", hidden_low, w_proj, preferred_element_type=jnp.float32)
    pre_conv = projected[:3].astype(jnp.bfloat16)
    gate_rows = projected[3]
    logits = jnp.dot(hidden_low, w_beta, preferred_element_type=jnp.float32)
    halo_rows = passed_along(pre_conv[:, row_count - (CONV - 1) :], "seq", 1)
    extended = jnp.concatenate([halo_rows, pre_conv], axis=1).astype(jnp.float32)
    mixed_out, mix_back = jax.vjp(
        partial(mixing, valid), extended, w_conv.astype(jnp.float32), logits
    )
    query_r, key_r, value_r, beta_r = mixed_out
    query_c = to_spans(query_r, span_count)
    key_c = to_spans(key_r, span_count)
    value_c = to_spans(value_r, span_count)
    beta_c = jnp.transpose(beta_r.reshape(span_count, SPAN, -1), (2, 0, 1))
    prepared, prep_back = jax.vjp(partial(prepare, resets), key_c, value_c, beta_c)
    w_key, w_val, p_span, b_span, p_dev, b_dev = prepared
    zero_stack = jnp.zeros_like(b_dev)

    def relay(turn, state_in):
        return passed_along(
            (jnp.matmul(state_in, p_dev, precision=HIGHEST_PREC) + b_dev).astype(jnp.bfloat16),
            "seq",
            1,
        ).astype(jnp.float32)

    state_in = lax.fori_loop(0, lax.axis_size("seq") - 1, relay, zero_stack)
    applied, apply_back = jax.vjp(
        apply_state, query_c, key_c, w_key, w_val, p_span, b_span, p_dev, b_dev, state_in
    )
    outputs_c, state_out = applied
    out_rows = from_spans(outputs_c).reshape(row_count, width_loc)
    normed, gate_back = jax.vjp(gated, out_rows, gate_rows, gain_o)
    mixed_low = normed.astype(jnp.bfloat16)
    attn_out = lax.psum(jnp.dot(mixed_low, w_out, preferred_element_type=jnp.float32), "head")
    x_one = x_full + attn_out
    h_two, norm_two_back = jax.vjp(rms_norm, x_one, gain_m)
    h_two_low = h_two.astype(jnp.bfloat16)
    gate_up = jnp.einsum("td,cdf->ctf", h_two_low, w_mlp, preferred_element_type=jnp.float32)
    activated, glu_back = jax.vjp(swiglu, gate_up)
    act_low = activated.astype(jnp.bfloat16)
    mlp_out = lax.psum(
        jnp.dot(act_low, w_down, preferred_element_type=jnp.float32).astype(jnp.bfloat16), "head"
    ).astype(jnp.float32)
    result = x_one + mlp_out
    grad_down = jnp.einsum("tf,td->fd", act_low, cotangent, preferred_element_type=jnp.float32)
    grad_act = jnp.einsum("td,fd->tf", cotangent, w_down, preferred_element_type=jnp.float32)
    grad_gate_up = glu_back(grad_act)[0].astype(jnp.bfloat16)
    grad_mlp = jnp.einsum(
        "td,ctf->cdf", h_two_low, grad_gate_up, preferred_element_type=jnp.float32
    )
    grad_h_two = lax.psum(
        jnp.einsum("ctf,cdf->td", grad_gate_up, w_mlp, preferred_element_type=jnp.float32).astype(
            jnp.bfloat16
        ),
        "head",
    ).astype(jnp.float32)
    grad_x_part, grad_gain_m = norm_two_back(grad_h_two)
    grad_x_one = cotangent.astype(jnp.float32) + grad_x_part
    grad_attn_low = grad_x_one.astype(jnp.bfloat16)
    grad_out = jnp.einsum("tw,td->wd", mixed_low, grad_attn_low, preferred_element_type=jnp.float32)
    grad_normed = jnp.einsum("td,wd->tw", grad_attn_low, w_out, preferred_element_type=jnp.float32)
    grad_out_rows, grad_gate, grad_gain_o = gate_back(grad_normed)
    grad_outputs_c = to_spans(grad_out_rows.reshape(row_count, -1, DK), span_count)
    first_cot = apply_back((grad_outputs_c, jnp.zeros_like(state_out)))
    carry_term = first_cot[8]
    p_trans = jnp.swapaxes(p_dev, 1, 2)

    def relay_back(turn, from_above):
        return passed_along(
            (carry_term + jnp.matmul(from_above, p_trans, precision=HIGHEST_PREC)).astype(
                jnp.bfloat16
            ),
            "seq",
            -1,
        ).astype(jnp.float32)

    from_above = lax.fori_loop(0, lax.axis_size("seq") - 1, relay_back, jnp.zeros_like(carry_term))
    second_cot = apply_back((jnp.zeros_like(grad_outputs_c), from_above))
    total_cot = jax.tree.map(jnp.add, first_cot, second_cot)
    grad_key_b, grad_value_c, grad_beta_c = prep_back(
        (total_cot[2], total_cot[3], total_cot[4], total_cot[5], total_cot[6], total_cot[7])
    )
    grad_query_r = from_spans(total_cot[0])
    grad_key_r = from_spans(total_cot[1] + grad_key_b)
    grad_value_r = from_spans(grad_value_c)
    grad_beta_r = jnp.transpose(grad_beta_c, (1, 2, 0)).reshape(row_count, -1)
    grad_extended, grad_conv, grad_logits = mix_back(
        (grad_query_r, grad_key_r, grad_value_r, grad_beta_r)
    )
    back_rows = passed_along(grad_extended[:, : CONV - 1], "seq", -1)
    grad_pre = grad_extended[:, CONV - 1 :].at[:, row_count - (CONV - 1) :].add(back_rows)
    grad_proj_low = jnp.concatenate([grad_pre, grad_gate[None]], axis=0).astype(jnp.bfloat16)
    grad_logits_low = grad_logits.astype(jnp.bfloat16)
    grad_proj = jnp.einsum(
        "td,cte->cde", hidden_low, grad_proj_low, preferred_element_type=jnp.float32
    )
    grad_beta = jnp.einsum(
        "td,th->dh", hidden_low, grad_logits_low, preferred_element_type=jnp.float32
    )
    grad_hidden_part = jnp.einsum(
        "cte,cde->td", grad_proj_low, w_proj, preferred_element_type=jnp.float32
    ) + jnp.einsum("th,dh->td", grad_logits_low, w_beta, preferred_element_type=jnp.float32)
    grad_hidden, grad_gain_o_sum = (
        lax.psum(grad_hidden_part.astype(jnp.bfloat16), "head").astype(jnp.float32),
        lax.psum(grad_gain_o.astype(jnp.bfloat16), "head").astype(jnp.float32),
    )
    grad_x_rest, grad_gain_a = norm_back(grad_hidden)
    input_grad = grad_x_one + grad_x_rest
    grad_gains = jnp.concatenate([grad_gain_a, grad_gain_m, grad_gain_o_sum])
    summed_proj, summed_beta, summed_conv, summed_out, summed_mlp, summed_down, summed_gains = (
        lax.psum_scatter(
            grad_proj.astype(jnp.bfloat16), "seq", scatter_dimension=1, tiled=True
        ).astype(jnp.float32),
        lax.psum_scatter(
            grad_beta.astype(jnp.bfloat16), "seq", scatter_dimension=0, tiled=True
        ).astype(jnp.float32),
        lax.psum_scatter(
            grad_conv.astype(jnp.bfloat16), "seq", scatter_dimension=2, tiled=True
        ).astype(jnp.float32),
        lax.psum_scatter(
            grad_out.astype(jnp.bfloat16), "seq", scatter_dimension=1, tiled=True
        ).astype(jnp.float32),
        lax.psum_scatter(
            grad_mlp.astype(jnp.bfloat16), "seq", scatter_dimension=1, tiled=True
        ).astype(jnp.float32),
        lax.psum_scatter(
            grad_down.astype(jnp.bfloat16), "seq", scatter_dimension=1, tiled=True
        ).astype(jnp.float32),
        lax.psum_scatter(
            grad_gains.astype(jnp.bfloat16), "seq", scatter_dimension=0, tiled=True
        ).astype(jnp.float32),
    )
    proj_new, proj_first_new, proj_second_new = adam_update(
        proj_master, proj_first, proj_second, summed_proj, rate_matrix, decay_matrix
    )
    beta_new, beta_first_new, beta_second_new = adam_update(
        beta_master, beta_first, beta_second, summed_beta, rate_beta, decay_matrix
    )
    conv_new, conv_first_new, conv_second_new = adam_update(
        conv_master, conv_first, conv_second, summed_conv, rate_conv, decay_matrix
    )
    out_new, out_first_new, out_second_new = adam_update(
        out_master, out_first, out_second, summed_out, rate_matrix, decay_matrix
    )
    mlp_new, mlp_first_new, mlp_second_new = adam_update(
        mlp_master, mlp_first, mlp_second, summed_mlp, rate_matrix, decay_matrix
    )
    down_new, down_first_new, down_second_new = adam_update(
        down_master, down_first, down_second, summed_down, rate_down, decay_matrix
    )
    gains_new, gains_first_new, gains_second_new = adam_update(
        gains_master, gains_first, gains_second, summed_gains, rate_gains, 0.0
    )
    return (
        result,
        input_grad,
        proj_new,
        proj_first_new,
        proj_second_new,
        proj_new.astype(jnp.bfloat16),
        beta_new,
        beta_first_new,
        beta_second_new,
        beta_new.astype(jnp.bfloat16),
        conv_new,
        conv_first_new,
        conv_second_new,
        conv_new.astype(jnp.bfloat16),
        out_new,
        out_first_new,
        out_second_new,
        out_new.astype(jnp.bfloat16),
        mlp_new,
        mlp_first_new,
        mlp_second_new,
        mlp_new.astype(jnp.bfloat16),
        down_new,
        down_first_new,
        down_second_new,
        down_new.astype(jnp.bfloat16),
        gains_new,
        gains_first_new,
        gains_second_new,
    )


def solution(mesh):
    return jax.shard_map(
        per_device,
        mesh=mesh,
        in_specs=(
            P("seq", None),
            P("seq", None),
            P(),
            P(None, "seq", "head"),
            P(None, "seq", "head"),
            P(None, "seq", "head"),
            P("seq", "head"),
            P("seq", "head"),
            P("seq", "head"),
            P(None, None, ("head", "seq")),
            P(None, None, ("head", "seq")),
            P(None, None, ("head", "seq")),
            P("head", "seq"),
            P("head", "seq"),
            P("head", "seq"),
            P(None, "seq", "head"),
            P(None, "seq", "head"),
            P(None, "seq", "head"),
            P("head", "seq"),
            P("head", "seq"),
            P("head", "seq"),
            P("seq"),
            P("seq"),
            P("seq"),
        ),
        out_specs=(
            P("seq", None),
            P("seq", None),
            P(None, "seq", "head"),
            P(None, "seq", "head"),
            P(None, "seq", "head"),
            P(None, "seq", "head"),
            P("seq", "head"),
            P("seq", "head"),
            P("seq", "head"),
            P("seq", "head"),
            P(None, None, ("head", "seq")),
            P(None, None, ("head", "seq")),
            P(None, None, ("head", "seq")),
            P(None, None, ("head", "seq")),
            P("head", "seq"),
            P("head", "seq"),
            P("head", "seq"),
            P("head", "seq"),
            P(None, "seq", "head"),
            P(None, "seq", "head"),
            P(None, "seq", "head"),
            P(None, "seq", "head"),
            P("head", "seq"),
            P("head", "seq"),
            P("head", "seq"),
            P("head", "seq"),
            P("seq"),
            P("seq"),
            P("seq"),
        ),
        check_vma=False,
    )
```

profile of v0, /device:TPU:0, one launch (start us, length us, event | category | flops | bytes accessed | tf_op | source)
XLA Modules:
  0.0 2063.0 jit_solution(5828294504473155097)
XLA Ops:
  12.6 40.1 %all-reduce.13 = bf16[4224]{0:T(1024)(128)(2,1)S(1)} all-reduce(bf16[4224]{0:T(1024)(128)(2,1)S(1)} %dynamic-update-slice.3), channel_id=1, replica_groups=mesh['seq'=8,'head'=4] {'seq'}, use_global_device_ids=true, to_apply=%add.13 | all-reduce | flops 4224 | bytes 16896
  55.4 32.9 %all_gather.21 = bf16[3,4,512]{1,0,2:T(4,128)(2,1)S(1)} all-gather(bf16[3,4,64]{1,0,2:T(4,128)(2,1)S(1)} %copy.421), channel_id=1, replica_groups=mesh['seq'=8,'head'=4] {'seq'}, dimensions={2}, use_global_device_ids=true | all-gather | bytes 13824 | tf_op jit(solution)/shard_map/all_gather | solution.py:185
  90.9 26.5 %all_gather.24 = bf16[2048,4]{0,1:T(4,128)(2,1)S(1)} all-gather(bf16[256,4]{0,1:T(4,128)(2,1)S(1)} %convert_element_type.193), channel_id=1, replica_groups=mesh['seq'=8,'head'=4] {'seq'}, dimensions={0}, use_global_device_ids=true | all-gather | bytes 18432 | tf_op jit(solution)/shard_map/all_gather | solution.py:184
  118.3 25.3 %all-gather.5.cloned.1.call-done = bf16[4,2048,512]{2,1,0:T(8,128)(2,1)} async-done(((bf16[4,256,512]{2,1,0:T(8,128)(2,1)}), bf16[4,2048,512]{2,1,0:T(8,128)(2,1)}) %all-gather.5.cloned.1.call-update) | async-done | bytes 8388624 | tf_op jit(solution)/shard_map/all_gather | solution.py:183
  143.6 9.6 fusion.255
  183.6 158.2 %custom-call.15 = f32[4,8,1,64,64]{3,4,2,1,0:T(8,128)S(1)} custom-call(f32[4,8,1,64,64]{4,3,2,1,0:T(8,128)} %fusion.122), custom_call_target="InvertDiagBlocksLowerTriangular" | custom-call | tf_op jit(solution)/shard_map/jvp()/triangular_solve/custom-call.1 | solution.py:95
  364.2 49.9 %while.63 = (s32[]{:T(128)}, f32[4,128,128]{2,1,0:T(8,128)S(1)}, f32[4,128,128]{2,1,0:T(8,128)S(1)}, f32[8,4,128,128]{3,2,1,0:T(8,128)}, f32[8,4,128,128]{3,2,1,...) while((s32[]{:T(128)}, f32[4,128,128]{2,1,0:T(8,128)S(1)}, ...), condition=%wide.region_4.6_spmd.clone, body=%wide.region_3.5_spmd.clone.sunk | while | flops 201785344 | bytes 3935919 | solution.py:122
  422.9 54.1 %while.64 = (s32[]{:T(128)}, f32[4,128,128]{2,1,0:T(8,128)S(1)}, f32[4,128,128]{2,1,0:T(8,128)S(1)}, f32[4,128,128]{2,1,0:T(8,128)S(1)}, s32[]{:T(128)}, /*index=5*/s32[]{:T(128)}) while((s32[]{:T(128)}, f32[4,128,128]{2,1,0:T(8,128)S(1)}, f32[4,128,128]{2,1,0:T(8,128)S(1)}, f32[4,128,128]{2,1,0:T(8,128)S(1)}, s32[]{:T(128)}, ...), condition=%wide.region_6.8_spmd.clone, body=%wide.region_5.7_spmd.clone.sunk | while | flops 100925440 | bytes 1835127 | solution.py:234
  528.8 63.5 %all-reduce.20.cloned.1.call-done = f32[512,2048]{1,0:T(8,128)} async-done(((f32[512,2048]{1,0:T(8,128)}), f32[512,2048]{1,0:T(8,128)}) %all-reduce.20.cloned.1.call-update) | async-done | bytes 4194320 | tf_op jit(solution)/shard_map/psum | solution.py:242
  597.7 161.3 %all-gather.9.cloned.1.call-done = bf16[2,2048,1408]{2,1,0:T(8,128)(2,1)} async-done(((bf16[2,256,1408]{2,1,0:T(8,128)(2,1)}), bf16[2,2048,1408]{2,1,0:T(8,128)(2,1)}) %all-gather.9.cloned.1.call-update) | async-done | bytes 11534352 | tf_op jit(solution)/shard_map/all_gather | solution.py:187
  759.0 13.0 convolution_bitcast_fusion.2
  772.0 81.5 %all-gather.11.cloned.1.call-done = bf16[1408,2048]{1,0:T(8,128)(2,1)} async-done(((bf16[1408,256]{1,0:T(8,128)(2,1)}), bf16[1408,2048]{1,0:T(8,128)(2,1)}) %all-gather.11.cloned.1.call-update) | async-done | bytes 5767184 | tf_op jit(solution)/shard_map/all_gather | solution.py:188
  853.5 10.5 multiply_bitcast_fusion
  866.5 7.3 bitcast_convert_fusion
  893.4 7.9 convolution_convert_fusion.2
  901.3 22.3 %all-reduce.22.cloned.1.call-done = bf16[512,2048]{1,0:T(8,128)(2,1)} async-done(((bf16[512,2048]{1,0:T(8,128)(2,1)}), bf16[512,2048]{1,0:T(8,128)(2,1)}) %all-reduce.22.cloned.1.call-update) | async-done | bytes 2097168 | tf_op jit(solution)/shard_map/psum | solution.py:259
  969.9 75.7 %while.65 = (s32[]{:T(128)}, f32[4,128,128]{2,1,0:T(8,128)}, f32[4,128,128]{2,1,0:T(8,128)}, f32[4,128,128]{2,1,0:T(8,128)}, s32[]{:T(128)}, /*index=5*/s32[]{:T(128)}) while((s32[]{:T(128)}, f32[4,128,128]{2,1,0:T(8,128)}, f32[4,128,128]{2,1,0:T(8,128)}, f32[4,128,128]{2,1,0:T(8,128)}, s32[]{:T(128)}, ...), condition=%wide.region_15.17_spmd.clone, body=%wide.region_14.16_spmd.clone.sunk | while | flops 100925440 | bytes 1835127 | solution.py:285
  993.4 6.6 collective-permute-done.1
  1051.5 7.0 add_bitcast_fusion.1
  1061.6 128.6 %while.62 = (s32[]{:T(128)}, f32[4,128,128]{1,2,0:T(8,128)}, f32[4,128,128]{1,2,0:T(8,128)}, f32[8,4,128,128]{3,2,1,0:T(8,128)}, f32[8,4,128,128]{2,3,1,0:T(8,12...) while((s32[]{:T(128)}, f32[4,128,128]{1,2,0:T(8,128)}, ...), condition=%wide.region_17.19_spmd, body=%wide.region_16.18_spmd.sunk | while | flops 402980864 | bytes 6556845 | solution.py:122
  1298.2 7.6 fusion.111
  1322.0 8.4 convert_bitcast_fusion.1
  1331.1 12.5 convert_bitcast_fusion
  1370.5 45.9 %reduce-scatter.19.cloned.1.call-done = bf16[256,4]{1,0:T(8,128)(2,1)} async-done(((bf16[2048,4]{1,0:T(8,128)(2,1)}), bf16[256,4]{1,0:T(8,128)(2,1)}) %reduce-scatter.19.cloned.1.call-update) | async-done | bytes 2064
  1418.0 86.3 %all-reduce.24.cloned.1.call-done = (bf16[512,2048]{1,0:T(8,128)(2,1)}, bf16[512,2048]{1,0:T(8,128)(2,1)}) async-done(((bf16[512,2048]{1,0:T(8,128)(2,1)}, bf16[512,2048]{1,0:T(8,128)(2,1)}), (bf16[512,2048]{1,0:T(8,128)(2,1)}, bf16[512,2048]{1,0:T(8,128)(2,1)})) %all-reduce.24.cloned.1.call-update) | async-done | bytes 4194320 | tf_op jit(solution)/shard_map/psum | solution.py:249
  1507.7 37.7 %all-reduce.14 = bf16[4224]{0:T(1024)(128)(2,1)S(1)} all-reduce(bf16[4224]{0:T(1024)(128)(2,1)S(1)} %pad_maximum_fusion.3), channel_id=8, replica_groups=mesh['seq'=8,'head'=4] {'seq'}, use_global_device_ids=true, to_apply=%region_39.43.clone | all-reduce | flops 4224 | bytes 16896
  1555.2 21.0 %reduce-scatter.13.cloned.1.call-done = bf16[512,256]{1,0:T(8,128)(2,1)} async-done(((bf16[512,2048]{1,0:T(8,128)(2,1)}), bf16[512,256]{1,0:T(8,128)(2,1)}) %reduce-scatter.13.cloned.1.call-update) | async-done | bytes 262160 | tf_op jit(solution)/shard_map/reduce_scatter | solution.py:328
  1579.1 110.1 %reduce-scatter.17.cloned.1.call-done = bf16[1408,256]{1,0:T(8,128)(2,1)} async-done(((bf16[1408,2048]{1,0:T(8,128)(2,1)}), bf16[1408,256]{1,0:T(8,128)(2,1)}) %reduce-scatter.17.cloned.1.call-update) | async-done | bytes 720912 | tf_op jit(solution)/shard_map/reduce_scatter | solution.py:334
  1694.3 147.7 %reduce-scatter.11.cloned.1.call-done = bf16[4,256,512]{1,2,0:T(8,128)(2,1)} async-done(((bf16[4,2048,512]{1,2,0:T(8,128)(2,1)}), bf16[4,256,512]{1,2,0:T(8,128)(2,1)}) %reduce-scatter.11.cloned.1.call-update) | async-done | bytes 1048592 | tf_op jit(solution)/shard_map/reduce_scatter | solution.py:319
  1842.0 6.7 fusion.246
  1858.8 179.2 %reduce-scatter.15.cloned.1.call-done = bf16[2,256,1408]{1,2,0:T(8,128)(2,1)} async-done(((bf16[2,2048,1408]{1,2,0:T(8,128)(2,1)}), bf16[2,256,1408]{1,2,0:T(8,128)(2,1)}) %reduce-scatter.15.cloned.1.call-update) | async-done | bytes 1441808 | tf_op jit(solution)/shard_map/reduce_scatter | solution.py:331
  2038.0 6.6 fusion.233
  (718 shorter events, 701.3 us)
Async XLA Ops:
  7.3 136.4 %all-gather.5.cloned.1.call-start = ((), (), s32[]{:S(2)}) async-start(), calls=%async_computation.6 | async-start | bytes 9437184 | tf_op jit(solution)/shard_map/all_gather | solution.py:183
  10.2 487.8 %all-gather.7.cloned.1.call-start = ((), (), s32[]{:S(2)}) async-start(), calls=%async_computation.7 | async-start | bytes 2359296 | tf_op jit(solution)/shard_map/all_gather | solution.py:186
  11.0 581.3 %all-reduce.20.cloned.1.call-start = ((), (), s32[]{:S(2)}) async-start(), calls=%async_computation.8 | async-start | bytes 8388608 | tf_op jit(solution)/shard_map/psum | solution.py:242
  52.7 875.8 %copy-start.100 = (f32[2048]{0:T(1024)}, f32[2048]{0:T(1024)S(1)}, u32[]{:S(2)}) copy-start(f32[2048]{0:T(1024)S(1)} %get-tuple-element.795) | copy-start | bytes 24580
  154.5 9.3 collective-permute-start.2
  419.7 530.4 %copy-start.84 = (f32[8,64,4]{1,0,2:T(8,128)}, f32[8,64,4]{1,0,2:T(8,128)S(1)}, u32[]{:S(2)}) copy-start(f32[8,64,4]{1,0,2:T(8,128)S(1)} %rsqrt.65) | copy-start | bytes 24580
  423.3 6.0 collective-permute-start
  429.7 6.9 collective-permute-start
  437.0 6.9 collective-permute-start
  444.3 6.9 collective-permute-start
  451.6 7.3 collective-permute-start
  459.4 9.3 collective-permute-start
  469.2 7.7 collective-permute-start
  503.0 256.0 %all-gather.9.cloned.1.call-start = ((), (), s32[]{:S(2)}) async-start(), calls=%async_computation.9 | async-start | bytes 12976128 | tf_op jit(solution)/shard_map/all_gather | solution.py:187
  506.1 347.3 %all-gather.11.cloned.1.call-start = ((), (), s32[]{:S(2)}) async-start(), calls=%async_computation.10 | async-start | bytes 6488064 | tf_op jit(solution)/shard_map/all_gather | solution.py:188
  508.5 415.1 %all-reduce.22.cloned.1.call-start = ((), (), s32[]{:S(2)}) async-start(), calls=%async_computation.11 | async-start | bytes 4194304 | tf_op jit(solution)/shard_map/psum | solution.py:259
  597.7 330.8 %copy-start.125 = (f32[512]{0:T(512)}, f32[512]{0:T(512)S(1)}, u32[]{:S(2)}) copy-start(f32[512]{0:T(512)S(1)} %fusion.213) | copy-start | bytes 6148
  873.9 495.1 %reduce-scatter.21.cloned.1.call-start = ((), (), s32[]{:S(2)}) async-start(), calls=%async_computation.17 | async-start | bytes 147456
  971.4 7.2 collective-permute-start.1
  981.7 7.3 collective-permute-start.1
  992.1 7.9 collective-permute-start.1
  1003.1 7.9 collective-permute-start.1
  1014.1 7.9 collective-permute-start.1
  1025.1 7.9 collective-permute-start.1
  1036.1 7.9 collective-permute-start.1
  1280.8 15.2 collective-permute-start.3
  1287.7 128.8 %reduce-scatter.19.cloned.1.call-start = ((), (), s32[]{:S(2)}) async-start(), calls=%async_computation.16 | async-start | bytes 589824
  1295.9 208.4 %all-reduce.24.cloned.1.call-start = ((), (), s32[]{:S(2)}) async-start(), calls=%async_computation.18 | async-start | bytes 8388608 | tf_op jit(solution)/shard_map/psum | solution.py:249
  1308.0 268.3 %reduce-scatter.13.cloned.1.call-start = ((), (), s32[]{:S(2)}) async-start(), calls=%async_computation.13 | async-start | bytes 2359296 | tf_op jit(solution)/shard_map/reduce_scatter | solution.py:328
  1313.8 375.5 %reduce-scatter.17.cloned.1.call-start = ((), (), s32[]{:S(2)}) async-start(), calls=%async_computation.15 | async-start | bytes 6488064 | tf_op jit(solution)/shard_map/reduce_scatter | solution.py:334
  1320.3 521.7 %reduce-scatter.11.cloned.1.call-start = ((), (), s32[]{:S(2)}) async-start(), calls=%async_computation.12 | async-start | bytes 9437184 | tf_op jit(solution)/shard_map/reduce_scatter | solution.py:319
  1330.5 707.5 %reduce-scatter.15.cloned.1.call-start = ((), (), s32[]{:S(2)}) async-start(), calls=%async_computation.14 | async-start | bytes 12976128 | tf_op jit(solution)/shard_map/reduce_scatter | solution.py:331
  (149 other events, 3897.4 us)
Sparse Core Ops, SparseCore 0:
  10.9 132.7 all-gather.4
  146.2 50.7 all-gather.6
  503.1 89.1 all-reduce.19
  595.2 163.7 all-gather.8
  761.7 91.7 all-gather.10
  874.0 49.5 all-reduce.21
  1287.8 63.7 reduce-scatter.20
  1355.4 60.9 reduce-scatter.18
  1419.6 84.6 all-reduce.23
  1507.7 68.4 reduce-scatter.12
  1579.9 109.3 reduce-scatter.16
  1692.7 149.2 reduce-scatter.10
  1846.0 191.8 reduce-scatter.14
where the time goes:
time: 2070 us; the launch traced here: 2060 us
  waiting for transfers between devices  1010 us (49%)
  matrix products  359 us (17%)
  other arithmetic  285 us (14%)
  local copies, waits for them, and re-layouts  203 us (10%)
  blocking collectives  143 us (7%)
  starting transfers between devices  47.4 us (2%)
    reduce_scatter x1, waiting for transfers between devices, per_device(): lax.psum_scatter(grad_mlp.astype(jnp.bfloat16), 'seq', scatter_dimension=...  179 us
    all_gather x1, waiting for transfers between devices, per_device(): lax.all_gather(mlp_master.astype(jnp.bfloat16), 'seq', axis=1, tiled=True)  161 us
    another operation x3, other arithmetic, prepare(): lax.linalg.triangular_solve(system, beta_c[..., None] * key_c, left_side=...  161 us
    reduce_scatter x1, waiting for transfers between devices, per_device(): lax.psum_scatter(grad_proj.astype(jnp.bfloat16), 'seq', scatter_dimension...  148 us
    reduce_scatter x1, waiting for transfers between devices, per_device(): lax.psum_scatter(grad_down.astype(jnp.bfloat16), 'seq', scatter_dimension...  110 us
    psum x1, waiting for transfers between devices, per_device(): lax.psum(jnp.dot(act_low, w_down, preferred_element_type=jnp.float32).ast...  86.3 us
    all_gather x1, waiting for transfers between devices, per_device(): lax.all_gather(down_master.astype(jnp.bfloat16), 'seq', axis=1, tiled=True)  81.5 us
    unnamed x2, blocking collectives  77.7 us
  transfers between devices with their start and end apart: 29, of which 25 were waited for; matrix products, arithmetic and copies ran while one was open for 24% of the time, Pallas kernels for 0%

commit v1 on v0

v1 whole, which is shorter than its diff:
```python
from functools import partial

import jax
import jax.numpy as jnp
from jax import lax
from jax.experimental import pallas as pl
from jax.experimental.pallas import tpu as pltpu
from jax.sharding import PartitionSpec as P

D = 2048
DK = 128
CONV = 4
SPAN = 64
STEP = 10

eps_norm = 1e-05
eps_unit = 1e-06
beta_one = 0.9
beta_two = 0.95
eps_adam = 1e-08
rate_matrix = 0.04
rate_beta = 0.12
rate_down = 0.03
rate_conv = 0.3
rate_gains = 0.4
decay_matrix = 0.1


SPANROWS = 128


def _mm(a, b):
    return jnp.dot(
        a.astype(jnp.bfloat16), b.astype(jnp.bfloat16), preferred_element_type=jnp.float32
    )


def _mm_nt(a, b):
    return lax.dot_general(
        a.astype(jnp.bfloat16),
        b.astype(jnp.bfloat16),
        (((1,), (1,)), ((), ())),
        preferred_element_type=jnp.float32,
    )


def _mm_tn(a, b):
    return lax.dot_general(
        a.astype(jnp.bfloat16),
        b.astype(jnp.bfloat16),
        (((0,), (0,)), ((), ())),
        preferred_element_type=jnp.float32,
    )


def _pair_masks():
    row = lax.broadcasted_iota(jnp.int32, (SPANROWS, SPANROWS), 0)
    col = lax.broadcasted_iota(jnp.int32, (SPANROWS, SPANROWS), 1)
    same = (row // SPAN) == (col // SPAN)
    return row, col, same


def _tap_masks(scal_ref, rows):
    edge, base = scal_ref[0], scal_ref[1]
    token = lax.broadcasted_iota(jnp.int32, (rows, DK), 0)
    after = token >= edge
    masks = [None]
    for shift in range(1, CONV):
        good = jnp.where(after, token - edge, token + base) >= shift
        masks.append(good.astype(jnp.float32))
    return masks


def _keep(scal_ref, span):
    edge, base = scal_ref[0], scal_ref[1]
    start = span * SPAN
    hit = (edge == start) | ((base + start) == 0)
    return jnp.where(hit, 0.0, 1.0).astype(jnp.float32)


def _convolved(ext_ref, pre, halo, taps, masks):
    rows = pre.shape[0]
    ext_ref[0:8] = halo[8:16].astype(jnp.float32)
    ext_ref[8 : 8 + rows] = pre.astype(jnp.float32)
    total = taps[CONV - 1 : CONV] * ext_ref[8 : 8 + rows]
    for shift in range(1, CONV):
        total = (
            total
            + taps[CONV - 1 - shift : CONV - shift]
            * ext_ref[8 - shift : 8 - shift + rows]
            * masks[shift]
        )
    return total


def _unit(act):
    return act * lax.rsqrt(jnp.sum(act * act, axis=-1, keepdims=True) + eps_unit)


def _column(table, index):
    lane = lax.broadcasted_iota(jnp.int32, table.shape, 1)
    return jnp.sum(jnp.where(lane == index, table, 0.0), axis=1, keepdims=True)


def _local_kernel(
    heads, scal_ref, pre_ref, halo_ref, taps_ref, logit_ref, q_ref, k_ref, w_ref, uv_ref, t_ref,
    bt_ref, pt_ref, ext_ref,
):
    rows = pre_ref.shape[1]
    pairs = rows // SPANROWS
    masks = _tap_masks(scal_ref, rows)
    row, col, same = _pair_masks()
    strict = same & (row > col)
    eye = (row == col).astype(jnp.float32)
    levels = []
    for bit in range(6):
        inside = ((row >> (bit + 1)) == (col >> (bit + 1))) & same
        levels.append(
            (inside & (((row >> bit) & 1) == 1) & (((col >> bit) & 1) == 0)).astype(jnp.float32)
        )
    logit = logit_ref[...]
    first_head = pl.program_id(0) * heads
    keys, lowers, sides = [], [], []
    for head in range(heads):
        lanes = slice(head * DK, (head + 1) * DK)
        beta = jax.nn.sigmoid(_column(logit, first_head + head))
        acts = []
        for part in range(3):
            mixed = _convolved(
                ext_ref.at[head * 3 + part], pre_ref[part, :, lanes], halo_ref[part, :, lanes],
                taps_ref[part, :, lanes], masks,
            )
            acts.append(mixed * jax.nn.sigmoid(mixed))
        query = _unit(acts[0])
        key = _unit(acts[1])
        q_ref[:, lanes] = query.astype(jnp.bfloat16)
        key_low = key.astype(jnp.bfloat16)
        k_ref[:, lanes] = key_low
        side = jnp.concatenate([beta * key, beta * acts[2]], axis=1).astype(jnp.bfloat16)
        for pair in range(pairs):
            part = slice(pair * SPANROWS, (pair + 1) * SPANROWS)
            gram = _mm_nt(key_low[part], key_low[part])
            lowers.append(jnp.where(strict, gram * beta[part], 0.0))
            sides.append(side[part])
        keys.append(key_low)
    inverses = [eye - low * levels[0] for low in lowers]
    for bit in range(1, 6):
        middle = [_mm(low * levels[bit], inv) for low, inv in zip(lowers, inverses)]
        inverses = [inv - _mm(inv, mid) for mid, inv in zip(middle, inverses)]
    carried = []
    w_all, uv_all = [], []
    for head in range(heads):
        lanes = slice(head * DK, (head + 1) * DK)
        w_rows, uv_rows = [], []
        for pair in range(pairs):
            part = slice(pair * SPANROWS, (pair + 1) * SPANROWS)
            inv = inverses[head * pairs + pair].astype(jnp.bfloat16)
            t_ref[part, lanes] = inv
            both = _mm(inv, sides[head * pairs + pair])
            w_part = both[:, :DK].astype(jnp.bfloat16)
            w_ref[part, lanes] = w_part
            uv_ref[part, lanes] = both[:, DK:]
            w_rows.append(w_part)
            uv_rows.append(both[:, DK:])
        w_all.append(w_rows)
        uv_all.append(uv_rows)
        carried.append(jnp.concatenate([jnp.zeros((DK, DK), jnp.float32), eye], axis=1))
    for span in range(rows // SPAN):
        keep = _keep(scal_ref, span)
        pair, half = divmod(span, SPANROWS // SPAN)
        part = slice(half * SPAN, (half + 1) * SPAN)
        for head in range(heads):
            state = carried[head] * keep
            w_part = w_all[head][pair][part]
            source = jnp.concatenate(
                [uv_all[head][pair][part], jnp.zeros((SPAN, DK), jnp.float32)], axis=1
            )
            change = source - _mm(w_part, state)
            carried[head] = state + _mm_tn(
                keys[head][span * SPAN : (span + 1) * SPAN], change
            )
    for head in range(heads):
        bt_ref[head] = carried[head][:, :DK]
        pt_ref[head] = carried[head][:, DK:].astype(jnp.bfloat16)


def _apply_kernel(
    heads, scal_ref, q_ref, k_ref, w_ref, uv_ref, state_ref, gate_ref, gain_ref, n_ref, o_ref,
    u_ref, s_ref,
):
    rows = q_ref.shape[0]
    pairs = rows // SPANROWS
    row, col, same = _pair_masks()
    lower = same & (row >= col)
    states = [state_ref[head].astype(jnp.float32) for head in range(heads)]
    moved = [[] for _ in range(heads)]
    crossed = [[] for _ in range(heads)]
    for span in range(rows // SPAN):
        keep = _keep(scal_ref, span)
        part = slice(span * SPAN, (span + 1) * SPAN)
        for head in range(heads):
            lanes = slice(head * DK, (head + 1) * DK)
            state = states[head] * keep
            state_low = state.astype(jnp.bfloat16)
            s_ref[head, span] = state_low
            both = _mm(
                jnp.concatenate([w_ref[part, lanes], q_ref[part, lanes]], axis=0), state_low
            )
            change = (uv_ref[part, lanes] - both[:SPAN]).astype(jnp.bfloat16)
            crossed[head].append(both[SPAN:])
            moved[head].append(change)
            states[head] = state + _mm_tn(k_ref[part, lanes], change)
    for head in range(heads):
        lanes = slice(head * DK, (head + 1) * DK)
        for pair in range(pairs):
            part = slice(pair * SPANROWS, (pair + 1) * SPANROWS)
            change = jnp.concatenate([moved[head][2 * pair], moved[head][2 * pair + 1]], axis=0)
            cross = jnp.concatenate([crossed[head][2 * pair], crossed[head][2 * pair + 1]], axis=0)
            u_ref[part, lanes] = change
            scores = jnp.where(lower, _mm_nt(q_ref[part, lanes], k_ref[part, lanes]), 0.0)
            out = cross + _mm(scores, change)
            o_ref[part, lanes] = out
            scaled = out * lax.rsqrt(jnp.mean(out * out, axis=-1, keepdims=True) + eps_norm)
            gate = gate_ref[part, lanes]
            n_ref[part, lanes] = (
                scaled * gain_ref[...] * (gate * jax.nn.sigmoid(gate))
            ).astype(jnp.bfloat16)


def _back_local_kernel(
    heads, scal_ref, dn_ref, gate_ref, gain_ref, o_ref, q_ref, k_ref, w_ref, dg_ref, dgo_ref,
    do_ref, p_ref, carry_ref,
):
    rows = q_ref.shape[0]
    pairs = rows // SPANROWS
    row, col, same = _pair_masks()
    lower = same & (row >= col)
    gain = gain_ref[...]
    grad_outs = [[] for _ in range(heads)]
    passed = [[] for _ in range(heads)]
    for head in range(heads):
        lanes = slice(head * DK, (head + 1) * DK)
        gain_sum = jnp.zeros((1, DK), jnp.float32)
        for pair in range(pairs):
            part = slice(pair * SPANROWS, (pair + 1) * SPANROWS)
            out = o_ref[part, lanes]
            gate = gate_ref[part, lanes]
            grad_n = dn_ref[part, lanes]
            inv = lax.rsqrt(jnp.mean(out * out, axis=-1, keepdims=True) + eps_norm)
            sig = jax.nn.sigmoid(gate)
            act = gate * sig
            scaled = out * inv
            with_gain = grad_n * gain
            dg_ref[part, lanes] = (
                with_gain * scaled * (sig * (1.0 + gate * (1.0 - sig)))
            ).astype(jnp.bfloat16)
            gain_sum = gain_sum + jnp.sum(grad_n * scaled * act, axis=0, keepdims=True)
            inner = with_gain * act
            grad_out = (
                inv * inner
                - out * (inv * inv * inv) * jnp.mean(inner * out, axis=-1, keepdims=True)
            ).astype(jnp.bfloat16)
            do_ref[part, lanes] = grad_out
            scores = jnp.where(lower, _mm_nt(q_ref[part, lanes], k_ref[part, lanes]), 0.0)
            through = _mm_tn(scores, grad_out)
            p_ref[part, lanes] = through
            grad_outs[head].append(grad_out)
            passed[head].append(through)
        dgo_ref[head] = jnp.broadcast_to(gain_sum, (8, DK))
    carried = [jnp.zeros((DK, DK), jnp.float32) for _ in range(heads)]
    for span in reversed(range(rows // SPAN)):
        keep = _keep(scal_ref, span)
        rows_in = slice(span * SPAN, (span + 1) * SPAN)
        pair, half = divmod(span, SPANROWS // SPAN)
        part = slice(half * SPAN, (half + 1) * SPAN)
        for head in range(heads):
            lanes = slice(head * DK, (head + 1) * DK)
            change = passed[head][pair][part] + _mm(k_ref[rows_in, lanes], carried[head])
            carried[head] = keep * (
                carried[head]
                + _mm_tn(q_ref[rows_in, lanes], grad_outs[head][pair][part])
                - _mm_tn(w_ref[rows_in, lanes], change)
            )
    for head in range(heads):
        carry_ref[head] = carried[head]


def _back_kernel(
    heads, scal_ref, pre_ref, halo_ref, taps_ref, logit_ref, q_ref, k_ref, w_ref, t_ref, u_ref,
    s_ref, do_ref, p_ref, above_ref, dpre_ref, tail_ref, dhalo_ref, dtaps_ref, dlogit_ref,
    ext_ref, pad_ref,
):
    rows = q_ref.shape[0]
    pairs = rows // SPANROWS
    masks = _tap_masks(scal_ref, rows)
    row, col, same = _pair_masks()
    lower = same & (row >= col)
    strict = same & (row > col)
    edge, base = scal_ref[0], scal_ref[1]
    token = lax.broadcasted_iota(jnp.int32, (rows + 8, DK), 0) - 8
    back_masks = []
    for shift in range(CONV):
        good = jnp.where(token + shift >= edge, token - edge, token + base) >= 0
        back_masks.append(good.astype(jnp.float32))
    logit = logit_ref[...]
    first_head = pl.program_id(0) * heads
    carried = [above_ref[head].astype(jnp.float32) for head in range(heads)]
    changes = [[None] * (rows // SPAN) for _ in range(heads)]
    crossed = [[None] * (rows // SPAN) for _ in range(heads)]
    for span in reversed(range(rows // SPAN)):
        keep = _keep(scal_ref, span)
        part = slice(span * SPAN, (span + 1) * SPAN)
        for head in range(heads):
            lanes = slice(head * DK, (head + 1) * DK)
            above = carried[head].astype(jnp.bfloat16)
            change = (p_ref[part, lanes] + _mm(k_ref[part, lanes], above)).astype(jnp.bfloat16)
            changes[head][span] = change
            crossed[head][span] = _mm_nt(u_ref[part, lanes], above)
            carried[head] = keep * (
                carried[head]
                + _mm_tn(q_ref[part, lanes], do_ref[part, lanes])
                - _mm_tn(w_ref[part, lanes], change)
            )
    lane_index = lax.broadcasted_iota(jnp.int32, logit.shape, 1)
    grad_logit = jnp.zeros(logit.shape, jnp.float32)
    for head in range(heads):
        lanes = slice(head * DK, (head + 1) * DK)
        taps = taps_ref[:, :, lanes]
        beta = jax.nn.sigmoid(_column(logit, first_head + head))
        acts, slopes = [], []
        for which in range(3):
            mixed = _convolved(
                ext_ref.at[head * 3 + which], pre_ref[which, :, lanes], halo_ref[which, :, lanes],
                taps[which], masks,
            )
            sig = jax.nn.sigmoid(mixed)
            acts.append(mixed * sig)
            slopes.append(sig * (1.0 + mixed * (1.0 - sig)))
        query_inv = lax.rsqrt(jnp.sum(acts[0] * acts[0], axis=-1, keepdims=True) + eps_unit)
        key_inv = lax.rsqrt(jnp.sum(acts[1] * acts[1], axis=-1, keepdims=True) + eps_unit)
        query = acts[0] * query_inv
        key = acts[1] * key_inv
        value = acts[2]
        grad_q, grad_k, grad_v, grad_b = [], [], [], []
        for pair in range(pairs):
            part = slice(pair * SPANROWS, (pair + 1) * SPANROWS)
            spans = (2 * pair, 2 * pair + 1)
            q_low, k_low = q_ref[part, lanes], k_ref[part, lanes]
            u_low, do_low = u_ref[part, lanes], do_ref[part, lanes]
            change = jnp.concatenate([changes[head][span] for span in spans], axis=0)
            solved = _mm_tn(t_ref[part, lanes], change)
            solved_low = solved.astype(jnp.bfloat16)
            both = [
                _mm_nt(
                    jnp.concatenate(
                        [
                            do_low[half * SPAN : (half + 1) * SPAN],
                            solved_low[half * SPAN : (half + 1) * SPAN],
                        ],
                        axis=0,
                    ),
                    s_ref[head, span],
                )
                for half, span in enumerate(spans)
            ]
            out_state = jnp.concatenate([both[0][:SPAN], both[1][:SPAN]], axis=0)
            solved_state = jnp.concatenate([both[0][SPAN:], both[1][SPAN:]], axis=0)
            weights = jnp.where(lower, _mm_nt(do_low, u_low), 0.0).astype(jnp.bfloat16)
            grad_q.append(out_state + _mm(weights, k_low))
            grad_low = jnp.where(strict, -_mm_nt(solved_low, u_low), 0.0)
            gram = _mm_nt(k_low, k_low)
            beta_part = beta[part]
            grad_gram = (grad_low * beta_part).astype(jnp.bfloat16)
            grad_k.append(
                _mm_tn(weights, q_low)
                + jnp.concatenate([crossed[head][span] for span in spans], axis=0)
                - beta_part * solved_state
                + _mm(grad_gram, k_low)
                + _mm_tn(grad_gram, k_low)
            )
            grad_v.append(beta_part * solved)
            grad_b.append(
                jnp.sum(grad_low * gram, axis=1, keepdims=True)
                + jnp.sum(solved * value[part] - solved_state * key[part], axis=1, keepdims=True)
            )
        grad_query = jnp.concatenate(grad_q, axis=0)
        grad_key = jnp.concatenate(grad_k, axis=0)
        grad_beta = jnp.concatenate(grad_b, axis=0)
        grad_logit = grad_logit + jnp.where(
            lane_index == first_head + head, grad_beta * beta * (1.0 - beta), 0.0
        )
        grad_acts = [
            (grad_query - query * jnp.sum(query * grad_query, axis=-1, keepdims=True)) * query_inv,
            (grad_key - key * jnp.sum(key * grad_key, axis=-1, keepdims=True)) * key_inv,
            jnp.concatenate(grad_v, axis=0),
        ]
        for which in range(3):
            grad_mixed = grad_acts[which] * slopes[which]
            pad = pad_ref.at[head * 3 + which]
            ext = ext_ref.at[head * 3 + which]
            pad[0:8] = jnp.zeros((8, DK), jnp.float32)
            pad[8 : 8 + rows] = grad_mixed
            pad[8 + rows : 16 + rows] = jnp.zeros((8, DK), jnp.float32)
            total = jnp.zeros((rows + 8, DK), jnp.float32)
            for shift in range(CONV):
                tap = CONV - 1 - shift
                shifted = pad[shift : shift + rows + 8] * back_masks[shift]
                total = total + taps[which, tap : tap + 1] * shifted
                dtaps_ref[which, tap : tap + 1, lanes] = jnp.sum(
                    shifted * ext[0 : rows + 8], axis=0, keepdims=True
                )
            dhalo_ref[which, :, lanes] = total[:8]
            dpre_ref[which, :, lanes] = total[8:].astype(jnp.bfloat16)
            tail_ref[which, :, lanes] = total[rows:]

    @pl.when(pl.program_id(0) == 0)
    def _():
        dlogit_ref[...] = grad_logit

    @pl.when(pl.program_id(0) > 0)
    def _():
        dlogit_ref[...] += grad_logit


HEADS_AT_ONCE = 2


def _specs(heads, rows):
    wide = heads * DK
    return dict(
        scal=pl.BlockSpec(memory_space=pltpu.SMEM),
        flat=pl.BlockSpec((rows, wide), lambda h: (0, h)),
        three=pl.BlockSpec((3, rows, wide), lambda h: (0, 0, h)),
        halo=pl.BlockSpec((3, 16, wide), lambda h: (0, 0, h)),
        edge=pl.BlockSpec((3, 8, wide), lambda h: (0, 0, h)),
        taps=pl.BlockSpec((3, CONV, wide), lambda h: (0, 0, h)),
        square=pl.BlockSpec((heads, DK, DK), lambda h: (h, 0, 0)),
        spans=pl.BlockSpec((heads, rows // SPAN, DK, DK), lambda h: (h, 0, 0, 0)),
        gain=pl.BlockSpec((1, DK), lambda h: (0, 0)),
        small=pl.BlockSpec((heads, 8, DK), lambda h: (h, 0, 0)),
    )


def _params():
    return pltpu.CompilerParams(
        dimension_semantics=("arbitrary",), vmem_limit_bytes=48 * 1024 * 1024
    )


def delta_local(scal, pre, halo, taps, logits):
    _, rows, width = pre.shape
    total = width // DK
    heads = min(HEADS_AT_ONCE, total)
    sp = _specs(heads, rows)
    table = pl.BlockSpec((rows, total), lambda h: (0, 0))
    low = jax.ShapeDtypeStruct((rows, width), jnp.bfloat16)
    return pl.pallas_call(
        partial(_local_kernel, heads),
        grid=(total // heads,),
        in_specs=[sp["scal"], sp["three"], sp["halo"], sp["taps"], table],
        out_specs=[sp["flat"]] * 5 + [sp["square"]] * 2,
        out_shape=[
            low,
            low,
            low,
            jax.ShapeDtypeStruct((rows, width), jnp.float32),
            low,
            jax.ShapeDtypeStruct((total, DK, DK), jnp.float32),
            jax.ShapeDtypeStruct((total, DK, DK), jnp.bfloat16),
        ],
        scratch_shapes=[pltpu.VMEM((3 * heads, rows + 8, DK), jnp.float32)],
        compiler_params=_params(),
        cost_estimate=pl.CostEstimate(flops=2 * 10**9, bytes_accessed=8 * 10**6, transcendentals=0),
        name="delta_local",
    )(scal, pre, halo, taps, logits)


def delta_apply(scal, q, k, w, uv, state_in, gate, gain):
    rows, width = q.shape
    total = width // DK
    heads = min(HEADS_AT_ONCE, total)
    sp = _specs(heads, rows)
    low = jax.ShapeDtypeStruct((rows, width), jnp.bfloat16)
    return pl.pallas_call(
        partial(_apply_kernel, heads),
        grid=(total // heads,),
        in_specs=[sp["scal"]] + [sp["flat"]] * 4 + [sp["square"], sp["flat"], sp["gain"]],
        out_specs=[sp["flat"]] * 3 + [sp["spans"]],
        out_shape=[
            low,
            jax.ShapeDtypeStruct((rows, width), jnp.float32),
            low,
            jax.ShapeDtypeStruct((total, rows // SPAN, DK, DK), jnp.bfloat16),
        ],
        compiler_params=_params(),
        cost_estimate=pl.CostEstimate(flops=2 * 10**9, bytes_accessed=8 * 10**6, transcendentals=0),
        name="delta_apply",
    )(scal, q, k, w, uv, state_in, gate, gain)


def delta_back_local(scal, dn, gate, gain, o, q, k, w):
    rows, width = q.shape
    total = width // DK
    heads = min(HEADS_AT_ONCE, total)
    sp = _specs(heads, rows)
    low = jax.ShapeDtypeStruct((rows, width), jnp.bfloat16)
    return pl.pallas_call(
        partial(_back_local_kernel, heads),
        grid=(total // heads,),
        in_specs=[sp["scal"], sp["flat"], sp["flat"], sp["gain"]] + [sp["flat"]] * 4,
        out_specs=[sp["flat"], sp["small"], sp["flat"], sp["flat"], sp["square"]],
        out_shape=[
            low,
            jax.ShapeDtypeStruct((total, 8, DK), jnp.float32),
            low,
            jax.ShapeDtypeStruct((rows, width), jnp.float32),
            jax.ShapeDtypeStruct((total, DK, DK), jnp.float32),
        ],
        compiler_params=_params(),
        cost_estimate=pl.CostEstimate(flops=2 * 10**9, bytes_accessed=8 * 10**6, transcendentals=0),
        name="delta_back_local",
    )(scal, dn, gate, gain, o, q, k, w)


def delta_back(scal, pre, halo, taps, logits, q, k, w, t, u, s, do, p, above):
    _, rows, width = pre.shape
    total = width // DK
    heads = min(HEADS_AT_ONCE, total)
    sp = _specs(heads, rows)
    table = pl.BlockSpec((rows, total), lambda h: (0, 0))
    edge = jax.ShapeDtypeStruct((3, 8, width), jnp.float32)
    return pl.pallas_call(
        partial(_back_kernel, heads),
        grid=(total // heads,),
        in_specs=[sp["scal"], sp["three"], sp["halo"], sp["taps"], table]
        + [sp["flat"]] * 5
        + [sp["spans"], sp["flat"], sp["flat"], sp["square"]],
        out_specs=[sp["three"], sp["edge"], sp["edge"], sp["taps"], table],
        out_shape=[
            jax.ShapeDtypeStruct((3, rows, width), jnp.bfloat16),
            edge,
            edge,
            jax.ShapeDtypeStruct((3, CONV, width), jnp.float32),
            jax.ShapeDtypeStruct((rows, total), jnp.float32),
        ],
        scratch_shapes=[
            pltpu.VMEM((3 * heads, rows + 8, DK), jnp.float32),
            pltpu.VMEM((3 * heads, rows + 16, DK), jnp.float32),
        ],
        compiler_params=_params(),
        cost_estimate=pl.CostEstimate(
            flops=4 * 10**9, bytes_accessed=12 * 10**6, transcendentals=0
        ),
        name="delta_back",
    )(scal, pre, halo, taps, logits, q, k, w, t, u, s, do, p, above)


def ring_order(count):
    return list(range(0, count, 2)) + list(range(count - 1, 0, -2))


def ring_pairs(count):
    order = ring_order(count)
    return [(order[place], order[(place + 1) % count]) for place in range(count)]


def send_up(value):
    return lax.ppermute(value, "seq", ring_pairs(lax.axis_size("seq")))


def send_down(value):
    return lax.ppermute(value, "seq", [(b, a) for a, b in ring_pairs(lax.axis_size("seq"))])


def ring_place():
    count = lax.axis_size("seq")
    index = lax.axis_index("seq")
    return jnp.where(index % 2 == 0, index // 2, count - (index + 1) // 2)


def to_ring(value):
    count = lax.axis_size("seq")
    piece = value.shape[-1] // count
    parts = [value[..., one * piece : (one + 1) * piece] for one in ring_order(count)]
    doubled = jnp.concatenate(parts + parts[:-1], axis=-1)
    return lax.dynamic_slice_in_dim(doubled, ring_place() * piece, count * piece, value.ndim - 1)


def from_ring(value):
    count = lax.axis_size("seq")
    piece = value.shape[-1] // count
    doubled = jnp.concatenate([value, value[..., : (count - 1) * piece]], axis=-1)
    start = lax.rem(count - ring_place(), count) * piece
    placed = lax.dynamic_slice_in_dim(doubled, start, count * piece, value.ndim - 1)
    order = ring_order(count)
    parts = []
    for one in range(count):
        place = order.index(one)
        parts.append(placed[..., place * piece : (place + 1) * piece])
    return jnp.concatenate(parts, axis=-1)


def ring_gather(first, second):
    count = lax.axis_size("seq")
    half = count // 2
    one = {0: first}
    two = {0: second}
    for step in range(1, half + 1):
        one[count - step] = send_up(one[(count - step + 1) % count])
        two[step] = send_down(two[step - 1])
        if step < half:
            one[step] = send_down(one[step - 1])
            two[count - step] = send_up(two[(count - step + 1) % count])
    late = (one[count - half + 1], two[half - 1])
    return [one[key] for key in range(count)], [two[key] for key in range(count)], late


def ring_scatter(first, second):
    count = lax.axis_size("seq")
    half = count // 2

    def low(value):
        return value.astype(jnp.bfloat16)

    one_up, one_down = low(first(half)), low(first(half + 1))
    two_up, two_down = low(second(half - 1)), low(second(half))
    for step in range(1, half):
        one_up = low(first(half - step) + send_up(one_up).astype(jnp.float32))
        two_down = low(second(half + step) + send_down(two_down).astype(jnp.float32))
        if step < half - 1:
            one_down = low(first(half + 1 + step) + send_down(one_down).astype(jnp.float32))
            two_up = low(second(half - 1 - step) + send_up(two_up).astype(jnp.float32))
    one = first(0) + send_up(one_up).astype(jnp.float32) + send_down(one_down).astype(jnp.float32)
    two = second(0) + send_up(two_up).astype(jnp.float32) + send_down(two_down).astype(jnp.float32)
    return one, two


def swap(value, axis, bit):
    count = lax.axis_size(axis)
    return lax.ppermute(value, axis, [(one, one ^ bit) for one in range(count)])


def gather_small(value):
    index = lax.axis_index("seq")
    held = value[None]
    bit = 1
    while bit < lax.axis_size("seq"):
        other = swap(held, "seq", bit)
        mine_first = (index & bit) == 0
        held = jnp.where(
            mine_first,
            jnp.concatenate([held, other], axis=0),
            jnp.concatenate([other, held], axis=0),
        )
        bit *= 2
    return held


def scatter_small(value):
    index = lax.axis_index("seq")
    held = value
    bit = lax.axis_size("seq") // 2
    while bit >= 1:
        low, high = held[: held.shape[0] // 2], held[held.shape[0] // 2 :]
        upper = (index & bit) != 0
        got = swap(jnp.where(upper, low, high), "seq", bit)
        held = jnp.where(upper, high, low) + got
        bit //= 2
    return held[0]


def own_half(value):
    rows = value.shape[0] // 2
    return lax.dynamic_slice_in_dim(value, (lax.axis_index("head") & 1) * rows, rows, 0)


def other_half(value):
    rows = value.shape[0] // 2
    return lax.dynamic_slice_in_dim(value, (1 - (lax.axis_index("head") & 1)) * rows, rows, 0)


def both_halves(value):
    other = swap(value, "head", 1)
    return jnp.where(
        (lax.axis_index("head") & 1) == 0,
        jnp.concatenate([value, other], axis=0),
        jnp.concatenate([other, value], axis=0),
    )


def summed_half(partial_rows):
    low = partial_rows.astype(jnp.bfloat16)
    pair = own_half(partial_rows) + swap(other_half(low), "head", 1).astype(jnp.float32)
    total = pair
    bit = 2
    while bit < lax.axis_size("head"):
        total = total + swap(total.astype(jnp.bfloat16), "head", bit).astype(jnp.float32)
        bit *= 2
    return total


def chunk_of(value, index):
    piece = value.shape[-1] // lax.axis_size("seq")
    return value[..., index * piece : (index + 1) * piece]


def dot(a, b):
    return jnp.dot(a, b, preferred_element_type=jnp.float32)


def dot_tn(a, b):
    return lax.dot_general(a, b, (((0,), (0,)), ((), ())), preferred_element_type=jnp.float32)


def dot_nt(a, b):
    return lax.dot_general(a, b, (((1,), (1,)), ((), ())), preferred_element_type=jnp.float32)


def after(values, others):
    return lax.optimization_barrier((values, others))[0]


def passed_along(value, steps):
    count = lax.axis_size("seq")
    leading, last = (max(0, -steps), min(count, count - steps))
    return lax.ppermute(
        value, "seq", [(source, source + steps) for source in range(leading, last)]
    )


def adam_update(master, first_m, second_m, gradient, step_rate, decay_rate):
    first_new = beta_one * first_m + (1.0 - beta_one) * gradient
    second_new = beta_two * second_m + (1.0 - beta_two) * gradient * gradient
    first_hat = first_new / (1.0 - beta_one**STEP)
    second_hat = second_new / (1.0 - beta_two**STEP)
    master_new = master - step_rate * (
        first_hat / (jnp.sqrt(second_hat) + eps_adam) + decay_rate * master
    )
    return (master_new, first_new, second_new)


def norm_back(rows, inv, gain, grad):
    weighted = grad * gain
    mean = jnp.mean(weighted * rows, axis=-1, keepdims=True)
    return inv * weighted - rows * (inv * inv * inv) * mean


def inverse_size(rows):
    return lax.rsqrt(jnp.mean(rows * rows, axis=-1, keepdims=True) + eps_norm)


def per_device(
    block_input, cotangent, lengths,
    proj_master, proj_first, proj_second,
    beta_master, beta_first, beta_second,
    conv_master, conv_first, conv_second,
    out_master, out_first, out_second,
    mlp_master, mlp_first, mlp_second,
    down_master, down_first, down_second,
    gains_master, gains_first, gains_second,
):
    bf16, f32 = jnp.bfloat16, jnp.float32
    count = lax.axis_size("seq")
    seq_index = lax.axis_index("seq")
    rows = block_input.shape[0]
    width = proj_master.shape[2]
    units = mlp_master.shape[2]
    shard = proj_master.shape[1]
    heads = width // DK
    scal = jnp.stack([lengths[0] - seq_index * rows, seq_index * rows]).astype(jnp.int32)
    qkv = jnp.transpose(proj_master[:3], (1, 0, 2)).reshape(shard, 3 * width).astype(bf16)
    wide = 3 * width // 2
    w_qkv_a, w_qkv_b, late = ring_gather(qkv[:, :wide], qkv[:, wide:])
    w_gate, w_out, late = ring_gather(
        *after((proj_master[3].astype(bf16), out_master.astype(bf16)), late)
    )
    cut = (units // 2 + DK - 1) // DK * DK
    down_low = down_master.astype(bf16)
    w_down_a, w_down_b, late = ring_gather(*after((down_low[:cut], down_low[cut:]), late))
    mlp_low = mlp_master.astype(bf16)
    w_mlp_g, w_mlp_u, late = ring_gather(*after((mlp_low[0], mlp_low[1]), late))
    sizes = [conv_master.size, beta_master.size, gains_master.size]
    packed = jnp.concatenate(
        [conv_master.reshape(-1), beta_master.reshape(-1), gains_master.reshape(-1)]
    ).astype(bf16)
    packed = jnp.pad(packed, (0, -packed.size % 2048))
    small = gather_small(packed)
    conv_all = small[:, : sizes[0]].reshape(count, 3, CONV, -1)
    taps = jnp.transpose(conv_all, (1, 2, 0, 3)).reshape(3, CONV, width).astype(f32)
    beta_all = small[:, sizes[0] : sizes[0] + sizes[1]].reshape(D, heads)
    gains_all = small[:, sizes[0] + sizes[1] : sum(sizes)].reshape(-1)
    columns = to_ring(
        jnp.concatenate([gains_all[: 2 * D].reshape(2, D), jnp.transpose(beta_all)], axis=0)
    )
    gain_a = columns[0:1].astype(f32)
    gain_m = columns[1:2].astype(f32)
    w_beta = columns[2:]
    gain_o = gains_all[2 * D :].astype(f32)[None]
    x_ring = to_ring(block_input)
    dy_ring = to_ring(cotangent)
    x_rows = x_ring.astype(f32)
    x_inv = inverse_size(x_rows)
    hidden = (x_rows * x_inv * gain_a).astype(bf16)
    logits = dot_nt(hidden, w_beta)

    def over_chunks(value, weights, order):
        total = None
        for one in order:
            term = dot(chunk_of(value, one), weights[one])
            total = term if total is None else total + term
        return total

    order = [0]
    for step in range(1, count // 2):
        order += [count - step, step]
    order.append(count // 2)
    pre = jnp.concatenate(
        [over_chunks(hidden, w_qkv_a, order), over_chunks(hidden, w_qkv_b, order)], axis=1
    ).astype(bf16)
    pre = jnp.transpose(pre.reshape(rows, 3, width), (1, 0, 2))
    halo = passed_along(pre[:, rows - 16 :], 1)
    q, k, w, uv, t, state_add, state_map = delta_local(scal, pre, halo, taps, logits)
    gate = over_chunks(hidden, w_gate, order)
    hops = -(-5 * count // 8) - 1
    state_in = passed_along(state_add.astype(bf16), 1)
    for _ in range(hops - 1):
        moved = jnp.einsum("hij,hjk->hik", state_map, state_in, preferred_element_type=f32)
        state_in = passed_along((moved + state_add).astype(bf16), 1)
    normed, out_rows, change, states = delta_apply(scal, q, k, w, uv, state_in, gate, gain_o)
    attn_part = jnp.concatenate([dot(normed, w_out[one]) for one in range(count)], axis=1)
    x_one = own_half(x_rows) + summed_half(attn_part)
    one_inv = inverse_size(x_one)
    h_two = both_halves((x_one * one_inv * gain_m).astype(bf16))
    grad_act_a = None
    grad_act_b = None
    for one in order:
        term_a = dot_nt(chunk_of(dy_ring, one), w_down_a[one])
        term_b = dot_nt(chunk_of(dy_ring, one), w_down_b[one])
        grad_act_a = term_a if grad_act_a is None else grad_act_a + term_a
        grad_act_b = term_b if grad_act_b is None else grad_act_b + term_b
    grad_act = jnp.concatenate([grad_act_a, grad_act_b], axis=1)
    gate_u = over_chunks(h_two, w_mlp_g, order)
    up_u = over_chunks(h_two, w_mlp_u, order)
    sig = jax.nn.sigmoid(gate_u)
    act = gate_u * sig
    act_low = (act * up_u).astype(bf16)
    grad_gate_u = (grad_act * up_u * (sig * (1.0 + gate_u * (1.0 - sig)))).astype(bf16)
    grad_up_u = (grad_act * act).astype(bf16)
    grad_h_part = jnp.concatenate(
        [
            dot_nt(grad_gate_u, w_mlp_g[one]) + dot_nt(grad_up_u, w_mlp_u[one])
            for one in range(count)
        ],
        axis=1,
    )
    grad_h_two = summed_half(grad_h_part)
    x_half_grad = norm_back(x_one, one_inv, gain_m, grad_h_two)
    grad_gain_m = 0.5 * jnp.sum(grad_h_two * x_one * one_inv, axis=0, keepdims=True)
    grad_x_one = own_half(dy_ring).astype(f32) + x_half_grad
    grad_attn = both_halves(grad_x_one.astype(bf16))
    down_a_sum, down_b_sum = ring_scatter(
        lambda one: dot_tn(act_low[:, :cut], chunk_of(dy_ring, one)),
        lambda one: dot_tn(act_low[:, cut:], chunk_of(dy_ring, one)),
    )
    mlp_g_sum, mlp_u_sum = ring_scatter(
        lambda one: dot_tn(chunk_of(h_two, one), grad_gate_u),
        lambda one: dot_tn(chunk_of(h_two, one), grad_up_u),
    )
    mlp_part = jnp.concatenate(
        [
            dot(act_low[:, :cut], w_down_a[one]) + dot(act_low[:, cut:], w_down_b[one])
            for one in range(count)
        ],
        axis=1,
    )
    result = from_ring(both_halves(x_one + summed_half(mlp_part)))
    grad_normed = sum(dot_nt(chunk_of(grad_attn, one), w_out[one]) for one in range(count))
    grad_gate, grad_gain_o, grad_out, through, carry = delta_back_local(
        scal, grad_normed, gate, gain_o, out_rows, q, k, w
    )
    gate_sum, out_sum = ring_scatter(
        lambda one: dot_tn(chunk_of(hidden, one), grad_gate),
        lambda one: dot_tn(normed, chunk_of(grad_attn, one)),
    )
    above = passed_along(carry.astype(bf16), -1)
    for _ in range(hops - 1):
        moved = jnp.einsum("hji,hjk->hik", state_map, above, preferred_element_type=f32)
        above = passed_along((moved + carry).astype(bf16), -1)
    grad_pre, tail, back_halo, grad_taps, grad_logits = delta_back(
        scal, pre, halo, taps, logits, q, k, w, t, change, states, grad_out, through, above
    )
    fixed = (tail + passed_along(back_halo, -1)).astype(bf16)
    grad_pre = lax.dynamic_update_slice_in_dim(grad_pre, fixed, rows - 8, 1)
    grad_qkv = jnp.transpose(grad_pre, (1, 0, 2)).reshape(rows, 3 * width)
    grad_logits = grad_logits.astype(bf16)
    qkv_a_sum, qkv_b_sum = ring_scatter(
        lambda one: dot_tn(chunk_of(hidden, one), grad_qkv[:, :wide]),
        lambda one: dot_tn(chunk_of(hidden, one), grad_qkv[:, wide:]),
    )
    grad_hidden = jnp.concatenate(
        [
            dot_nt(grad_qkv[:, :wide], w_qkv_a[one])
            + dot_nt(grad_qkv[:, wide:], w_qkv_b[one])
            + dot_nt(grad_gate, w_gate[one])
            for one in range(count)
        ],
        axis=1,
    ) + dot(grad_logits, w_beta)
    grad_gain_a = jnp.sum(grad_hidden * x_rows * x_inv, axis=0, keepdims=True)
    grad_hidden_half = summed_half(grad_hidden)
    grad_x_rest = norm_back(own_half(x_rows), own_half(x_inv), gain_a, grad_hidden_half)
    input_grad = from_ring(both_halves(grad_x_one + grad_x_rest))
    grad_beta = dot_tn(grad_logits, hidden)
    stacked = from_ring(jnp.concatenate([grad_gain_a, grad_gain_m, grad_beta], axis=0))
    grad_gains = jnp.concatenate(
        [stacked[:2].reshape(-1), jnp.sum(grad_gain_o[:, 0], axis=0)]
    ).reshape(count, -1)
    grad_conv = jnp.transpose(
        grad_taps.reshape(3, CONV, count, width // count), (2, 0, 1, 3)
    ).reshape(count, -1)
    grad_beta = jnp.transpose(stacked[2:]).reshape(count, -1)
    small_sum = scatter_small(jnp.concatenate([grad_conv, grad_beta, grad_gains], axis=1))
    gains_sum = small_sum[sizes[0] + sizes[1] :]
    bit = 1
    while bit < lax.axis_size("head"):
        gains_sum = gains_sum + swap(gains_sum, "head", bit)
        bit *= 2
    summed_conv = small_sum[: sizes[0]].reshape(conv_master.shape)
    summed_beta = small_sum[sizes[0] : sizes[0] + sizes[1]].reshape(beta_master.shape)
    qkv_sum = jnp.concatenate([qkv_a_sum, qkv_b_sum], axis=1).reshape(shard, 3, width)
    summed_proj = jnp.concatenate([jnp.transpose(qkv_sum, (1, 0, 2)), gate_sum[None]], axis=0)
    summed_mlp = jnp.stack([mlp_g_sum, mlp_u_sum])
    summed_down = jnp.concatenate([down_a_sum, down_b_sum], axis=0)
    proj_new, proj_first_new, proj_second_new = adam_update(
        proj_master, proj_first, proj_second, summed_proj, rate_matrix, decay_matrix
    )
    beta_new, beta_first_new, beta_second_new = adam_update(
        beta_master, beta_first, beta_second, summed_beta, rate_beta, decay_matrix
    )
    conv_new, conv_first_new, conv_second_new = adam_update(
        conv_master, conv_first, conv_second, summed_conv, rate_conv, decay_matrix
    )
    out_new, out_first_new, out_second_new = adam_update(
        out_master, out_first, out_second, out_sum, rate_matrix, decay_matrix
    )
    mlp_new, mlp_first_new, mlp_second_new = adam_update(
        mlp_master, mlp_first, mlp_second, summed_mlp, rate_matrix, decay_matrix
    )
    down_new, down_first_new, down_second_new = adam_update(
        down_master, down_first, down_second, summed_down, rate_down, decay_matrix
    )
    gains_new, gains_first_new, gains_second_new = adam_update(
        gains_master, gains_first, gains_second, gains_sum, rate_gains, 0.0
    )
    return (
        result,
        input_grad,
        proj_new, proj_first_new, proj_second_new, proj_new.astype(bf16),
        beta_new, beta_first_new, beta_second_new, beta_new.astype(bf16),
        conv_new, conv_first_new, conv_second_new, conv_new.astype(bf16),
        out_new, out_first_new, out_second_new, out_new.astype(bf16),
        mlp_new, mlp_first_new, mlp_second_new, mlp_new.astype(bf16),
        down_new, down_first_new, down_second_new, down_new.astype(bf16),
        gains_new, gains_first_new, gains_second_new,
    )


def solution(mesh):
    rows = P("seq", None)
    proj = P(None, "seq", "head")
    tall = P("seq", "head")
    conv = P(None, None, ("head", "seq"))
    flat = P("head", "seq")
    gains = P("seq")
    return jax.shard_map(
        per_device,
        mesh=mesh,
        in_specs=(rows, rows, P())
        + (proj,) * 3
        + (tall,) * 3
        + (conv,) * 3
        + (flat,) * 3
        + (proj,) * 3
        + (flat,) * 3
        + (gains,) * 3,
        out_specs=(rows, rows)
        + (proj,) * 4
        + (tall,) * 4
        + (conv,) * 4
        + (flat,) * 4
        + (proj,) * 4
        + (flat,) * 4
        + (gains,) * 3,
        check_vma=False,
    )
```

time: 2070 us -> 910 us (0.44)
  waiting for transfers between devices: 1010 us -> 304 us
  other arithmetic: 285 us -> 72.9 us
  matrix products: 359 us -> 180 us
  blocking collectives: 143 us -> 0 us
  starting transfers between devices: 47.4 us -> 183 us
  local copies, waits for them, and re-layouts: 203 us -> 111 us
  Pallas kernels: 0 us -> 43.2 us
    reduce_scatter x4 -> x0, waiting for transfers between devices: 458 us -> none  [the longest x1 179 us: per_device(): lax.psum_scatter(grad_mlp.astype(jnp.bfloat16), 'seq', scatter_dimension=...]
    all_gather x4 -> x0, waiting for transfers between devices: 268 us -> none  [the longest x1 161 us: per_device(): lax.all_gather(mlp_master.astype(jnp.bfloat16), 'seq', axis=1, tiled=True)]
    ppermute x16 -> x142, waiting for transfers between devices: 63.5 us -> 304 us  [the longest x56 129 us: send_up(): return lax.ppermute(value, 'seq', ring_pairs(lax.axis_size('seq')))]
    psum x3 -> x0, waiting for transfers between devices: 172 us -> none  [the longest x1 86.3 us: per_device(): lax.psum(jnp.dot(act_low, w_down, preferred_element_type=jnp.float32).ast...]
    dot_general x115 -> x201, matrix products: 345 us -> 180 us  [the longest x65 61.3 us: dot(): return jnp.dot(a, b, preferred_element_type=jnp.float32)]
    another operation x4 -> x5, other arithmetic: 161 us -> 0.19 us  [the longest x3 161 us: prepare(): lax.linalg.triangular_solve(system, beta_c[..., None] * key_c, left_side=...]
    ppermute x16 -> x142, starting transfers between devices: 45.9 us -> 183 us  [the longest x56 81.8 us: send_up(): return lax.ppermute(value, 'seq', ring_pairs(lax.axis_size('seq')))]
    unnamed x2 -> x0, blocking collectives: 77.7 us -> none
  transfers between devices with their start and end apart: 29 -> 142, of which waited for: 25 -> 60; matrix products, arithmetic and copies ran while one was open for 24% -> 31% of each run, Pallas kernels for 0% -> 5%
where the time goes in v1:
time: 910 us; the launch traced here: 899 us
  waiting for transfers between devices  304 us (33%)
  starting transfers between devices  183 us (20%)
  matrix products  180 us (20%)
  local copies, waits for them, and re-layouts  111 us (12%)
  other arithmetic  72.9 us (8%)
  Pallas kernels  43.2 us (5%)
    ppermute x56, waiting for transfers between devices, send_up(): return lax.ppermute(value, 'seq', ring_pairs(lax.axis_size('seq')))  129 us
    ppermute x56, waiting for transfers between devices, send_down(): lax.ppermute(value, 'seq', [(b, a) for a, b in ring_pairs(lax.axis_size('...  125 us
    ppermute x56, starting transfers between devices, send_up(): return lax.ppermute(value, 'seq', ring_pairs(lax.axis_size('seq')))  81.8 us
    unnamed x414, local copies, waits for them, and re-layouts  78.4 us
    dot_general x65, matrix products, dot(): return jnp.dot(a, b, preferred_element_type=jnp.float32)  61.3 us
    dot_general x65, matrix products, dot_tn(): lax.dot_general(a, b, (((0,), (0,)), ((), ())), preferred_element_type=jn...  60.5 us
    ppermute x56, starting transfers between devices, send_down(): lax.ppermute(value, 'seq', [(b, a) for a, b in ring_pairs(lax.axis_size('...  59.5 us
    dot_general x65, matrix products, dot_nt(): lax.dot_general(a, b, (((1,), (1,)), ((), ())), preferred_element_type=jn...  57 us
  transfers between devices with their start and end apart: 142, of which 60 were waited for; matrix products, arithmetic and copies ran while one was open for 31% of the time, Pallas kernels for 5%

profile of v1, /device:TPU:0, one launch (start us, length us, event | category | flops | bytes accessed | tf_op | source)
XLA Modules:
  0.0 898.6 jit_solution(3318824804457063065)
XLA Ops:
  84.4 7.3 collective-permute-done.13
  96.7 9.0 %collective-permute-done.15 = bf16[256,768]{0,1:T(8,128)(2,1)S(1)} collective-permute-done((bf16[256,768]{0,1:T(8,128)(2,1)S(1)}, bf16[256,768]{0,1:T(8,128)(2,1)S(1)}, u32[]{:S(2)}, u32[]{:S(2)}) %collective-permute-start.15) | collective-permute-done | bytes 393248 | tf_op jit(solution)/shard_map/ppermute | solution.py:572
  120.8 5.3 collective-permute-done.9
  139.3 10.8 %delta_local.1 = (bf16[512,512]{1,0:T(8,128)(2,1)S(1)}, bf16[512,512]{1,0:T(8,128)(2,1)S(1)}, bf16[512,512]{1,0:T(8,128)(2,1)S(1)}, f32[512,512]{1,0:T(8,128)S(1...) custom-call(s32[2]{0:T(128)S(1)} %pad_add_fusion.scal_ref, ...), custom_call_target="tpu_custom_call" | custom-call | flops 2000000000 | bytes 8000000 | tf_op jit(solution)/shard_map/delta_local/pallas_call | solution.py:457
  178.4 5.1 collective-permute-done.28
  193.0 6.7 delta_apply.1
  224.8 6.2 collective-permute-done.40
  239.3 5.6 collective-permute-done.41
  247.3 8.0 collective-permute-done.37
  269.2 18.7 %collective-permute-done.62 = bf16[768,256]{1,0:T(8,128)(2,1)S(1)} collective-permute-done((bf16[768,256]{1,0:T(8,128)(2,1)S(1)}, bf16[768,256]{1,0:T(8,128)(2,1)S(1)}, u32[]{:S(2)}, u32[]{:S(2)}) %collective-permute-start.62) | collective-permute-done | bytes 393248 | tf_op jit(solution)/shard_map/ppermute | solution.py:568
  290.4 12.9 %collective-permute-done.47 = bf16[256,1408]{1,0:T(8,128)(2,1)S(1)} collective-permute-done((bf16[256,1408]{1,0:T(8,128)(2,1)S(1)}, bf16[256,1408]{1,0:T(8,128)(2,1)S(1)}, u32[]{:S(2)}, u32[]{:S(2)}) %collective-permute-start.47) | collective-permute-done | bytes 720928 | tf_op jit(solution)/shard_map/ppermute | solution.py:568
  320.2 9.9 %collective-permute-done.57 = bf16[256,1408]{1,0:T(8,128)(2,1)} collective-permute-done((bf16[256,1408]{1,0:T(8,128)(2,1)S(1)}, bf16[256,1408]{1,0:T(8,128)(2,1)}, u32[]{:S(2)}, u32[]{:S(2)}) %collective-permute-start.57) | collective-permute-done | bytes 720928 | tf_op jit(solution)/shard_map/ppermute | solution.py:572
  352.1 7.5 collective-permute-done.58
  406.3 7.0 collective-permute-done.126
  416.3 19.1 %collective-permute-done.134 = bf16[640,256]{1,0:T(8,128)(2,1)S(1)} collective-permute-done((bf16[640,256]{1,0:T(8,128)(2,1)S(1)}, bf16[640,256]{1,0:T(8,128)(2,1)S(1)}, u32[]{:S(2)}, u32[]{:S(2)}) %collective-permute-start.134) | collective-permute-done | bytes 327712 | tf_op jit(solution)/shard_map/ppermute | solution.py:568
  440.2 14.2 %collective-permute-done.116 = bf16[256,1408]{1,0:T(8,128)(2,1)S(1)} collective-permute-done((bf16[256,1408]{1,0:T(8,128)(2,1)S(1)}, bf16[256,1408]{1,0:T(8,128)(2,1)S(1)}, u32[]{:S(2)}, u32[]{:S(2)}) %collective-permute-start.116) | collective-permute-done | bytes 720928 | tf_op jit(solution)/shard_map/ppermute | solution.py:572
  457.7 12.2 %collective-permute-done.122 = bf16[256,1408]{1,0:T(8,128)(2,1)S(1)} collective-permute-done((bf16[256,1408]{1,0:T(8,128)(2,1)S(1)}, bf16[256,1408]{1,0:T(8,128)(2,1)S(1)}, u32[]{:S(2)}, u32[]{:S(2)}) %collective-permute-start.122) | collective-permute-done | bytes 720928 | tf_op jit(solution)/shard_map/ppermute | solution.py:572
  472.7 5.6 collective-permute-done.131
  490.9 12.2 %collective-permute-done.128 = bf16[768,256]{1,0:T(8,128)(2,1)S(1)} collective-permute-done((bf16[768,256]{1,0:T(8,128)(2,1)S(1)}, bf16[768,256]{1,0:T(8,128)(2,1)S(1)}, u32[]{:S(2)}, u32[]{:S(2)}) %collective-permute-start.128) | collective-permute-done | bytes 393248 | tf_op jit(solution)/shard_map/ppermute | solution.py:568
  534.5 5.0 fusion.467
  539.5 16.9 %collective-permute-done.71 = bf16[256,2048]{0,1:T(8,128)(2,1)} collective-permute-done((bf16[256,2048]{0,1:T(8,128)(2,1)}, bf16[256,2048]{0,1:T(8,128)(2,1)}, u32[]{:S(2)}, u32[]{:S(2)}) %collective-permute-start.71) | collective-permute-done | bytes 1048608 | tf_op jit(solution)/shard_map/ppermute | solution.py:640
  563.9 6.7 collective-permute-done.124
  601.4 9.0 %delta_back_local.1 = (bf16[512,512]{1,0:T(8,128)(2,1)S(1)}, f32[4,8,128]{2,1,0:T(8,128)S(1)}, bf16[512,512]{1,0:T(8,128)(2,1)S(1)}, f32[512,512]{1,0:T(8,128)S(1)}, f32[4,128,128]{2,1,0:T(8,128)S(1)}) custom-call(s32[2]{0:T(128)S(1)} %pad_add_fusion.scal_ref, f32[512,512]{1,0:T(8,128)S(1)} %fusion.34.dn_ref, f32[512,512]{1,0:T(8,128)S(1)} %copy-done.1, ...), custom_call_target="tpu_custom_call" | custom-call | flops 2000000000 | bytes 8000000 | tf_op jit(solution)/shard_map/delta_back_local/pallas_call | solution.py:507
  655.1 16.6 %delta_back.1 = (bf16[3,512,512]{2,1,0:T(8,128)(2,1)}, f32[3,8,512]{2,1,0:T(8,128)S(1)}, f32[3,8,512]{2,1,0:T(8,128)S(1)}, f32[3,4,512]{2,1,0:T(4,128)S(1)}, f32[512,4]{1,0:T(8,128)S(1)}) custom-call(s32[2]{0:T(128)S(1)} %pad_add_fusion.scal_ref, bf16[3,512,512]{2,1,0:T(8,128)(2,1)} %bitcast.253, bf16[3,16,512]{2,1,0:T(8,128)(2,1)S(1)} %collective-permute-done.17.halo_ref, ...), custom_call_target="tpu_custom_call" | custom-call | flops 4000000000 | bytes 12000000 | tf_op jit(solution)/shard_map/delta_back/pallas_call | solution.py:532
  743.0 5.4 collective-permute-done.81
  764.9 6.3 maximum_select_fusion
  791.4 5.3 collective-permute-done.92
  816.4 5.5 collective-permute-done.84
  833.1 6.9 fusion.477
  858.2 8.6 fusion
  877.3 5.3 copy.221
  893.1 5.3 copy.220
  (1010 shorter events, 607.4 us)
Async XLA Ops:
  5.8 67.4 %collective-permute-start.3 = (bf16[256,768]{0,1:T(8,128)(2,1)}, bf16[256,768]{0,1:T(8,128)(2,1)}, u32[]{:S(2)}, u32[]{:S(2)}) collective-permute-start(bf16[256,768]{0,1:T(8,128)(2,1)} %get-tuple-element.256), channel_id=1, source_target_pairs={{0,8},{8,16},{16,24},{24,28},{28,20},{20,12},{12,4},{4,0},{1,9},{9... | collective-permute-start | bytes 1179656 | tf_op jit(solution)/shard_map/ppermute | solution.py:568
  8.8 62.3 %collective-permute-start.4 = (bf16[256,768]{0,1:T(8,128)(2,1)}, bf16[256,768]{0,1:T(8,128)(2,1)}, u32[]{:S(2)}, u32[]{:S(2)}) collective-permute-start(bf16[256,768]{0,1:T(8,128)(2,1)} %get-tuple-element.256), channel_id=1, source_target_pairs={{8,0},{16,8},{24,16},{28,24},{20,28},{12,20},{4,12},{0,4},{9,1},{1... | collective-permute-start | bytes 1179656 | tf_op jit(solution)/shard_map/ppermute | solution.py:572
  8.8 67.4 %collective-permute-start.11 = (bf16[256,768]{0,1:T(8,128)(2,1)}, bf16[256,768]{0,1:T(8,128)(2,1)}, u32[]{:S(2)}, u32[]{:S(2)}) collective-permute-start(bf16[256,768]{0,1:T(8,128)(2,1)} %get-tuple-element.257), channel_id=1, source_target_pairs={{8,0},{16,8},{24,16},{28,24},{20,28},{12,20},{4,12},{0,4},{9,1},{1... | collective-permute-start | bytes 1179656 | tf_op jit(solution)/shard_map/ppermute | solution.py:572
  10.8 67.4 %collective-permute-start.10 = (bf16[256,768]{0,1:T(8,128)(2,1)}, bf16[256,768]{0,1:T(8,128)(2,1)}, u32[]{:S(2)}, u32[]{:S(2)}) collective-permute-start(bf16[256,768]{0,1:T(8,128)(2,1)} %get-tuple-element.257), channel_id=1, source_target_pairs={{0,8},{8,16},{16,24},{24,28},{28,20},{20,12},{12,4},{4,0},{1,9},{9... | collective-permute-start | bytes 1179656 | tf_op jit(solution)/shard_map/ppermute | solution.py:568
  11.9 36.7 %collective-permute-start = (bf16[1,4096]{1,0:T(2,128)(2,1)}, bf16[1,4096]{1,0:T(2,128)(2,1)}, u32[]{:S(2)}, u32[]{:S(2)}) collective-permute-start(bf16[1,4096]{1,0:T(2,128)(2,1)} %broadcast_in_dim.19), channel_id=1, source_target_pairs={{0,4},{4,0},{8,12},{12,8},{16,20},{20,16},{24,28},{28,24},{1,5},{5... | collective-permute-start | bytes 24584 | tf_op jit(solution)/shard_map/ppermute | solution.py:640
  117.9 35.4 %collective-permute-start.25 = (bf16[256,512]{0,1:T(8,128)(2,1)}, bf16[256,512]{0,1:T(8,128)(2,1)}, u32[]{:S(2)}, u32[]{:S(2)}) collective-permute-start(bf16[256,512]{0,1:T(8,128)(2,1)} %collective-permute-done.23), channel_id=1, source_target_pairs={{8,0},{16,8},{24,16},{28,24},{20,28},{12,20},{4,12},{0,4},{9,1},{1... | collective-permute-start | bytes 786440 | tf_op jit(solution)/shard_map/ppermute | solution.py:572
  158.1 46.6 %collective-permute-start.35 = (bf16[512,256]{1,0:T(8,128)(2,1)}, bf16[512,256]{1,0:T(8,128)(2,1)}, u32[]{:S(2)}, u32[]{:S(2)}) collective-permute-start(bf16[512,256]{1,0:T(8,128)(2,1)} %collective-permute-done.34), channel_id=1, source_target_pairs={{0,8},{8,16},{16,24},{24,28},{28,20},{20,12},{12,4},{4,0},{1,9},{9... | collective-permute-start | bytes 786440 | tf_op jit(solution)/shard_map/ppermute | solution.py:568
  171.5 44.1 %collective-permute-start.39 = (bf16[768,256]{1,0:T(8,128)(2,1)S(1)}, bf16[768,256]{1,0:T(8,128)(2,1)}, u32[]{:S(2)}, u32[]{:S(2)}) collective-permute-start(bf16[768,256]{1,0:T(8,128)(2,1)S(1)} %copy-done.39), channel_id=1, source_target_pairs={{0,8},{8,16},{16,24},{24,28},{28,20},{20,12},{12,4},{4,0},{1,9},{9... | collective-permute-start | bytes 1179656 | tf_op jit(solution)/shard_map/ppermute | solution.py:568
  171.8 41.5 %collective-permute-start.59 = (bf16[768,256]{1,0:T(8,128)(2,1)S(1)}, bf16[768,256]{1,0:T(8,128)(2,1)}, u32[]{:S(2)}, u32[]{:S(2)}) collective-permute-start(bf16[768,256]{1,0:T(8,128)(2,1)S(1)} %copy-done.39), channel_id=1, source_target_pairs={{8,0},{16,8},{24,16},{28,24},{20,28},{12,20},{4,12},{0,4},{9,1},{1... | collective-permute-start | bytes 1179656 | tf_op jit(solution)/shard_map/ppermute | solution.py:572
  264.0 39.3 %collective-permute-start.47 = (bf16[256,1408]{1,0:T(8,128)(2,1)S(1)}, bf16[256,1408]{1,0:T(8,128)(2,1)S(1)}, u32[]{:S(2)}, u32[]{:S(2)}) collective-permute-start(bf16[256,1408]{1,0:T(8,128)(2,1)S(1)} %collective-permute-done.45), channel_id=1, source_target_pairs={{0,8},{8,16},{16,24},{24,28},{28,20},{20,12},{12,4},{4,0},{1,9},{9... | collective-permute-start | bytes 2162696 | tf_op jit(solution)/shard_map/ppermute | solution.py:568
  268.2 36.5 %collective-permute-start.55 = (bf16[256,1408]{1,0:T(8,128)(2,1)S(1)}, bf16[256,1408]{1,0:T(8,128)(2,1)S(1)}, u32[]{:S(2)}, u32[]{:S(2)}) collective-permute-start(bf16[256,1408]{1,0:T(8,128)(2,1)S(1)} %collective-permute-done.53), channel_id=1, source_target_pairs={{8,0},{16,8},{24,16},{28,24},{20,28},{12,20},{4,12},{0,4},{9,1},{1... | collective-permute-start | bytes 2162696 | tf_op jit(solution)/shard_map/ppermute | solution.py:572
  287.8 47.8 %collective-permute-start.38 = (bf16[256,2048]{0,1:T(8,128)(2,1)S(1)}, bf16[256,2048]{0,1:T(8,128)(2,1)S(1)}, u32[]{:S(2)}, u32[]{:S(2)}) collective-permute-start(bf16[256,2048]{0,1:T(8,128)(2,1)S(1)} %multiply_convert_fusion.4), channel_id=1, source_target_pairs={{0,1},{1,0},{2,3},{3,2},{4,5},{5,4},{6,7},{7,6},{8,9},{9,8},{10,11... | collective-permute-start | bytes 3145736 | tf_op jit(solution)/shard_map/ppermute | solution.py:640
  385.0 101.0 %collective-permute-start.67 = (bf16[256,2048]{0,1:T(8,128)(2,1)S(1)}, bf16[256,2048]{0,1:T(8,128)(2,1)S(1)}, u32[]{:S(2)}, u32[]{:S(2)}) collective-permute-start(bf16[256,2048]{0,1:T(8,128)(2,1)S(1)} %dynamic-slice_convert_fusion.2), channel_id=1, source_target_pairs={{0,1},{1,0},{2,3},{3,2},{4,5},{5,4},{6,7},{7,6},{8,9},{9,8},{10,11... | collective-permute-start | bytes 3145736 | tf_op jit(solution)/shard_map/ppermute | solution.py:640
  401.3 86.3 %collective-permute-start.70 = (bf16[256,2048]{0,1:T(8,128)(2,1)S(1)}, bf16[256,2048]{0,1:T(8,128)(2,1)S(1)}, u32[]{:S(2)}, u32[]{:S(2)}) collective-permute-start(bf16[256,2048]{0,1:T(8,128)(2,1)S(1)} %dynamic-slice_convert_fusion.1), channel_id=1, source_target_pairs={{0,1},{1,0},{2,3},{3,2},{4,5},{5,4},{6,7},{7,6},{8,9},{9,8},{10,11... | collective-permute-start | bytes 3145736 | tf_op jit(solution)/shard_map/ppermute | solution.py:640
  403.9 33.8 %collective-permute-start.112 = (bf16[256,1408]{1,0:T(8,128)(2,1)S(1)}, bf16[256,1408]{1,0:T(8,128)(2,1)S(1)}, u32[]{:S(2)}, u32[]{:S(2)}) collective-permute-start(bf16[256,1408]{1,0:T(8,128)(2,1)S(1)} %convolution_convert_fusion.3), channel_id=1, source_target_pairs={{0,8},{8,16},{16,24},{24,28},{28,20},{20,12},{12,4},{4,0},{1,9},{9... | collective-permute-start | bytes 2162696 | tf_op jit(solution)/shard_map/ppermute | solution.py:568
  469.9 35.1 %collective-permute-start.135 = (bf16[640,256]{1,0:T(8,128)(2,1)S(1)}, bf16[640,256]{1,0:T(8,128)(2,1)S(1)}, u32[]{:S(2)}, u32[]{:S(2)}) collective-permute-start(bf16[640,256]{1,0:T(8,128)(2,1)S(1)} %add_convert_fusion.20), channel_id=1, source_target_pairs={{0,8},{8,16},{16,24},{24,28},{28,20},{20,12},{12,4},{4,0},{1,9},{9... | collective-permute-start | bytes 983048 | tf_op jit(solution)/shard_map/ppermute | solution.py:568
  478.3 34.7 %collective-permute-start.113 = (bf16[256,1408]{1,0:T(8,128)(2,1)S(1)}, bf16[256,1408]{1,0:T(8,128)(2,1)S(1)}, u32[]{:S(2)}, u32[]{:S(2)}) collective-permute-start(bf16[256,1408]{1,0:T(8,128)(2,1)S(1)} %fusion.16), channel_id=1, source_target_pairs={{0,8},{8,16},{16,24},{24,28},{28,20},{20,12},{12,4},{4,0},{1,9},{9... | collective-permute-start | bytes 2162696 | tf_op jit(solution)/shard_map/ppermute | solution.py:568
  513.0 61.4 %collective-permute-start.68 = (bf16[256,2048]{0,1:T(8,128)(2,1)}, bf16[256,2048]{0,1:T(8,128)(2,1)}, u32[]{:S(2)}, u32[]{:S(2)}) collective-permute-start(bf16[256,2048]{0,1:T(8,128)(2,1)} %fusion.36), channel_id=1, source_target_pairs={{0,2},{1,3},{2,0},{3,1},{4,6},{5,7},{6,4},{7,5},{8,10},{9,11},{10,... | collective-permute-start | bytes 3145736 | tf_op jit(solution)/shard_map/ppermute | solution.py:640
  515.9 40.5 %collective-permute-start.71 = (bf16[256,2048]{0,1:T(8,128)(2,1)}, bf16[256,2048]{0,1:T(8,128)(2,1)}, u32[]{:S(2)}, u32[]{:S(2)}) collective-permute-start(bf16[256,2048]{0,1:T(8,128)(2,1)} %fusion.37), channel_id=1, source_target_pairs={{0,2},{1,3},{2,0},{3,1},{4,6},{5,7},{6,4},{7,5},{8,10},{9,11},{10,... | collective-permute-start | bytes 3145736 | tf_op jit(solution)/shard_map/ppermute | solution.py:640
  525.6 34.8 %collective-permute-start.114 = (bf16[256,1408]{1,0:T(8,128)(2,1)}, bf16[256,1408]{1,0:T(8,128)(2,1)}, u32[]{:S(2)}, u32[]{:S(2)}) collective-permute-start(bf16[256,1408]{1,0:T(8,128)(2,1)} %fusion.15), channel_id=1, source_target_pairs={{0,8},{8,16},{16,24},{24,28},{28,20},{20,12},{12,4},{4,0},{1,9},{9... | collective-permute-start | bytes 2162696 | tf_op jit(solution)/shard_map/ppermute | solution.py:568
  532.3 46.2 %collective-permute-start.118 = (bf16[256,1408]{1,0:T(8,128)(2,1)}, bf16[256,1408]{1,0:T(8,128)(2,1)}, u32[]{:S(2)}, u32[]{:S(2)}) collective-permute-start(bf16[256,1408]{1,0:T(8,128)(2,1)} %fusion.17), channel_id=1, source_target_pairs={{8,0},{16,8},{24,16},{28,24},{20,28},{12,20},{4,12},{0,4},{9,1},{1... | collective-permute-start | bytes 2162696 | tf_op jit(solution)/shard_map/ppermute | solution.py:572
  533.8 47.1 %collective-permute-start.121 = (bf16[256,1408]{1,0:T(8,128)(2,1)}, bf16[256,1408]{1,0:T(8,128)(2,1)}, u32[]{:S(2)}, u32[]{:S(2)}) collective-permute-start(bf16[256,1408]{1,0:T(8,128)(2,1)} %fusion.19), channel_id=1, source_target_pairs={{0,8},{8,16},{16,24},{24,28},{28,20},{20,12},{12,4},{4,0},{1,9},{9... | collective-permute-start | bytes 2162696 | tf_op jit(solution)/shard_map/ppermute | solution.py:568
  578.5 185.3 %collective-permute-start.69 = (f32[256,2048]{0,1:T(8,128)}, f32[256,2048]{0,1:T(8,128)}, u32[]{:S(2)}, u32[]{:S(2)}) collective-permute-start(f32[256,2048]{0,1:T(8,128)} %get-tuple-element.241), channel_id=1, source_target_pairs={{0,1},{1,0},{2,3},{3,2},{4,5},{5,4},{6,7},{7,6},{8,9},{9,8},{10,11... | collective-permute-start | bytes 6291464 | tf_op jit(solution)/shard_map/ppermute | solution.py:640
  638.7 34.0 %collective-permute-start.106 = (bf16[512,256]{1,0:T(8,128)(2,1)S(1)}, bf16[512,256]{1,0:T(8,128)(2,1)S(1)}, u32[]{:S(2)}, u32[]{:S(2)}) collective-permute-start(bf16[512,256]{1,0:T(8,128)(2,1)S(1)} %fusion.78), channel_id=1, source_target_pairs={{0,8},{8,16},{16,24},{24,28},{28,20},{20,12},{12,4},{4,0},{1,9},{9... | collective-permute-start | bytes 786440 | tf_op jit(solution)/shard_map/ppermute | solution.py:568
  642.8 33.1 %collective-permute-start.109 = (bf16[512,256]{1,0:T(8,128)(2,1)S(1)}, bf16[512,256]{1,0:T(8,128)(2,1)S(1)}, u32[]{:S(2)}, u32[]{:S(2)}) collective-permute-start(bf16[512,256]{1,0:T(8,128)(2,1)S(1)} %fusion.81), channel_id=1, source_target_pairs={{8,0},{16,8},{24,16},{28,24},{20,28},{12,20},{4,12},{0,4},{9,1},{1... | collective-permute-start | bytes 786440 | tf_op jit(solution)/shard_map/ppermute | solution.py:572
  645.0 39.1 %collective-permute-start.96 = (bf16[256,512]{1,0:T(8,128)(2,1)S(1)}, bf16[256,512]{1,0:T(8,128)(2,1)S(1)}, u32[]{:S(2)}, u32[]{:S(2)}) collective-permute-start(bf16[256,512]{1,0:T(8,128)(2,1)S(1)} %fusion.74), channel_id=1, source_target_pairs={{0,8},{8,16},{16,24},{24,28},{28,20},{20,12},{12,4},{4,0},{1,9},{9... | collective-permute-start | bytes 786440 | tf_op jit(solution)/shard_map/ppermute | solution.py:568
  677.9 93.3 %collective-permute-start.107 = (bf16[512,256]{1,0:T(8,128)(2,1)}, bf16[512,256]{1,0:T(8,128)(2,1)}, u32[]{:S(2)}, u32[]{:S(2)}) collective-permute-start(bf16[512,256]{1,0:T(8,128)(2,1)} %fusion.77), channel_id=1, source_target_pairs={{0,8},{8,16},{16,24},{24,28},{28,20},{20,12},{12,4},{4,0},{1,9},{9... | collective-permute-start | bytes 786440 | tf_op jit(solution)/shard_map/ppermute | solution.py:568
  682.0 56.2 %collective-permute-start.110 = (bf16[512,256]{1,0:T(8,128)(2,1)}, bf16[512,256]{1,0:T(8,128)(2,1)}, u32[]{:S(2)}, u32[]{:S(2)}) collective-permute-start(bf16[512,256]{1,0:T(8,128)(2,1)} %fusion.80), channel_id=1, source_target_pairs={{8,0},{16,8},{24,16},{28,24},{20,28},{12,20},{4,12},{0,4},{9,1},{1... | collective-permute-start | bytes 786440 | tf_op jit(solution)/shard_map/ppermute | solution.py:572
  686.0 54.6 %collective-permute-start.97 = (bf16[256,512]{1,0:T(8,128)(2,1)}, bf16[256,512]{1,0:T(8,128)(2,1)}, u32[]{:S(2)}, u32[]{:S(2)}) collective-permute-start(bf16[256,512]{1,0:T(8,128)(2,1)} %fusion.73), channel_id=1, source_target_pairs={{0,8},{8,16},{16,24},{24,28},{28,20},{20,12},{12,4},{4,0},{1,9},{9... | collective-permute-start | bytes 786440 | tf_op jit(solution)/shard_map/ppermute | solution.py:568
  736.6 75.3 %collective-permute-start.101 = (bf16[256,512]{1,0:T(8,128)(2,1)}, bf16[256,512]{1,0:T(8,128)(2,1)S(1)}, u32[]{:S(2)}, u32[]{:S(2)}) collective-permute-start(bf16[256,512]{1,0:T(8,128)(2,1)} %fusion.75), channel_id=1, source_target_pairs={{8,0},{16,8},{24,16},{28,24},{20,28},{12,20},{4,12},{0,4},{9,1},{1... | collective-permute-start | bytes 786440 | tf_op jit(solution)/shard_map/ppermute | solution.py:572
  763.8 48.6 %collective-permute-start.98 = (bf16[256,512]{1,0:T(8,128)(2,1)S(1)}, bf16[256,512]{1,0:T(8,128)(2,1)S(1)}, u32[]{:S(2)}, u32[]{:S(2)}) collective-permute-start(bf16[256,512]{1,0:T(8,128)(2,1)S(1)} %fusion.72), channel_id=1, source_target_pairs={{0,8},{8,16},{16,24},{24,28},{28,20},{20,12},{12,4},{4,0},{1,9},{9... | collective-permute-start | bytes 786440 | tf_op jit(solution)/shard_map/ppermute | solution.py:568
  805.9 44.1 %collective-permute-start.80 = (f32[256,2048]{0,1:T(8,128)}, f32[256,2048]{0,1:T(8,128)}, u32[]{:S(2)}, u32[]{:S(2)}) collective-permute-start(f32[256,2048]{0,1:T(8,128)} %subtract_add_fusion), channel_id=1, source_target_pairs={{0,1},{1,0},{2,3},{3,2},{4,5},{5,4},{6,7},{7,6},{8,9},{9,8},{10,11... | collective-permute-start | bytes 6291464 | tf_op jit(solution)/shard_map/ppermute | solution.py:640
  (284 other events, 3565.6 us)

commit v2 on v1

--- a/solution.py
+++ b/solution.py
@@ -103,10 +103,11 @@
 
 
 def _local_kernel(
-    heads, scal_ref, pre_ref, halo_ref, taps_ref, logit_ref, q_ref, k_ref, w_ref, uv_ref, t_ref,
-    bt_ref, pt_ref, ext_ref,
+    heads, scal_ref, pre_q, pre_k, pre_v, halo_q, halo_k, halo_v, taps_ref, logit_ref, q_ref, k_ref,
+    w_ref, uv_ref, t_ref, bt_ref, pt_ref, ext_ref,
 ):
-    rows = pre_ref.shape[1]
+    pre_refs, halo_refs = (pre_q, pre_k, pre_v), (halo_q, halo_k, halo_v)
+    rows = pre_q.shape[0]
     pairs = rows // SPANROWS
     masks = _tap_masks(scal_ref, rows)
     row, col, same = _pair_masks()
@@ -127,7 +128,7 @@
         acts = []
         for part in range(3):
             mixed = _convolved(
-                ext_ref.at[head * 3 + part], pre_ref[part, :, lanes], halo_ref[part, :, lanes],
+                ext_ref.at[head * 3 + part], pre_refs[part][:, lanes], halo_refs[part][:, lanes],
                 taps_ref[part, :, lanes], masks,
             )
             acts.append(mixed * jax.nn.sigmoid(mixed))
@@ -286,10 +287,11 @@
 
 
 def _back_kernel(
-    heads, scal_ref, pre_ref, halo_ref, taps_ref, logit_ref, q_ref, k_ref, w_ref, t_ref, u_ref,
-    s_ref, do_ref, p_ref, above_ref, dpre_ref, tail_ref, dhalo_ref, dtaps_ref, dlogit_ref,
-    ext_ref, pad_ref,
+    heads, scal_ref, pre_q, pre_k, pre_v, halo_q, halo_k, halo_v, taps_ref, logit_ref, q_ref, k_ref,
+    w_ref, t_ref, u_ref, s_ref, do_ref, p_ref, above_ref, dpre_ref, tail_ref, dhalo_ref, dtaps_ref,
+    dlogit_ref, ext_ref, pad_ref,
 ):
+    pre_refs, halo_refs = (pre_q, pre_k, pre_v), (halo_q, halo_k, halo_v)
     rows = q_ref.shape[0]
     pairs = rows // SPANROWS
     masks = _tap_masks(scal_ref, rows)
@@ -330,7 +332,7 @@
         acts, slopes = [], []
         for which in range(3):
             mixed = _convolved(
-                ext_ref.at[head * 3 + which], pre_ref[which, :, lanes], halo_ref[which, :, lanes],
+                ext_ref.at[head * 3 + which], pre_refs[which][:, lanes], halo_refs[which][:, lanes],
                 taps[which], masks,
             )
             sig = jax.nn.sigmoid(mixed)
@@ -431,7 +433,6 @@
         scal=pl.BlockSpec(memory_space=pltpu.SMEM),
         flat=pl.BlockSpec((rows, wide), lambda h: (0, h)),
         three=pl.BlockSpec((3, rows, wide), lambda h: (0, 0, h)),
-        halo=pl.BlockSpec((3, 16, wide), lambda h: (0, 0, h)),
         edge=pl.BlockSpec((3, 8, wide), lambda h: (0, 0, h)),
         taps=pl.BlockSpec((3, CONV, wide), lambda h: (0, 0, h)),
         square=pl.BlockSpec((heads, DK, DK), lambda h: (h, 0, 0)),
@@ -441,6 +442,21 @@
     )
 
 
+def _three_specs(heads, rows, total):
+    def one(tall, part):
+        return pl.BlockSpec((tall, heads * DK), lambda h: (0, part * (total // heads) + h))
+
+    return [one(rows, 0)] * 3 + [one(16, part) for part in range(3)]
+
+
+def _cost(microseconds):
+    return pl.CostEstimate(
+        flops=microseconds * 11 * 10**8,
+        bytes_accessed=microseconds * 36 * 10**5,
+        transcendentals=0,
+    )
+
+
 def _params():
     return pltpu.CompilerParams(
         dimension_semantics=("arbitrary",), vmem_limit_bytes=48 * 1024 * 1024
@@ -448,7 +464,7 @@
 
 
 def delta_local(scal, pre, halo, taps, logits):
-    _, rows, width = pre.shape
+    rows, width = pre[0].shape
     total = width // DK
     heads = min(HEADS_AT_ONCE, total)
     sp = _specs(heads, rows)
@@ -457,7 +473,7 @@
     return pl.pallas_call(
         partial(_local_kernel, heads),
         grid=(total // heads,),
-        in_specs=[sp["scal"], sp["three"], sp["halo"], sp["taps"], table],
+        in_specs=[sp["scal"]] + _three_specs(heads, rows, total) + [sp["taps"], table],
         out_specs=[sp["flat"]] * 5 + [sp["square"]] * 2,
         out_shape=[
             low,
@@ -470,9 +486,9 @@
         ],
         scratch_shapes=[pltpu.VMEM((3 * heads, rows + 8, DK), jnp.float32)],
         compiler_params=_params(),
-        cost_estimate=pl.CostEstimate(flops=2 * 10**9, bytes_accessed=8 * 10**6, transcendentals=0),
+        cost_estimate=_cost(11),
         name="delta_local",
-    )(scal, pre, halo, taps, logits)
+    )(scal, *pre, halo, halo, halo, taps, logits)
 
 
 def delta_apply(scal, q, k, w, uv, state_in, gate, gain):
@@ -493,7 +509,7 @@
             jax.ShapeDtypeStruct((total, rows // SPAN, DK, DK), jnp.bfloat16),
         ],
         compiler_params=_params(),
-        cost_estimate=pl.CostEstimate(flops=2 * 10**9, bytes_accessed=8 * 10**6, transcendentals=0),
+        cost_estimate=_cost(7),
         name="delta_apply",
     )(scal, q, k, w, uv, state_in, gate, gain)
 
@@ -517,13 +533,13 @@
             jax.ShapeDtypeStruct((total, DK, DK), jnp.float32),
         ],
         compiler_params=_params(),
-        cost_estimate=pl.CostEstimate(flops=2 * 10**9, bytes_accessed=8 * 10**6, transcendentals=0),
+        cost_estimate=_cost(9),
         name="delta_back_local",
     )(scal, dn, gate, gain, o, q, k, w)
 
 
 def delta_back(scal, pre, halo, taps, logits, q, k, w, t, u, s, do, p, above):
-    _, rows, width = pre.shape
+    rows, width = pre[0].shape
     total = width // DK
     heads = min(HEADS_AT_ONCE, total)
     sp = _specs(heads, rows)
@@ -532,7 +548,9 @@
     return pl.pallas_call(
         partial(_back_kernel, heads),
         grid=(total // heads,),
-        in_specs=[sp["scal"], sp["three"], sp["halo"], sp["taps"], table]
+        in_specs=[sp["scal"]]
+        + _three_specs(heads, rows, total)
+        + [sp["taps"], table]
         + [sp["flat"]] * 5
         + [sp["spans"], sp["flat"], sp["flat"], sp["square"]],
         out_specs=[sp["three"], sp["edge"], sp["edge"], sp["taps"], table],
@@ -548,11 +566,11 @@
             pltpu.VMEM((3 * heads, rows + 16, DK), jnp.float32),
         ],
         compiler_params=_params(),
-        cost_estimate=pl.CostEstimate(
-            flops=4 * 10**9, bytes_accessed=12 * 10**6, transcendentals=0
-        ),
+        cost_estimate=_cost(17),
         name="delta_back",
-    )(scal, pre, halo, taps, logits, q, k, w, t, u, s, do, p, above)
+    )(
+        scal, *pre, halo, halo, halo, taps, logits, q, k, w, t, u, s, do, p, above
+    )
 
 
 def ring_order(count):
@@ -578,61 +596,316 @@
     return jnp.where(index % 2 == 0, index // 2, count - (index + 1) // 2)
 
 
-def to_ring(value):
+def ring_sources():
     count = lax.axis_size("seq")
-    piece = value.shape[-1] // count
-    parts = [value[..., one * piece : (one + 1) * piece] for one in ring_order(count)]
-    doubled = jnp.concatenate(parts + parts[:-1], axis=-1)
-    return lax.dynamic_slice_in_dim(doubled, ring_place() * piece, count * piece, value.ndim - 1)
-
-
-def from_ring(value):
+    order = jnp.asarray(ring_order(count), jnp.int32)
+    return jnp.take(order, (ring_place() + jnp.arange(count, dtype=jnp.int32)) % count)
+
+
+def ring_targets():
     count = lax.axis_size("seq")
-    piece = value.shape[-1] // count
-    doubled = jnp.concatenate([value, value[..., : (count - 1) * piece]], axis=-1)
-    start = lax.rem(count - ring_place(), count) * piece
-    placed = lax.dynamic_slice_in_dim(doubled, start, count * piece, value.ndim - 1)
     order = ring_order(count)
-    parts = []
-    for one in range(count):
-        place = order.index(one)
-        parts.append(placed[..., place * piece : (place + 1) * piece])
-    return jnp.concatenate(parts, axis=-1)
-
-
-def ring_gather(first, second):
+    places = jnp.asarray([order.index(one) for one in range(count)], jnp.int32)
+    return (places + count - ring_place()) % count
+
+
+def _pick_kernel(pieces, index_ref, value_ref, out_ref):
+    piece = out_ref.shape[1] // pieces
+    for one in range(pieces):
+        start = pl.multiple_of(index_ref[one] * piece, DK)
+        out_ref[:, one * piece : (one + 1) * piece] = value_ref[:, pl.ds(start, piece)]
+
+
+def _join_kernel(pieces, index_ref, own_ref, other_ref, out_ref):
+    piece = out_ref.shape[1] // pieces
+    own = (pl.program_id(0) >= pl.num_programs(0) // 2) == (index_ref[pieces] == 1)
+    for one in range(pieces):
+        start = pl.multiple_of(index_ref[one] * piece, DK)
+        out_ref[:, one * piece : (one + 1) * piece] = jnp.where(
+            own, own_ref[:, pl.ds(start, piece)], other_ref[:, pl.ds(start, piece)]
+        )
+
+
+def pick_columns(value, index):
+    count = index.shape[0]
+    rows, wide = value.shape
+    piece = wide // count
+    if piece % DK:
+        return jnp.take(value.reshape(rows, count, piece), index, axis=1).reshape(rows, wide)
+    tall = rows // 4
+    return pl.pallas_call(
+        partial(_pick_kernel, count),
+        grid=(4,),
+        in_specs=[
+            pl.BlockSpec(memory_space=pltpu.SMEM),
+            pl.BlockSpec((tall, wide), lambda i: (i, 0)),
+        ],
+        out_specs=pl.BlockSpec((tall, wide), lambda i: (i, 0)),
+        out_shape=jax.ShapeDtypeStruct(value.shape, value.dtype),
+        compiler_params=_params(),
+        cost_estimate=_cost(3),
+        name="pick_columns",
+    )(index, value)
+
+
+def join_columns(own, index):
+    other = swap(own, "head", 1)
+    bit = lax.axis_index("head") & 1
+    count = index.shape[0]
+    rows, wide = own.shape
+    if (wide // count) % DK:
+        both = jnp.where(
+            bit == 0,
+            jnp.concatenate([own, other], axis=0),
+            jnp.concatenate([other, own], axis=0),
+        )
+        return pick_columns(both, index)
+    tall = rows // 2
+    half = pl.BlockSpec((tall, wide), lambda i: (i % 2, 0))
+    return pl.pallas_call(
+        partial(_join_kernel, count),
+        grid=(4,),
+        in_specs=[pl.BlockSpec(memory_space=pltpu.SMEM), half, half],
+        out_specs=pl.BlockSpec((tall, wide), lambda i: (i, 0)),
+        out_shape=jax.ShapeDtypeStruct((2 * rows, wide), own.dtype),
+        compiler_params=_params(),
+        cost_estimate=_cost(4),
+        name="join_columns",
+    )(jnp.concatenate([index, bit[None].astype(jnp.int32)]), own, other)
+
+
+def low(value):
+    return value.astype(jnp.bfloat16)
+
+
+class Gather:
+    def __init__(self, first, second):
+        self.count = lax.axis_size("seq")
+        self.half = self.count // 2
+        self.held = ({0: first}, {0: second})
+
+    def fresh(self, slot):
+        return [self.held[slot]] if slot < 2 else []
+
+    def send(self, slot):
+        step, second = slot // 2 + 1, slot % 2
+        held = self.held[second]
+        back, forth = (self.count - step) % self.count, step
+        keys = []
+        if step < self.half or not second:
+            held[back] = send_up(held[(back + 1) % self.count])
+            keys.append((held, back))
+        if step < self.half or second:
+            held[forth] = send_down(held[forth - 1])
+            keys.append((held, forth))
+        return keys
+
+
+class Scatter:
+    def __init__(self, first, second):
+        self.count = lax.axis_size("seq")
+        self.half = self.count // 2
+        self.terms = (first, second)
+        self.got = ({}, {})
+
+    def places(self, slot):
+        step, second = slot // 2, slot % 2
+        up = self.half - step - (1 if second else 0)
+        down = self.half + step + (0 if second else 1)
+        return up, down
+
+    def fresh(self, slot):
+        if slot > 1:
+            return []
+        self.first = {0: dict(zip(("up", "down"), map(self.terms[slot], self.places(slot))))}
+        return [self.first]
+
+    def send(self, slot):
+        got = self.got[slot % 2]
+        keys = []
+        for way, send, place in zip(("up", "down"), (send_up, send_down), self.places(slot)):
+            if 0 < place < self.count:
+                if way in got:
+                    term = self.terms[slot % 2](place)
+                    term = low(term.astype(jnp.float32) + got[way].astype(jnp.float32))
+                else:
+                    term = self.first[0][way]
+                got[way] = send(term)
+                keys.append((got, way))
+        return keys
+
+    def sums(self):
+        return [
+            terms(0).astype(jnp.float32) + got["up"].astype(jnp.float32) + got["down"].astype(jnp.float32)
+            for terms, got in zip(self.terms, self.got)
+        ]
+
+
+class Flow:
+    def __init__(self):
+        self.flying = []
+
+    def step(self, ring, stage, values=()):
+        each = lax.axis_size("seq") // 8
+        for slot in range(stage * each, (stage + 1) * each):
+            keys = self.flying.pop(0) if len(self.flying) > 1 else []
+            arrived = [held[key] for held, key in keys]
+            fresh = ring.fresh(slot)
+            arrived, first, values = lax.optimization_barrier(
+                (arrived, [held[0] for held in fresh], values)
+            )
+            for held, value in zip(fresh, first):
+                held[0] = value
+            for (held, key), value in zip(keys, arrived):
+                held[key] = value
+            self.flying.append(ring.send(slot))
+        return values
+
+
+def _rows_dot_kernel(count, operands, outs, *refs):
+    size = len(operands)
+    value_ref = refs[0]
+    weights = [refs[1 + one * count : 1 + (one + 1) * count] for one in range(size)]
+    out_refs = refs[1 + size * count : -1 - size]
+    held = refs[-1 - size : -1]
+    sems = refs[-1]
+
+    def copy(one, place):
+        first, columns = operands[one]
+        piece = weights[one][place].shape[0]
+        return pltpu.make_async_copy(
+            weights[one][place].at[:, pl.ds(first, columns)],
+            held[one].at[pl.ds(place * piece, piece)],
+            sems.at[one, place],
+        )
+
+    for one in range(size):
+        for place in range(count):
+            copy(one, place).start()
+    for one in range(size):
+        for place in range(count):
+            copy(one, place).wait()
+        for source, start, columns, out, at in outs:
+            if source == one:
+                out_refs[out][:, at : at + columns] = jnp.dot(
+                    value_ref[...],
+                    held[one][:, start : start + columns],
+                    preferred_element_type=jnp.float32,
+                ).astype(out_refs[out].dtype)
+
+
+def rows_dot(value, operands, outs, shapes):
+    count = len(operands[0][0])
+    vmem = pl.BlockSpec(memory_space=pltpu.VMEM)
+    ranges = [(first, columns) for _, first, columns in operands]
+    whole = [
+        jax.ShapeDtypeStruct((value.shape[1], columns), jnp.bfloat16) for _, columns in ranges
+    ]
+    results = pl.pallas_call(
+        partial(_rows_dot_kernel, count, ranges, outs),
+        in_specs=[vmem] + [pl.BlockSpec(memory_space=pl.ANY)] * (len(operands) * count),
+        out_specs=[vmem] * (len(shapes) + len(whole)),
+        out_shape=list(shapes) + whole,
+        scratch_shapes=[pltpu.SemaphoreType.DMA((len(operands), count))],
+        compiler_params=pltpu.CompilerParams(vmem_limit_bytes=48 * 1024 * 1024),
+        cost_estimate=_cost(12),
+        name="rows_dot",
+    )(value, *[pieces[place] for pieces, _, _ in operands for place in range(count)])
+    return results[: len(shapes)], results[len(shapes) :]
+
+
+def _glu_early_kernel(count, *refs):
+    half = count // 2
+    late = (half - 1, half, half + 1)
+    value_ref = refs[0]
+    weights = (refs[1 : 1 + count], refs[1 + count : 1 + 2 * count])
+    outs = refs[1 + 2 * count : 3 + 2 * count]
+    held = refs[3 + 2 * count : 5 + 2 * count]
+    sems = refs[-1]
+    piece = weights[0][0].shape[0]
+    places = [place for place in range(count) if place not in late]
+
+    def copy(one, place):
+        return pltpu.make_async_copy(
+            weights[one][place], held[one].at[pl.ds(place * piece, piece)], sems.at[one, place]
+        )
+
+    for one in range(2):
+        for place in places:
+            copy(one, place).start()
+    stop, again = (half - 1) * piece, (half + 2) * piece
+    for one in range(2):
+        held[one][stop:again] = jnp.zeros((3 * piece, held[one].shape[1]), jnp.bfloat16)
+    for one in range(2):
+        for place in places:
+            copy(one, place).wait()
+        outs[one][...] = jnp.dot(
+            value_ref[:, :stop], held[one][:stop], preferred_element_type=jnp.float32
+        ) + jnp.dot(value_ref[:, again:], held[one][again:], preferred_element_type=jnp.float32)
+
+
+def glu_early(value, gates, ups):
     count = lax.axis_size("seq")
-    half = count // 2
-    one = {0: first}
-    two = {0: second}
-    for step in range(1, half + 1):
-        one[count - step] = send_up(one[(count - step + 1) % count])
-        two[step] = send_down(two[step - 1])
-        if step < half:
-            one[step] = send_down(one[step - 1])
-            two[count - step] = send_up(two[(count - step + 1) % count])
-    late = (one[count - half + 1], two[half - 1])
-    return [one[key] for key in range(count)], [two[key] for key in range(count)], late
-
-
-def ring_scatter(first, second):
-    count = lax.axis_size("seq")
-    half = count // 2
-
-    def low(value):
-        return value.astype(jnp.bfloat16)
-
-    one_up, one_down = low(first(half)), low(first(half + 1))
-    two_up, two_down = low(second(half - 1)), low(second(half))
-    for step in range(1, half):
-        one_up = low(first(half - step) + send_up(one_up).astype(jnp.float32))
-        two_down = low(second(half + step) + send_down(two_down).astype(jnp.float32))
-        if step < half - 1:
-            one_down = low(first(half + 1 + step) + send_down(one_down).astype(jnp.float32))
-            two_up = low(second(half - 1 - step) + send_up(two_up).astype(jnp.float32))
-    one = first(0) + send_up(one_up).astype(jnp.float32) + send_down(one_down).astype(jnp.float32)
-    two = second(0) + send_up(two_up).astype(jnp.float32) + send_down(two_down).astype(jnp.float32)
-    return one, two
+    vmem = pl.BlockSpec(memory_space=pltpu.VMEM)
+    columns = gates[0].shape[1]
+    return pl.pallas_call(
+        partial(_glu_early_kernel, count),
+        in_specs=[vmem] + [pl.BlockSpec(memory_space=pl.ANY)] * (2 * count),
+        out_specs=[vmem] * 4,
+        out_shape=[jax.ShapeDtypeStruct((value.shape[0], columns), jnp.float32)] * 2
+        + [jax.ShapeDtypeStruct((value.shape[1], columns), jnp.bfloat16)] * 2,
+        scratch_shapes=[pltpu.SemaphoreType.DMA((2, count))],
+        compiler_params=pltpu.CompilerParams(vmem_limit_bytes=52 * 1024 * 1024),
+        cost_estimate=_cost(14),
+        name="glu_early",
+    )(
+        value,
+        *[gates.get(place, gates[0]) for place in range(count)],
+        *[ups.get(place, ups[0]) for place in range(count)],
+    )
+
+
+def _glu_late_kernel(value_ref, *refs):
+    gates_refs, ups_refs = refs[:3], refs[3:6]
+    gate_ref, up_ref, grad_ref, act_ref, dgate_ref, dup_ref = refs[6:]
+    columns = grad_ref.shape[1]
+    piece = gates_refs[0].shape[0]
+    wide = 256
+    for start in range(0, columns, wide):
+        part = slice(start, min(start + wide, columns))
+        gate, up = gate_ref[:, part], up_ref[:, part]
+        for one in range(3):
+            value = value_ref[:, one * piece : (one + 1) * piece]
+            gate = gate + jnp.dot(
+                value, gates_refs[one][:, part], preferred_element_type=jnp.float32
+            )
+            up = up + jnp.dot(value, ups_refs[one][:, part], preferred_element_type=jnp.float32)
+        grad = grad_ref[:, part]
+        sig = jax.nn.sigmoid(gate)
+        act = gate * sig
+        act_ref[:, part] = low(act * up)
+        dgate_ref[:, part] = low(grad * up * (sig * (1.0 + gate * (1.0 - sig))))
+        dup_ref[:, part] = low(grad * act)
+
+
+def glu_late(value, gates, ups, sums, grad):
+    rows, columns = grad.shape
+    tall = rows // 4
+
+    def by_rows(wide):
+        return pl.BlockSpec((tall, wide), lambda i: (i, 0))
+
+    whole = pl.BlockSpec(gates[0].shape, lambda i: (0, 0))
+    return pl.pallas_call(
+        _glu_late_kernel,
+        grid=(4,),
+        in_specs=[by_rows(value.shape[1])] + [whole] * 6 + [by_rows(columns)] * 3,
+        out_specs=[by_rows(columns)] * 3,
+        out_shape=[jax.ShapeDtypeStruct(grad.shape, jnp.bfloat16)] * 3,
+        compiler_params=_params(),
+        cost_estimate=_cost(8),
+        name="glu_late",
+    )(value, *gates, *ups, *sums, grad)
 
 
 def swap(value, axis, bit):
@@ -640,33 +913,24 @@
     return lax.ppermute(value, axis, [(one, one ^ bit) for one in range(count)])
 
 
-def gather_small(value):
-    index = lax.axis_index("seq")
-    held = value[None]
-    bit = 1
-    while bit < lax.axis_size("seq"):
-        other = swap(held, "seq", bit)
-        mine_first = (index & bit) == 0
-        held = jnp.where(
-            mine_first,
-            jnp.concatenate([held, other], axis=0),
-            jnp.concatenate([other, held], axis=0),
-        )
-        bit *= 2
-    return held
-
-
-def scatter_small(value):
-    index = lax.axis_index("seq")
-    held = value
-    bit = lax.axis_size("seq") // 2
-    while bit >= 1:
-        low, high = held[: held.shape[0] // 2], held[held.shape[0] // 2 :]
-        upper = (index & bit) != 0
-        got = swap(jnp.where(upper, low, high), "seq", bit)
-        held = jnp.where(upper, high, low) + got
-        bit //= 2
-    return held[0]
+def gather_round(held, bit):
+    other = swap(held, "seq", bit)
+    return jnp.where(
+        (lax.axis_index("seq") & bit) == 0,
+        jnp.concatenate([held, other], axis=0),
+        jnp.concatenate([other, held], axis=0),
+    )
+
+
+def scatter_round(held, bit):
+    low_rows, high_rows = held[: held.shape[0] // 2], held[held.shape[0] // 2 :]
+    upper = (lax.axis_index("seq") & bit) != 0
+    got = swap(jnp.where(upper, low_rows, high_rows), "seq", bit)
+    return jnp.where(upper, high_rows, low_rows) + got
+
+
+def bits_of(axis):
+    return [1 << bit for bit in range(lax.axis_size(axis).bit_length() - 1)]
 
 
 def own_half(value):
@@ -688,15 +952,22 @@
     )
 
 
-def summed_half(partial_rows):
-    low = partial_rows.astype(jnp.bfloat16)
-    pair = own_half(partial_rows) + swap(other_half(low), "head", 1).astype(jnp.float32)
-    total = pair
-    bit = 2
-    while bit < lax.axis_size("head"):
-        total = total + swap(total.astype(jnp.bfloat16), "head", bit).astype(jnp.float32)
-        bit *= 2
-    return total
+def summed_pair(partial_rows):
+    pair = own_half(partial_rows).astype(jnp.float32) + swap(
+        other_half(low(partial_rows)), "head", 1
+    ).astype(jnp.float32)
+    return pair
+
+
+def asked(total):
+    bits = bits_of("head")[1:]
+    for bit in bits[:-1]:
+        total = total + swap(low(total), "head", bit).astype(jnp.float32)
+    return total, swap(low(total), "head", bits[-1])
+
+
+def summed(parts):
+    return parts[0] + parts[1].astype(jnp.float32)
 
 
 def chunk_of(value, index):
@@ -768,150 +1039,215 @@
     shard = proj_master.shape[1]
     heads = width // DK
     scal = jnp.stack([lengths[0] - seq_index * rows, seq_index * rows]).astype(jnp.int32)
-    qkv = jnp.transpose(proj_master[:3], (1, 0, 2)).reshape(shard, 3 * width).astype(bf16)
-    wide = 3 * width // 2
-    w_qkv_a, w_qkv_b, late = ring_gather(qkv[:, :wide], qkv[:, wide:])
-    w_gate, w_out, late = ring_gather(
-        *after((proj_master[3].astype(bf16), out_master.astype(bf16)), late)
-    )
-    cut = (units // 2 + DK - 1) // DK * DK
-    down_low = down_master.astype(bf16)
-    w_down_a, w_down_b, late = ring_gather(*after((down_low[:cut], down_low[cut:]), late))
-    mlp_low = mlp_master.astype(bf16)
-    w_mlp_g, w_mlp_u, late = ring_gather(*after((mlp_low[0], mlp_low[1]), late))
+    flow = Flow()
     sizes = [conv_master.size, beta_master.size, gains_master.size]
-    packed = jnp.concatenate(
-        [conv_master.reshape(-1), beta_master.reshape(-1), gains_master.reshape(-1)]
-    ).astype(bf16)
-    packed = jnp.pad(packed, (0, -packed.size % 2048))
-    small = gather_small(packed)
+    packed = low(
+        jnp.concatenate(
+            [conv_master.reshape(-1), beta_master.reshape(-1), gains_master.reshape(-1)]
+        )
+    )
+    small = jnp.pad(packed, (0, -packed.size % 2048))[None]
+    seq_bits = bits_of("seq")
+    small = gather_round(small, seq_bits[0])
+    proj_low = low(proj_master)
+    ring_p = Gather(
+        jnp.concatenate([proj_low[0], proj_low[1]], axis=1),
+        jnp.concatenate([proj_low[2], proj_low[3]], axis=1),
+    )
+    flow.step(ring_p, 0)
+    flow.step(ring_p, 1)
+    cut = (units + width) // 2 // DK * DK
+    rest = units - cut
+    down_low = jnp.transpose(low(down_master))
+    out_low = jnp.transpose(low(out_master))
+    mlp_low = low(mlp_master)
+    sources, targets = ring_sources(), ring_targets()
+    x_ring = pick_columns(block_input, sources)
+    dy_ring = pick_columns(cotangent, sources)
+    x_rows = x_ring.astype(f32)
+    x_inv = inverse_size(x_rows)
+    x_ring, dy_ring, x_inv = flow.step(ring_p, 2, (x_ring, dy_ring, x_inv))
+    x_rows = x_ring.astype(f32)
+    small = flow.step(ring_p, 3, small)
+    ring_do = Gather(
+        down_low[:, :cut], jnp.concatenate([down_low[:, cut:], out_low], axis=1)
+    )
+    ring_m = Gather(mlp_low[0], mlp_low[1])
+    small = gather_round(small, seq_bits[1])
+    flow.step(ring_p, 4)
+    ring_do.held[0][0], ring_do.held[1][0], ring_m.held[0][0], ring_m.held[1][0], small = flow.step(
+        ring_p,
+        5,
+        (ring_do.held[0][0], ring_do.held[1][0], ring_m.held[0][0], ring_m.held[1][0], small),
+    )
+    flow.step(ring_p, 6)
+    for bit in seq_bits[2:]:
+        small = gather_round(small, bit)
+    small = flow.step(ring_p, 7, small)
     conv_all = small[:, : sizes[0]].reshape(count, 3, CONV, -1)
     taps = jnp.transpose(conv_all, (1, 2, 0, 3)).reshape(3, CONV, width).astype(f32)
     beta_all = small[:, sizes[0] : sizes[0] + sizes[1]].reshape(D, heads)
     gains_all = small[:, sizes[0] + sizes[1] : sum(sizes)].reshape(-1)
-    columns = to_ring(
-        jnp.concatenate([gains_all[: 2 * D].reshape(2, D), jnp.transpose(beta_all)], axis=0)
-    )
+    columns = jnp.concatenate([gains_all[: 2 * D].reshape(2, D), jnp.transpose(beta_all)], axis=0)
+    columns = jnp.take(columns.reshape(2 + heads, count, -1), sources, axis=1).reshape(-1, D)
     gain_a = columns[0:1].astype(f32)
     gain_m = columns[1:2].astype(f32)
     w_beta = columns[2:]
     gain_o = gains_all[2 * D :].astype(f32)[None]
-    x_ring = to_ring(block_input)
-    dy_ring = to_ring(cotangent)
-    x_rows = x_ring.astype(f32)
-    x_inv = inverse_size(x_rows)
     hidden = (x_rows * x_inv * gain_a).astype(bf16)
+    hidden = flow.step(ring_do, 0, hidden)
     logits = dot_nt(hidden, w_beta)
-
-    def over_chunks(value, weights, order):
-        total = None
-        for one in order:
-            term = dot(chunk_of(value, one), weights[one])
-            total = term if total is None else total + term
-        return total
-
-    order = [0]
-    for step in range(1, count // 2):
-        order += [count - step, step]
-    order.append(count // 2)
-    pre = jnp.concatenate(
-        [over_chunks(hidden, w_qkv_a, order), over_chunks(hidden, w_qkv_b, order)], axis=1
-    ).astype(bf16)
-    pre = jnp.transpose(pre.reshape(rows, 3, width), (1, 0, 2))
-    halo = passed_along(pre[:, rows - 16 :], 1)
+    logits = flow.step(ring_do, 1, logits)
+    w_qk, w_vg = ring_p.held
+    low_rows = jax.ShapeDtypeStruct((rows, width), bf16)
+    (pre_q, pre_k, pre_v, gate), (w_qk, w_vg) = rows_dot(
+        hidden,
+        [(w_qk, 0, 2 * width), (w_vg, 0, 2 * width)],
+        [(0, 0, width, 0, 0), (0, width, width, 1, 0), (1, 0, width, 2, 0), (1, width, width, 3, 0)],
+        [low_rows] * 3 + [jax.ShapeDtypeStruct((rows, width), f32)],
+    )
+    pre = (pre_q, pre_k, pre_v)
+    pre, gate = flow.step(ring_do, 2, (pre, gate))
+    halo = passed_along(jnp.concatenate([one[rows - 16 :] for one in pre], axis=1), 1)
+    halo = flow.step(ring_do, 3, halo)
     q, k, w, uv, t, state_add, state_map = delta_local(scal, pre, halo, taps, logits)
-    gate = over_chunks(hidden, w_gate, order)
+    state_add, state_map = flow.step(ring_do, 4, (state_add, state_map))
     hops = -(-5 * count // 8) - 1
-    state_in = passed_along(state_add.astype(bf16), 1)
-    for _ in range(hops - 1):
-        moved = jnp.einsum("hij,hjk->hik", state_map, state_in, preferred_element_type=f32)
-        state_in = passed_along((moved + state_add).astype(bf16), 1)
+    state_in = passed_along(low(state_add), 1)
+
+    def hop(state):
+        moved = jnp.einsum("hij,hjk->hik", state_map, state, preferred_element_type=f32)
+        return passed_along(low(moved + state_add), 1)
+
+    state_in = flow.step(ring_do, 5, state_in)
+    third = (hops - 1) // 3
+    for _ in range(third):
+        state_in = hop(state_in)
+    state_in = flow.step(ring_do, 6, state_in)
+    for _ in range(third):
+        state_in = hop(state_in)
+    state_in = flow.step(ring_do, 7, state_in)
+    for _ in range(hops - 1 - 2 * third):
+        state_in = hop(state_in)
+    state_in = flow.step(ring_m, 0, state_in)
     normed, out_rows, change, states = delta_apply(scal, q, k, w, uv, state_in, gate, gain_o)
-    attn_part = jnp.concatenate([dot(normed, w_out[one]) for one in range(count)], axis=1)
-    x_one = own_half(x_rows) + summed_half(attn_part)
+    normed = flow.step(ring_m, 1, normed)
+    w_do_a, w_do_b = ring_do.held
+    (grad_act,), (w_down_a, w_down_b, w_out) = rows_dot(
+        dy_ring,
+        [(w_do_a, 0, cut), (w_do_b, 0, rest), (w_do_b, rest, width)],
+        [(0, 0, cut, 0, 0), (1, 0, rest, 0, cut)],
+        [jax.ShapeDtypeStruct((rows, units), f32)],
+    )
+    w_out, normed, grad_act = flow.step(ring_m, 2, (w_out, normed, grad_act))
+    pair = summed_pair(low(dot_nt(normed, w_out)))
+    pair = flow.step(ring_m, 3, pair)
+    parts = asked(pair)
+    flow.step(ring_m, 4)
+    parts = flow.step(ring_m, 5, parts)
+    x_one = own_half(x_rows) + summed(parts)
     one_inv = inverse_size(x_one)
-    h_two = both_halves((x_one * one_inv * gain_m).astype(bf16))
-    grad_act_a = None
-    grad_act_b = None
-    for one in order:
-        term_a = dot_nt(chunk_of(dy_ring, one), w_down_a[one])
-        term_b = dot_nt(chunk_of(dy_ring, one), w_down_b[one])
-        grad_act_a = term_a if grad_act_a is None else grad_act_a + term_a
-        grad_act_b = term_b if grad_act_b is None else grad_act_b + term_b
-    grad_act = jnp.concatenate([grad_act_a, grad_act_b], axis=1)
-    gate_u = over_chunks(h_two, w_mlp_g, order)
-    up_u = over_chunks(h_two, w_mlp_u, order)
-    sig = jax.nn.sigmoid(gate_u)
-    act = gate_u * sig
-    act_low = (act * up_u).astype(bf16)
-    grad_gate_u = (grad_act * up_u * (sig * (1.0 + gate_u * (1.0 - sig)))).astype(bf16)
-    grad_up_u = (grad_act * act).astype(bf16)
-    grad_h_part = jnp.concatenate(
-        [
-            dot_nt(grad_gate_u, w_mlp_g[one]) + dot_nt(grad_up_u, w_mlp_u[one])
-            for one in range(count)
-        ],
-        axis=1,
-    )
-    grad_h_two = summed_half(grad_h_part)
-    x_half_grad = norm_back(x_one, one_inv, gain_m, grad_h_two)
+    h_two = both_halves(low(x_one * one_inv * gain_m))
+    h_two, x_one = flow.step(ring_m, 6, (h_two, x_one))
+    gates, ups = ring_m.held
+    half = count // 2
+    *sums, w_mlp_g, w_mlp_u = glu_early(
+        h_two,
+        {one: piece for one, piece in gates.items() if abs(one - half) > 1},
+        {one: piece for one, piece in ups.items() if abs(one - half) > 1},
+    )
+    sums, w_mlp_g, w_mlp_u, h_two = flow.step(ring_m, 7, (sums, w_mlp_g, w_mlp_u, h_two))
+    late = (half - 1, half, half + 1)
+    shard = gates[half].shape[0]
+    act_low, grad_gate_u, grad_up_u = glu_late(
+        h_two[:, late[0] * shard : (late[-1] + 1) * shard],
+        [gates[one] for one in late],
+        [ups[one] for one in late],
+        sums,
+        grad_act,
+    )
+    for one in late:
+        w_mlp_g = lax.dynamic_update_slice_in_dim(w_mlp_g, gates[one], one * shard, 0)
+        w_mlp_u = lax.dynamic_update_slice_in_dim(w_mlp_u, ups[one], one * shard, 0)
+    def rows_of(value):
+        piece = value.shape[0] // count
+        return lambda one: value[one * piece : (one + 1) * piece]
+
+    back_m = Scatter(
+        rows_of(low(dot_tn(h_two, grad_gate_u))), rows_of(low(dot_tn(h_two, grad_up_u)))
+    )
+    flow.step(back_m, 0)
+    grad_gate_u, grad_up_u, act_low = flow.step(back_m, 1, (grad_gate_u, grad_up_u, act_low))
+    part = low(dot_nt(grad_gate_u, w_mlp_g) + dot_nt(grad_up_u, w_mlp_u))
+    part = flow.step(back_m, 2, part)
+    pair, act_low = flow.step(back_m, 3, (summed_pair(part), act_low))
+    parts = asked(pair)
+    part = low(dot_nt(act_low[:, :cut], w_down_a) + dot_nt(act_low[:, cut:], w_down_b))
+    part = flow.step(back_m, 4, part)
+    parts, part = flow.step(back_m, 5, (parts, part))
+    mlp_pair = summed_pair(part)
+    grad_h_two = summed(parts)
     grad_gain_m = 0.5 * jnp.sum(grad_h_two * x_one * one_inv, axis=0, keepdims=True)
-    grad_x_one = own_half(dy_ring).astype(f32) + x_half_grad
-    grad_attn = both_halves(grad_x_one.astype(bf16))
-    down_a_sum, down_b_sum = ring_scatter(
-        lambda one: dot_tn(act_low[:, :cut], chunk_of(dy_ring, one)),
-        lambda one: dot_tn(act_low[:, cut:], chunk_of(dy_ring, one)),
-    )
-    mlp_g_sum, mlp_u_sum = ring_scatter(
-        lambda one: dot_tn(chunk_of(h_two, one), grad_gate_u),
-        lambda one: dot_tn(chunk_of(h_two, one), grad_up_u),
-    )
-    mlp_part = jnp.concatenate(
-        [
-            dot(act_low[:, :cut], w_down_a[one]) + dot(act_low[:, cut:], w_down_b[one])
-            for one in range(count)
-        ],
-        axis=1,
-    )
-    result = from_ring(both_halves(x_one + summed_half(mlp_part)))
-    grad_normed = sum(dot_nt(chunk_of(grad_attn, one), w_out[one]) for one in range(count))
+    grad_x_one = own_half(dy_ring).astype(f32) + norm_back(x_one, one_inv, gain_m, grad_h_two)
+    grad_attn = both_halves(low(grad_x_one))
+    grad_normed = dot(grad_attn, w_out)
+    grad_normed, grad_attn, mlp_pair, act_low = flow.step(
+        back_m, 6, (grad_normed, grad_attn, mlp_pair, act_low)
+    )
+    mlp_parts = asked(mlp_pair)
     grad_gate, grad_gain_o, grad_out, through, carry = delta_back_local(
         scal, grad_normed, gate, gain_o, out_rows, q, k, w
     )
-    gate_sum, out_sum = ring_scatter(
-        lambda one: dot_tn(chunk_of(hidden, one), grad_gate),
-        lambda one: dot_tn(normed, chunk_of(grad_attn, one)),
-    )
-    above = passed_along(carry.astype(bf16), -1)
-    for _ in range(hops - 1):
-        moved = jnp.einsum("hji,hjk->hik", state_map, above, preferred_element_type=f32)
-        above = passed_along((moved + carry).astype(bf16), -1)
+    grad_gate, carry, act_low = flow.step(back_m, 7, (grad_gate, carry, act_low))
+    above = passed_along(low(carry), -1)
+    grad_do_a = low(dot_tn(dy_ring, act_low[:, :cut]))
+    grad_do_b = jnp.concatenate(
+        [low(dot_tn(dy_ring, act_low[:, cut:])), low(dot_tn(grad_attn, normed))], axis=1
+    )
+    back_do = Scatter(rows_of(grad_do_a), rows_of(grad_do_b))
+
+    def hop_back(state):
+        moved = jnp.einsum("hji,hjk->hik", state_map, state, preferred_element_type=f32)
+        return passed_along(low(moved + carry), -1)
+
+    above = flow.step(back_do, 0, above)
+    for _ in range(third):
+        above = hop_back(above)
+    above, mlp_parts = flow.step(back_do, 1, (above, mlp_parts))
+    for _ in range(third):
+        above = hop_back(above)
+    above = flow.step(back_do, 2, above)
+    for _ in range(hops - 1 - 2 * third):
+        above = hop_back(above)
+    above = flow.step(back_do, 3, above)
     grad_pre, tail, back_halo, grad_taps, grad_logits = delta_back(
         scal, pre, halo, taps, logits, q, k, w, t, change, states, grad_out, through, above
     )
-    fixed = (tail + passed_along(back_halo, -1)).astype(bf16)
+    mlp_sum = flow.step(back_do, 4, summed(mlp_parts))
+    result = join_columns(x_one + mlp_sum, targets)
+    grad_pre, back_halo, tail, grad_logits, result = flow.step(
+        back_do, 5, (grad_pre, back_halo, tail, grad_logits, result)
+    )
+    fixed = low(tail + passed_along(back_halo, -1))
     grad_pre = lax.dynamic_update_slice_in_dim(grad_pre, fixed, rows - 8, 1)
-    grad_qkv = jnp.transpose(grad_pre, (1, 0, 2)).reshape(rows, 3 * width)
-    grad_logits = grad_logits.astype(bf16)
-    qkv_a_sum, qkv_b_sum = ring_scatter(
-        lambda one: dot_tn(chunk_of(hidden, one), grad_qkv[:, :wide]),
-        lambda one: dot_tn(chunk_of(hidden, one), grad_qkv[:, wide:]),
-    )
-    grad_hidden = jnp.concatenate(
-        [
-            dot_nt(grad_qkv[:, :wide], w_qkv_a[one])
-            + dot_nt(grad_qkv[:, wide:], w_qkv_b[one])
-            + dot_nt(grad_gate, w_gate[one])
-            for one in range(count)
-        ],
-        axis=1,
-    ) + dot(grad_logits, w_beta)
-    grad_gain_a = jnp.sum(grad_hidden * x_rows * x_inv, axis=0, keepdims=True)
-    grad_hidden_half = summed_half(grad_hidden)
-    grad_x_rest = norm_back(own_half(x_rows), own_half(x_inv), gain_a, grad_hidden_half)
-    input_grad = from_ring(both_halves(grad_x_one + grad_x_rest))
+    grad_qk = jnp.concatenate([grad_pre[0], grad_pre[1]], axis=1)
+    grad_vg = jnp.concatenate([grad_pre[2], grad_gate], axis=1)
+    grad_qk, grad_vg = flow.step(back_do, 6, (grad_qk, grad_vg))
+    back_p = Scatter(
+        rows_of(low(dot_tn(hidden, grad_qk))), rows_of(low(dot_tn(hidden, grad_vg)))
+    )
+    flow.step(back_do, 7)
+    grad_qk, grad_vg, grad_logits = flow.step(back_p, 0, (grad_qk, grad_vg, grad_logits))
+    grad_logits = low(grad_logits)
+    grad_hidden = low(
+        dot_nt(grad_qk, w_qk) + dot_nt(grad_vg, w_vg) + dot(grad_logits, w_beta)
+    )
     grad_beta = dot_tn(grad_logits, hidden)
-    stacked = from_ring(jnp.concatenate([grad_gain_a, grad_gain_m, grad_beta], axis=0))
+    grad_hidden, grad_beta = flow.step(back_p, 1, (grad_hidden, grad_beta))
+    pair = summed_pair(grad_hidden)
+    grad_gain_a = jnp.sum(grad_hidden.astype(f32) * x_rows * x_inv, axis=0, keepdims=True)
+    stacked = jnp.concatenate([grad_gain_a, grad_gain_m, grad_beta], axis=0)
+    stacked = jnp.take(stacked.reshape(2 + heads, count, -1), targets, axis=1).reshape(-1, D)
     grad_gains = jnp.concatenate(
         [stacked[:2].reshape(-1), jnp.sum(grad_gain_o[:, 0], axis=0)]
     ).reshape(count, -1)
@@ -919,18 +1255,48 @@
         grad_taps.reshape(3, CONV, count, width // count), (2, 0, 1, 3)
     ).reshape(count, -1)
     grad_beta = jnp.transpose(stacked[2:]).reshape(count, -1)
-    small_sum = scatter_small(jnp.concatenate([grad_conv, grad_beta, grad_gains], axis=1))
+    small_sum = jnp.concatenate([grad_conv, grad_beta, grad_gains], axis=1)
+    small_sum, pair = flow.step(back_p, 2, (small_sum, pair))
+    parts = asked(pair)
+    flow.step(back_p, 3)
+    small_sum, parts = flow.step(back_p, 4, (small_sum, parts))
+    small_sum = scatter_round(small_sum, seq_bits[-1])
+    mlp_g_sum, mlp_u_sum = back_m.sums()
+    mlp_new, mlp_first_new, mlp_second_new = adam_update(
+        mlp_master, mlp_first, mlp_second, jnp.stack([mlp_g_sum, mlp_u_sum]),
+        rate_matrix, decay_matrix,
+    )
+    small_sum, mlp_new, mlp_first_new, mlp_second_new = flow.step(
+        back_p, 5, (small_sum, mlp_new, mlp_first_new, mlp_second_new)
+    )
+    for bit in seq_bits[-2:0:-1]:
+        small_sum = scatter_round(small_sum, bit)
+    grad_x_rest = norm_back(own_half(x_rows), own_half(x_inv), gain_a, summed(parts))
+    input_half = grad_x_one + grad_x_rest
+    small_sum, input_half = flow.step(back_p, 6, (small_sum, input_half))
+    small_sum = scatter_round(small_sum, seq_bits[0])[0]
+    do_a_sum, do_b_sum = back_do.sums()
+    summed_down = jnp.transpose(jnp.concatenate([do_a_sum, do_b_sum[:, :rest]], axis=1))
+    out_sum = jnp.transpose(do_b_sum[:, rest:])
+    down_new, down_first_new, down_second_new = adam_update(
+        down_master, down_first, down_second, summed_down, rate_down, decay_matrix
+    )
+    out_new, out_first_new, out_second_new = adam_update(
+        out_master, out_first, out_second, out_sum, rate_matrix, decay_matrix
+    )
+    input_grad = join_columns(input_half, targets)
+    small_sum, input_grad, down_new, down_first_new, down_second_new = flow.step(
+        back_p, 7, (small_sum, input_grad, down_new, down_first_new, down_second_new)
+    )
     gains_sum = small_sum[sizes[0] + sizes[1] :]
-    bit = 1
-    while bit < lax.axis_size("head"):
+    for bit in bits_of("head"):
         gains_sum = gains_sum + swap(gains_sum, "head", bit)
-        bit *= 2
     summed_conv = small_sum[: sizes[0]].reshape(conv_master.shape)
     summed_beta = small_sum[sizes[0] : sizes[0] + sizes[1]].reshape(beta_master.shape)
-    qkv_sum = jnp.concatenate([qkv_a_sum, qkv_b_sum], axis=1).reshape(shard, 3, width)
-    summed_proj = jnp.concatenate([jnp.transpose(qkv_sum, (1, 0, 2)), gate_sum[None]], axis=0)
-    summed_mlp = jnp.stack([mlp_g_sum, mlp_u_sum])
-    summed_down = jnp.concatenate([down_a_sum, down_b_sum], axis=0)
+    qk_sum, vg_sum = back_p.sums()
+    summed_proj = jnp.stack(
+        [qk_sum[:, :width], qk_sum[:, width:], vg_sum[:, :width], vg_sum[:, width:]]
+    )
     proj_new, proj_first_new, proj_second_new = adam_update(
         proj_master, proj_first, proj_second, summed_proj, rate_matrix, decay_matrix
     )
@@ -939,15 +1305,6 @@
     )
     conv_new, conv_first_new, conv_second_new = adam_update(
         conv_master, conv_first, conv_second, summed_conv, rate_conv, decay_matrix
-    )
-    out_new, out_first_new, out_second_new = adam_update(
-        out_master, out_first, out_second, out_sum, rate_matrix, decay_matrix
-    )
-    mlp_new, mlp_first_new, mlp_second_new = adam_update(
-        mlp_master, mlp_first, mlp_second, summed_mlp, rate_matrix, decay_matrix
-    )
-    down_new, down_first_new, down_second_new = adam_update(
-        down_master, down_first, down_second, summed_down, rate_down, decay_matrix
     )
     gains_new, gains_first_new, gains_second_new = adam_update(
         gains_master, gains_first, gains_second, gains_sum, rate_gains, 0.0

time: 910 us -> 716 us (0.79)
  matrix products: 180 us -> 43.1 us
  Pallas kernels: 43.2 us -> 96.6 us
  local copies, waits for them, and re-layouts: 111 us -> 66.2 us
  starting transfers between devices: 183 us -> 143 us
  waiting for transfers between devices: 304 us -> 277 us
    ppermute x56 -> x42, waiting for transfers between devices: 125 us -> 49.4 us  [send_down(): lax.ppermute(value, 'seq', [(b, a) for a, b in ring_pairs(lax.axis_size('...]
    dot_general x65 -> x2, matrix products: 61.3 us -> 1.99 us  [dot(): return jnp.dot(a, b, preferred_element_type=jnp.float32)]
    pallas_call x0 -> x8, Pallas kernels: none -> 52.8 us  [the longest x2 23.1 us: rows_dot(): pl.pallas_call(partial(_rows_dot_kernel, count, ranges, outs), in_specs=[...]
    dot_general x65 -> x8, matrix products: 60.5 us -> 18.7 us  [dot_tn(): lax.dot_general(a, b, (((0,), (0,)), ((), ())), preferred_element_type=jn...]
    unnamed x414 -> x309, local copies, waits for them, and re-layouts: 78.4 us -> 39.6 us
    dot_general x65 -> x8, matrix products: 57 us -> 19.6 us  [dot_nt(): lax.dot_general(a, b, (((1,), (1,)), ((), ())), preferred_element_type=jn...]
    ppermute x10, waiting for transfers between devices: 17.2 us -> 47.8 us  [passed_along(): lax.ppermute(value, 'seq', [(source, source + steps) for source in range(...]
    convert_element_type x6 -> x28, other arithmetic: 0.56 us -> 27.8 us  [low(): return value.astype(jnp.bfloat16)]
  transfers between devices with their start and end apart: 142 -> 114, of which waited for: 60 -> 53; matrix products, arithmetic and copies ran while one was open for 31% -> 16% of each run, Pallas kernels for 5% -> 13%
where the time goes in v2:
time: 716 us; the launch traced here: 707 us
  waiting for transfers between devices  277 us (39%)
  starting transfers between devices  143 us (20%)
  Pallas kernels  96.6 us (13%)
  other arithmetic  76.8 us (11%)
  local copies, waits for them, and re-layouts  66.2 us (9%)
  matrix products  43.1 us (6%)
    ppermute x42, waiting for transfers between devices, send_up(): return lax.ppermute(value, 'seq', ring_pairs(lax.axis_size('seq')))  145 us
    ppermute x42, starting transfers between devices, send_up(): return lax.ppermute(value, 'seq', ring_pairs(lax.axis_size('seq')))  64.8 us
    ppermute x42, waiting for transfers between devices, send_down(): lax.ppermute(value, 'seq', [(b, a) for a, b in ring_pairs(lax.axis_size('...  49.4 us
    ppermute x10, waiting for transfers between devices, passed_along(): lax.ppermute(value, 'seq', [(source, source + steps) for source in range(...  47.8 us
    ppermute x42, starting transfers between devices, send_down(): lax.ppermute(value, 'seq', [(b, a) for a, b in ring_pairs(lax.axis_size('...  43.5 us
    unnamed x309, local copies, waits for them, and re-layouts  39.6 us
    ppermute x20, waiting for transfers between devices, swap(): return lax.ppermute(value, axis, [(one, one ^ bit) for one in range(count)])  34.9 us
    convert_element_type x28, other arithmetic, low(): return value.astype(jnp.bfloat16)  27.8 us
  transfers between devices with their start and end apart: 114, of which 53 were waited for; matrix products, arithmetic and copies ran while one was open for 16% of the time, Pallas kernels for 13%

profile of v2, /device:TPU:0, one launch (start us, length us, event | category | flops | bytes accessed | tf_op | source)
XLA Modules:
  0.0 706.7 jit_solution(5768418453164632433)
XLA Ops:
  38.5 7.0 collective-permute-done.5.refs_15_
  84.5 9.3 %collective-permute-done.16.refs_5_ = bf16[256,1024]{1,0:T(8,128)(2,1)S(1)} collective-permute-done((bf16[256,1024]{1,0:T(8,128)(2,1)}, bf16[256,1024]{1,0:T(8,128)(2,1)S(1)}, u32[]{:S(2)}, u32[]{:S(2)}) %collective-permute-start.16) | collective-permute-done | bytes 524320 | tf_op jit(solution)/shard_map/ppermute | solution.py:586
  98.9 11.0 %rows_dot.2 = (bf16[512,512]{1,0:T(8,128)(2,1)S(1)}, bf16[512,512]{1,0:T(8,128)(2,1)S(1)}, bf16[512,512]{1,0:T(8,128)(2,1)S(1)}, f32[512,512]{1,0:T(8,128)}, bf1...) custom-call(bf16[512,2048]{1,0:T(8,128)(2,1)} %copy-done.64, bf16[256,1024]{1,0:T(8,128)(2,1)} %pad_maximum_fusion.5.refs_1_, ...), custom_call_target="tpu_custom_call" | custom-call | flops 13200000000 | bytes 43200000 | tf_op jit(solution)/shard_map/rows_dot/pallas_call | solution.py:804
  125.4 10.8 %delta_local.1 = (bf16[512,512]{1,0:T(8,128)(2,1)S(1)}, bf16[512,512]{1,0:T(8,128)(2,1)S(1)}, bf16[512,512]{1,0:T(8,128)(2,1)S(1)}, f32[512,512]{1,0:T(8,128)S(1...) custom-call(s32[2]{0:T(128)S(1)} %pad_add_fusion.scal_ref, ...), custom_call_target="tpu_custom_call" | custom-call | flops 12099999744 | bytes 39600000 | tf_op jit(solution)/shard_map/delta_local/pallas_call | solution.py:473
  153.9 11.2 %collective-permute-done.31 = bf16[4,128,128]{2,1,0:T(8,128)(2,1)S(1)} collective-permute-done((bf16[4,128,128]{2,1,0:T(8,128)(2,1)S(1)}, bf16[4,128,128]{2,1,0:T(8,128)(2,1)S(1)}, u32[]{:S(2)}, u32[]{:S(2)}) %collective-permute-start.31) | collective-permute-done | bytes 131104 | tf_op jit(solution)/shard_map/ppermute | solution.py:997
  175.2 5.5 collective-permute-start.35
  184.8 5.2 collective-permute-start.38
  194.3 6.9 delta_apply.1
  203.1 12.1 %rows_dot.3 = (f32[512,1408]{1,0:T(8,128)}, bf16[2048,896]{1,0:T(8,128)(2,1)}, bf16[2048,512]{1,0:T(8,128)(2,1)}, bf16[2048,512]{1,0:T(8,128)(2,1)}) custom-call(bf16[512,2048]{1,0:T(8,128)(2,1)} %copy-done.2, bf16[256,896]{1,0:T(8,128)(2,1)S(1)} %copy-done.5, bf16[256,896]{1,0:T(8,128)(2,1)S(1)} %copy-done.23, bf16[256,896]{1,0:T(8,128)(2,1)S(1)} %copy-done.27, ...), custom_call_target="tpu_custom_call" | custom-call | flops 13200000000 | bytes 43200000 | tf_op jit(solution)/shard_map/rows_dot/pallas_call | solution.py:804
  225.3 14.0 %collective-permute-done.36.refs_16_ = bf16[256,1408]{1,0:T(8,128)(2,1)} collective-permute-done((bf16[256,1408]{1,0:T(8,128)(2,1)}, bf16[256,1408]{1,0:T(8,128)(2,1)}, u32[]{:S(2)}, u32[]{:S(2)}) %collective-permute-start.36) | collective-permute-done | bytes 720928 | tf_op jit(solution)/shard_map/ppermute | solution.py:586
  247.6 14.4 %collective-permute-done.41.refs_15_ = bf16[256,1408]{1,0:T(8,128)(2,1)S(1)} collective-permute-done((bf16[256,1408]{1,0:T(8,128)(2,1)}, bf16[256,1408]{1,0:T(8,128)(2,1)S(1)}, u32[]{:S(2)}, u32[]{:S(2)}) %collective-permute-start.41) | collective-permute-done | bytes 720928 | tf_op jit(solution)/shard_map/ppermute | solution.py:586
  267.7 7.9 %collective-permute-done.46.refs_7_ = bf16[256,1408]{1,0:T(8,128)(2,1)} collective-permute-done((bf16[256,1408]{1,0:T(8,128)(2,1)S(1)}, bf16[256,1408]{1,0:T(8,128)(2,1)}, u32[]{:S(2)}, u32[]{:S(2)}) %collective-permute-start.46) | collective-permute-done | bytes 720928 | tf_op jit(solution)/shard_map/ppermute | solution.py:586
  284.7 10.6 %collective-permute-done.48.refs_2_ = bf16[256,1408]{1,0:T(8,128)(2,1)S(1)} collective-permute-done((bf16[256,1408]{1,0:T(8,128)(2,1)}, bf16[256,1408]{1,0:T(8,128)(2,1)S(1)}, u32[]{:S(2)}, u32[]{:S(2)}) %collective-permute-start.48) | collective-permute-done | bytes 720928 | tf_op jit(solution)/shard_map/ppermute | solution.py:586
  296.2 12.3 %glu_early.1 = (f32[512,1408]{1,0:T(8,128)}, f32[512,1408]{1,0:T(8,128)}, bf16[2048,1408]{1,0:T(8,128)(2,1)}, bf16[2048,1408]{1,0:T(8,128)(2,1)}) custom-call(bf16[512,2048]{1,0:T(8,128)(2,1)} %maximum_select_fusion.refs_0_, bf16[256,1408]{1,0:T(8,128)(2,1)S(1)} %get-tuple-element.313.refs_1_.refs_4_.refs_5_.refs_6_, bf16[256,1408]{1,0:T(8,128)(2,1)S(1)} %copy-done.19, ...), custom_call_target="tpu_custom_call" | custom-call | flops 15399999488 | bytes 50400000 | tf_op jit(solution)/shard_map/glu_early/pallas_call | solution.py:851
  314.1 9.3 %collective-permute-done.51.refs_1_ = bf16[256,1408]{1,0:T(8,128)(2,1)S(1)} collective-permute-done((bf16[256,1408]{1,0:T(8,128)(2,1)S(1)}, bf16[256,1408]{1,0:T(8,128)(2,1)S(1)}, u32[]{:S(2)}, u32[]{:S(2)}) %collective-permute-start.51) | collective-permute-done | bytes 720928 | tf_op jit(solution)/shard_map/ppermute | solution.py:586
  327.2 7.5 %glu_late.1 = (bf16[512,1408]{1,0:T(8,128)(2,1)}, bf16[512,1408]{1,0:T(8,128)(2,1)}, bf16[512,1408]{1,0:T(8,128)(2,1)}) custom-call(bf16[512,768]{1,0:T(8,128)(2,1)S(1)} %slice.320.value_ref, bf16[256,1408]{1,0:T(8,128)(2,1)S(1)} %collective-permute-done.49.refs_0_, bf16[256,1408]{1,0:T(8,128)(2,1)S(1)} %collective-permute-done.51.refs_1_, ...), custom_call_target="tpu_custom_call" | custom-call | flops 8800000000 | bytes 28800000 | tf_op jit(solution)/shard_map/glu_late/pallas_call | solution.py:899
  358.0 6.0 collective-permute-done.55
  373.7 11.4 %collective-permute-done.53 = bf16[256,1408]{1,0:T(8,128)(2,1)S(1)} collective-permute-done((bf16[256,1408]{1,0:T(8,128)(2,1)}, bf16[256,1408]{1,0:T(8,128)(2,1)S(1)}, u32[]{:S(2)}, u32[]{:S(2)}) %collective-permute-start.53) | collective-permute-done | bytes 720928 | tf_op jit(solution)/shard_map/ppermute | solution.py:586
  394.4 6.2 collective-permute-done.61
  404.5 11.5 %collective-permute-done.58 = bf16[256,1408]{1,0:T(8,128)(2,1)S(1)} collective-permute-done((bf16[256,1408]{1,0:T(8,128)(2,1)S(1)}, bf16[256,1408]{1,0:T(8,128)(2,1)S(1)}, u32[]{:S(2)}, u32[]{:S(2)}) %collective-permute-start.58) | collective-permute-done | bytes 720928 | tf_op jit(solution)/shard_map/ppermute | solution.py:586
  433.2 9.2 %delta_back_local.1 = (bf16[512,512]{1,0:T(8,128)(2,1)S(1)}, f32[4,8,128]{2,1,0:T(8,128)S(1)}, bf16[512,512]{1,0:T(8,128)(2,1)S(1)}, f32[512,512]{1,0:T(8,128)S(1)}, f32[4,128,128]{2,1,0:T(8,128)S(1)}) custom-call(s32[2]{0:T(128)S(1)} %pad_add_fusion.scal_ref, f32[512,512]{1,0:T(8,128)S(1)} %fusion.64.dn_ref, f32[512,512]{1,0:T(8,128)S(1)} %copy-done.35, ...), custom_call_target="tpu_custom_call" | custom-call | flops 9900000256 | bytes 32400000 | tf_op jit(solution)/shard_map/delta_back_local/pallas_call | solution.py:523
  461.8 12.6 %collective-permute-done.71 = bf16[4,128,128]{2,1,0:T(8,128)(2,1)S(1)} collective-permute-done((bf16[4,128,128]{2,1,0:T(8,128)(2,1)S(1)}, bf16[4,128,128]{2,1,0:T(8,128)(2,1)S(1)}, u32[]{:S(2)}, u32[]{:S(2)}) %collective-permute-start.71) | collective-permute-done | bytes 131104 | tf_op jit(solution)/shard_map/ppermute | solution.py:997
  500.4 17.1 %collective-permute-done.79.above_ref = bf16[4,128,128]{2,1,0:T(8,128)(2,1)S(1)} collective-permute-done((bf16[4,128,128]{2,1,0:T(8,128)(2,1)S(1)}, bf16[4,128,128]{2,1,0:T(8,128)(2,1)S(1)}, u32[]{:S(2)}, u32[]{:S(2)}) %collective-permute-start.79) | collective-permute-done | bytes 131104 | tf_op jit(solution)/shard_map/ppermute | solution.py:997
  521.7 16.9 %delta_back.1 = (bf16[3,512,512]{2,1,0:T(8,128)(2,1)}, f32[3,8,512]{2,1,0:T(8,128)S(1)}, f32[3,8,512]{2,1,0:T(8,128)S(1)}, f32[3,4,512]{2,1,0:T(4,128)S(1)}, f32[512,4]{1,0:T(8,128)S(1)}) custom-call(s32[2]{0:T(128)S(1)} %pad_add_fusion.scal_ref, bf16[512,512]{1,0:T(8,128)(2,1)S(1)} %copy-done.8, bf16[512,512]{1,0:T(8,128)(2,1)S(1)} %copy-done.11, ...), custom_call_target="tpu_custom_call" | custom-call | flops 18699999232 | bytes 61200000 | tf_op jit(solution)/shard_map/delta_back/pallas_call | solution.py:548
  566.2 8.8 %collective-permute-done.91 = bf16[256,896]{0,1:T(8,128)(2,1)S(1)} collective-permute-done((bf16[256,896]{0,1:T(8,128)(2,1)S(1)}, bf16[256,896]{0,1:T(8,128)(2,1)S(1)}, u32[]{:S(2)}, u32[]{:S(2)}) %collective-permute-start.91) | collective-permute-done | bytes 458784 | tf_op jit(solution)/shard_map/ppermute | solution.py:586
  586.9 13.0 %collective-permute-done.90 = bf16[256,1024]{0,1:T(8,128)(2,1)S(1)} collective-permute-done((bf16[256,1024]{0,1:T(8,128)(2,1)S(1)}, bf16[256,1024]{0,1:T(8,128)(2,1)S(1)}, u32[]{:S(2)}, u32[]{:S(2)}) %collective-permute-start.90) | collective-permute-done | bytes 524320 | tf_op jit(solution)/shard_map/ppermute | solution.py:590
  625.1 8.7 %collective-permute-done.100 = bf16[256,1024]{1,0:T(8,128)(2,1)S(1)} collective-permute-done((bf16[256,1024]{1,0:T(8,128)(2,1)S(1)}, bf16[256,1024]{1,0:T(8,128)(2,1)S(1)}, u32[]{:S(2)}, u32[]{:S(2)}) %collective-permute-start.100) | collective-permute-done | bytes 524320 | tf_op jit(solution)/shard_map/ppermute | solution.py:590
  640.8 7.1 %collective-permute-done.102 = f32[4,2320]{1,0:T(4,128)S(1)} collective-permute-done((f32[4,2320]{1,0:T(4,128)S(1)}, f32[4,2320]{1,0:T(4,128)S(1)}, u32[]{:S(2)}, u32[]{:S(2)}) %collective-permute-start.102) | collective-permute-done | bytes 37152 | tf_op jit(solution)/shard_map/ppermute | solution.py:913
  648.7 8.0 %collective-permute-done.107 = f32[2,2320]{1,0:T(2,128)S(1)} collective-permute-done((f32[2,2320]{1,0:T(2,128)S(1)}, f32[2,2320]{1,0:T(2,128)S(1)}, u32[]{:S(2)}, u32[]{:S(2)}) %collective-permute-start.107) | collective-permute-done | bytes 18592 | tf_op jit(solution)/shard_map/ppermute | solution.py:913
  664.6 9.0 %collective-permute-done.108 = f32[1,2320]{1,0:T(1,128)S(1)} collective-permute-done((f32[1,2320]{1,0:T(1,128)S(1)}, f32[1,2320]{1,0:T(1,128)S(1)}, u32[]{:S(2)}, u32[]{:S(2)}) %collective-permute-start.108) | collective-permute-done | bytes 9312 | tf_op jit(solution)/shard_map/ppermute | solution.py:913
  677.2 7.3 %collective-permute-done.103 = bf16[256,1024]{1,0:T(8,128)(2,1)} collective-permute-done((bf16[256,1024]{1,0:T(8,128)(2,1)S(1)}, bf16[256,1024]{1,0:T(8,128)(2,1)}, u32[]{:S(2)}, u32[]{:S(2)}) %collective-permute-start.103) | collective-permute-done | bytes 524320 | tf_op jit(solution)/shard_map/ppermute | solution.py:586
  695.8 5.1 collective-permute-done.111
  (713 shorter events, 390.2 us)
Async XLA Ops:
  3.4 26.8 %collective-permute-start.2 = (bf16[256,1024]{1,0:T(8,128)(2,1)}, bf16[256,1024]{1,0:T(8,128)(2,1)}, u32[]{:S(2)}, u32[]{:S(2)}) collective-permute-start(bf16[256,1024]{1,0:T(8,128)(2,1)} %pad_maximum_fusion.6.refs_9_), channel_id=1, source_target_pairs={{0,8},{8,16},{16,24},{24,28},{28,20},{20,12},{12,4},{4,0},{1,9},{9... | collective-permute-start | bytes 1572872 | tf_op jit(solution)/shard_map/ppermute | solution.py:586
  7.3 26.9 %collective-permute-start = (bf16[256,1024]{1,0:T(8,128)(2,1)}, bf16[256,1024]{1,0:T(8,128)(2,1)}, u32[]{:S(2)}, u32[]{:S(2)}) collective-permute-start(bf16[256,1024]{1,0:T(8,128)(2,1)} %pad_maximum_fusion.5.refs_1_), channel_id=1, source_target_pairs={{0,8},{8,16},{16,24},{24,28},{28,20},{20,12},{12,4},{4,0},{1,9},{9... | collective-permute-start | bytes 1572872 | tf_op jit(solution)/shard_map/ppermute | solution.py:586
  9.3 24.9 %collective-permute-start.1 = (bf16[256,1024]{1,0:T(8,128)(2,1)}, bf16[256,1024]{1,0:T(8,128)(2,1)}, u32[]{:S(2)}, u32[]{:S(2)}) collective-permute-start(bf16[256,1024]{1,0:T(8,128)(2,1)} %pad_maximum_fusion.5.refs_1_), channel_id=1, source_target_pairs={{8,0},{16,8},{24,16},{28,24},{20,28},{12,20},{4,12},{0,4},{9,1},{1... | collective-permute-start | bytes 1572872 | tf_op jit(solution)/shard_map/ppermute | solution.py:590
  114.6 25.8 %collective-permute-start.24 = (bf16[256,896]{1,0:T(8,128)(2,1)}, bf16[256,896]{1,0:T(8,128)(2,1)S(1)}, u32[]{:S(2)}, u32[]{:S(2)}) collective-permute-start(bf16[256,896]{1,0:T(8,128)(2,1)} %copy-done.20), channel_id=1, source_target_pairs={{0,8},{8,16},{16,24},{24,28},{28,20},{20,12},{12,4},{4,0},{1,9},{9... | collective-permute-start | bytes 1376264 | tf_op jit(solution)/shard_map/ppermute | solution.py:586
  118.2 29.2 %collective-permute-start.22 = (bf16[256,1024]{1,0:T(8,128)(2,1)}, bf16[256,1024]{1,0:T(8,128)(2,1)}, u32[]{:S(2)}, u32[]{:S(2)}) collective-permute-start(bf16[256,1024]{1,0:T(8,128)(2,1)} %collective-permute-done.17.refs_16_.refs_24_), channel_id=1, source_target_pairs={{0,8},{8,16},{16,24},{24,28},{28,20},{20,12},{12,4},{4,0},{1,9},{9... | collective-permute-start | bytes 1572872 | tf_op jit(solution)/shard_map/ppermute | solution.py:586
  121.8 25.6 %collective-permute-start.23 = (bf16[256,1024]{1,0:T(8,128)(2,1)}, bf16[256,1024]{1,0:T(8,128)(2,1)}, u32[]{:S(2)}, u32[]{:S(2)}) collective-permute-start(bf16[256,1024]{1,0:T(8,128)(2,1)} %collective-permute-done.18.refs_10_.refs_18_), channel_id=1, source_target_pairs={{8,0},{16,8},{24,16},{28,24},{20,28},{12,20},{4,12},{0,4},{9,1},{1... | collective-permute-start | bytes 1572872 | tf_op jit(solution)/shard_map/ppermute | solution.py:590
  147.4 26.7 %collective-permute-start.27 = (bf16[256,1024]{1,0:T(8,128)(2,1)}, bf16[256,1024]{1,0:T(8,128)(2,1)}, u32[]{:S(2)}, u32[]{:S(2)}) collective-permute-start(bf16[256,1024]{1,0:T(8,128)(2,1)} %collective-permute-done.22.refs_15_.refs_23_), channel_id=1, source_target_pairs={{0,8},{8,16},{16,24},{24,28},{28,20},{20,12},{12,4},{4,0},{1,9},{9... | collective-permute-start | bytes 1572872 | tf_op jit(solution)/shard_map/ppermute | solution.py:586
  184.8 30.5 %collective-permute-start.38 = (bf16[256,1408]{1,0:T(8,128)(2,1)S(1)}, bf16[256,1408]{1,0:T(8,128)(2,1)S(1)}, u32[]{:S(2)}, u32[]{:S(2)}) collective-permute-start(bf16[256,1408]{1,0:T(8,128)(2,1)S(1)} %get-tuple-element.313.refs_1_.refs_4_.refs_5_.refs_6_), channel_id=1, source_target_pairs={{0,8},{8,16},{16,24},{24,28},{28,20},{20,12},{12,4},{4,0},{1,9},{9... | collective-permute-start | bytes 2162696 | tf_op jit(solution)/shard_map/ppermute | solution.py:586
  189.9 25.4 %collective-permute-start.39 = (bf16[256,1408]{1,0:T(8,128)(2,1)S(1)}, bf16[256,1408]{1,0:T(8,128)(2,1)S(1)}, u32[]{:S(2)}, u32[]{:S(2)}) collective-permute-start(bf16[256,1408]{1,0:T(8,128)(2,1)S(1)} %get-tuple-element.313.refs_1_.refs_4_.refs_5_.refs_6_), channel_id=1, source_target_pairs={{8,0},{16,8},{24,16},{28,24},{20,28},{12,20},{4,12},{0,4},{9,1},{1... | collective-permute-start | bytes 2162696 | tf_op jit(solution)/shard_map/ppermute | solution.py:590
  241.2 24.5 %collective-permute-start.43 = (bf16[256,2048]{1,0:T(8,128)(2,1)S(1)}, bf16[256,2048]{1,0:T(8,128)(2,1)S(1)}, u32[]{:S(2)}, u32[]{:S(2)}) collective-permute-start(bf16[256,2048]{1,0:T(8,128)(2,1)S(1)} %convert_element_type.541), channel_id=1, source_target_pairs={{0,2},{1,3},{2,0},{3,1},{4,6},{5,7},{6,4},{7,5},{8,10},{9,11},{10,... | collective-permute-start | bytes 3145736 | tf_op jit(solution)/shard_map/ppermute | solution.py:913
  245.4 30.3 %collective-permute-start.46 = (bf16[256,1408]{1,0:T(8,128)(2,1)S(1)}, bf16[256,1408]{1,0:T(8,128)(2,1)}, u32[]{:S(2)}, u32[]{:S(2)}) collective-permute-start(bf16[256,1408]{1,0:T(8,128)(2,1)S(1)} %copy-done.137), channel_id=1, source_target_pairs={{0,8},{8,16},{16,24},{24,28},{28,20},{20,12},{12,4},{4,0},{1,9},{9... | collective-permute-start | bytes 2162696 | tf_op jit(solution)/shard_map/ppermute | solution.py:586
  245.7 30.3 %collective-permute-start.47 = (bf16[256,1408]{1,0:T(8,128)(2,1)S(1)}, bf16[256,1408]{1,0:T(8,128)(2,1)}, u32[]{:S(2)}, u32[]{:S(2)}) collective-permute-start(bf16[256,1408]{1,0:T(8,128)(2,1)S(1)} %copy-done.18), channel_id=1, source_target_pairs={{8,0},{16,8},{24,16},{28,24},{20,28},{12,20},{4,12},{0,4},{9,1},{1... | collective-permute-start | bytes 2162696 | tf_op jit(solution)/shard_map/ppermute | solution.py:590
  278.0 32.7 %collective-permute-start.44 = (bf16[256,1408]{1,0:T(8,128)(2,1)}, bf16[256,1408]{1,0:T(8,128)(2,1)S(1)}, u32[]{:S(2)}, u32[]{:S(2)}) collective-permute-start(bf16[256,1408]{1,0:T(8,128)(2,1)} %copy-done.138), channel_id=1, source_target_pairs={{0,8},{8,16},{16,24},{24,28},{28,20},{20,12},{12,4},{4,0},{1,9},{9... | collective-permute-start | bytes 2162696 | tf_op jit(solution)/shard_map/ppermute | solution.py:586
  278.4 32.3 %collective-permute-start.45 = (bf16[256,1408]{1,0:T(8,128)(2,1)}, bf16[256,1408]{1,0:T(8,128)(2,1)S(1)}, u32[]{:S(2)}, u32[]{:S(2)}) collective-permute-start(bf16[256,1408]{1,0:T(8,128)(2,1)} %copy-done.139), channel_id=1, source_target_pairs={{8,0},{16,8},{24,16},{28,24},{20,28},{12,20},{4,12},{0,4},{9,1},{1... | collective-permute-start | bytes 2162696 | tf_op jit(solution)/shard_map/ppermute | solution.py:590
  295.7 27.7 %collective-permute-start.51 = (bf16[256,1408]{1,0:T(8,128)(2,1)S(1)}, bf16[256,1408]{1,0:T(8,128)(2,1)S(1)}, u32[]{:S(2)}, u32[]{:S(2)}) collective-permute-start(bf16[256,1408]{1,0:T(8,128)(2,1)S(1)} %collective-permute-done.48.refs_2_), channel_id=1, source_target_pairs={{0,8},{8,16},{16,24},{24,28},{28,20},{20,12},{12,4},{4,0},{1,9},{9... | collective-permute-start | bytes 2162696 | tf_op jit(solution)/shard_map/ppermute | solution.py:586
  370.1 30.5 %collective-permute-start.61 = (bf16[256,1408]{1,0:T(8,128)(2,1)S(1)}, bf16[256,1408]{1,0:T(8,128)(2,1)S(1)}, u32[]{:S(2)}, u32[]{:S(2)}) collective-permute-start(bf16[256,1408]{1,0:T(8,128)(2,1)S(1)} %get-tuple-element.604), channel_id=1, source_target_pairs={{0,8},{8,16},{16,24},{24,28},{28,20},{20,12},{12,4},{4,0},{1,9},{9... | collective-permute-start | bytes 2162696 | tf_op jit(solution)/shard_map/ppermute | solution.py:586
  370.5 30.3 %collective-permute-start.62 = (bf16[256,1408]{1,0:T(8,128)(2,1)S(1)}, bf16[256,1408]{1,0:T(8,128)(2,1)S(1)}, u32[]{:S(2)}, u32[]{:S(2)}) collective-permute-start(bf16[256,1408]{1,0:T(8,128)(2,1)S(1)} %get-tuple-element.603), channel_id=1, source_target_pairs={{8,0},{16,8},{24,16},{28,24},{20,28},{12,20},{4,12},{0,4},{9,1},{1... | collective-permute-start | bytes 2162696 | tf_op jit(solution)/shard_map/ppermute | solution.py:590
  387.1 28.9 %collective-permute-start.58 = (bf16[256,1408]{1,0:T(8,128)(2,1)S(1)}, bf16[256,1408]{1,0:T(8,128)(2,1)S(1)}, u32[]{:S(2)}, u32[]{:S(2)}) collective-permute-start(bf16[256,1408]{1,0:T(8,128)(2,1)S(1)} %get-tuple-element.606), channel_id=1, source_target_pairs={{0,8},{8,16},{16,24},{24,28},{28,20},{20,12},{12,4},{4,0},{1,9},{9... | collective-permute-start | bytes 2162696 | tf_op jit(solution)/shard_map/ppermute | solution.py:586
  387.8 28.4 %collective-permute-start.59 = (bf16[256,1408]{1,0:T(8,128)(2,1)S(1)}, bf16[256,1408]{1,0:T(8,128)(2,1)S(1)}, u32[]{:S(2)}, u32[]{:S(2)}) collective-permute-start(bf16[256,1408]{1,0:T(8,128)(2,1)S(1)} %get-tuple-element.605), channel_id=1, source_target_pairs={{8,0},{16,8},{24,16},{28,24},{20,28},{12,20},{4,12},{0,4},{9,1},{1... | collective-permute-start | bytes 2162696 | tf_op jit(solution)/shard_map/ppermute | solution.py:590
  389.3 26.9 %collective-permute-start.60 = (bf16[256,2048]{1,0:T(8,128)(2,1)S(1)}, bf16[256,2048]{1,0:T(8,128)(2,1)S(1)}, u32[]{:S(2)}, u32[]{:S(2)}) collective-permute-start(bf16[256,2048]{1,0:T(8,128)(2,1)S(1)} %convert_element_type.558), channel_id=1, source_target_pairs={{0,2},{1,3},{2,0},{3,1},{4,6},{5,7},{6,4},{7,5},{8,10},{9,11},{10,... | collective-permute-start | bytes 3145736 | tf_op jit(solution)/shard_map/ppermute | solution.py:913
  402.5 29.0 %collective-permute-start.65 = (bf16[256,1408]{1,0:T(8,128)(2,1)S(1)}, bf16[256,1408]{1,0:T(8,128)(2,1)S(1)}, u32[]{:S(2)}, u32[]{:S(2)}) collective-permute-start(bf16[256,1408]{1,0:T(8,128)(2,1)S(1)} %get-tuple-element.600), channel_id=1, source_target_pairs={{0,8},{8,16},{16,24},{24,28},{28,20},{20,12},{12,4},{4,0},{1,9},{9... | collective-permute-start | bytes 2162696 | tf_op jit(solution)/shard_map/ppermute | solution.py:586
  403.2 28.5 %collective-permute-start.66 = (bf16[256,1408]{1,0:T(8,128)(2,1)S(1)}, bf16[256,1408]{1,0:T(8,128)(2,1)S(1)}, u32[]{:S(2)}, u32[]{:S(2)}) collective-permute-start(bf16[256,1408]{1,0:T(8,128)(2,1)S(1)} %get-tuple-element.599), channel_id=1, source_target_pairs={{8,0},{16,8},{24,16},{28,24},{20,28},{12,20},{4,12},{0,4},{9,1},{1... | collective-permute-start | bytes 2162696 | tf_op jit(solution)/shard_map/ppermute | solution.py:590
  485.4 32.1 %collective-permute-start.74 = (bf16[256,1024]{0,1:T(8,128)(2,1)S(1)}, bf16[256,1024]{0,1:T(8,128)(2,1)S(1)}, u32[]{:S(2)}, u32[]{:S(2)}) collective-permute-start(bf16[256,1024]{0,1:T(8,128)(2,1)S(1)} %get-tuple-element.389), channel_id=1, source_target_pairs={{0,8},{8,16},{16,24},{24,28},{28,20},{20,12},{12,4},{4,0},{1,9},{9... | collective-permute-start | bytes 1572872 | tf_op jit(solution)/shard_map/ppermute | solution.py:586
  488.7 28.8 %collective-permute-start.75 = (bf16[256,1024]{0,1:T(8,128)(2,1)S(1)}, bf16[256,1024]{0,1:T(8,128)(2,1)S(1)}, u32[]{:S(2)}, u32[]{:S(2)}) collective-permute-start(bf16[256,1024]{0,1:T(8,128)(2,1)S(1)} %get-tuple-element.390), channel_id=1, source_target_pairs={{8,0},{16,8},{24,16},{28,24},{20,28},{12,20},{4,12},{0,4},{9,1},{1... | collective-permute-start | bytes 1572872 | tf_op jit(solution)/shard_map/ppermute | solution.py:590
  519.6 27.8 %collective-permute-start.80 = (bf16[256,1024]{0,1:T(8,128)(2,1)}, bf16[256,1024]{0,1:T(8,128)(2,1)}, u32[]{:S(2)}, u32[]{:S(2)}) collective-permute-start(bf16[256,1024]{0,1:T(8,128)(2,1)} %get-tuple-element.626), channel_id=1, source_target_pairs={{0,8},{8,16},{16,24},{24,28},{28,20},{20,12},{12,4},{4,0},{1,9},{9... | collective-permute-start | bytes 1572872 | tf_op jit(solution)/shard_map/ppermute | solution.py:586
  519.6 27.8 %collective-permute-start.81 = (bf16[256,1024]{0,1:T(8,128)(2,1)}, bf16[256,1024]{0,1:T(8,128)(2,1)}, u32[]{:S(2)}, u32[]{:S(2)}) collective-permute-start(bf16[256,1024]{0,1:T(8,128)(2,1)} %get-tuple-element.625), channel_id=1, source_target_pairs={{8,0},{16,8},{24,16},{28,24},{20,28},{12,20},{4,12},{0,4},{9,1},{1... | collective-permute-start | bytes 1572872 | tf_op jit(solution)/shard_map/ppermute | solution.py:590
  550.4 31.9 %collective-permute-start.88 = (bf16[256,1024]{0,1:T(8,128)(2,1)S(1)}, bf16[256,1024]{0,1:T(8,128)(2,1)S(1)}, u32[]{:S(2)}, u32[]{:S(2)}) collective-permute-start(bf16[256,1024]{0,1:T(8,128)(2,1)S(1)} %get-tuple-element.624), channel_id=1, source_target_pairs={{0,8},{8,16},{16,24},{24,28},{28,20},{20,12},{12,4},{4,0},{1,9},{9... | collective-permute-start | bytes 1572872 | tf_op jit(solution)/shard_map/ppermute | solution.py:586
  553.7 28.5 %collective-permute-start.89 = (bf16[256,1024]{0,1:T(8,128)(2,1)S(1)}, bf16[256,1024]{0,1:T(8,128)(2,1)S(1)}, u32[]{:S(2)}, u32[]{:S(2)}) collective-permute-start(bf16[256,1024]{0,1:T(8,128)(2,1)S(1)} %get-tuple-element.623), channel_id=1, source_target_pairs={{8,0},{16,8},{24,16},{28,24},{20,28},{12,20},{4,12},{0,4},{9,1},{1... | collective-permute-start | bytes 1572872 | tf_op jit(solution)/shard_map/ppermute | solution.py:590
  575.4 34.7 %collective-permute-start.96 = (bf16[256,1024]{1,0:T(8,128)(2,1)}, bf16[256,1024]{1,0:T(8,128)(2,1)}, u32[]{:S(2)}, u32[]{:S(2)}) collective-permute-start(bf16[256,1024]{1,0:T(8,128)(2,1)} %get-tuple-element.435), channel_id=1, source_target_pairs={{0,8},{8,16},{16,24},{24,28},{28,20},{20,12},{12,4},{4,0},{1,9},{9... | collective-permute-start | bytes 1572872 | tf_op jit(solution)/shard_map/ppermute | solution.py:586
  576.7 33.4 %collective-permute-start.97 = (bf16[256,1024]{1,0:T(8,128)(2,1)}, bf16[256,1024]{1,0:T(8,128)(2,1)}, u32[]{:S(2)}, u32[]{:S(2)}) collective-permute-start(bf16[256,1024]{1,0:T(8,128)(2,1)} %get-tuple-element.436), channel_id=1, source_target_pairs={{8,0},{16,8},{24,16},{28,24},{20,28},{12,20},{4,12},{0,4},{9,1},{1... | collective-permute-start | bytes 1572872 | tf_op jit(solution)/shard_map/ppermute | solution.py:590
  610.4 25.0 %collective-permute-start.101 = (bf16[256,2048]{1,0:T(8,128)(2,1)S(1)}, bf16[256,2048]{1,0:T(8,128)(2,1)S(1)}, u32[]{:S(2)}, u32[]{:S(2)}) collective-permute-start(bf16[256,2048]{1,0:T(8,128)(2,1)S(1)} %convert_element_type.648), channel_id=1, source_target_pairs={{0,2},{1,3},{2,0},{3,1},{4,6},{5,7},{6,4},{7,5},{8,10},{9,11},{10,... | collective-permute-start | bytes 3145736 | tf_op jit(solution)/shard_map/ppermute | solution.py:913
  623.0 24.9 %collective-permute-start.94 = (bf16[256,1024]{1,0:T(8,128)(2,1)S(1)}, bf16[256,1024]{1,0:T(8,128)(2,1)S(1)}, u32[]{:S(2)}, u32[]{:S(2)}) collective-permute-start(bf16[256,1024]{1,0:T(8,128)(2,1)S(1)} %get-tuple-element.618), channel_id=1, source_target_pairs={{0,8},{8,16},{16,24},{24,28},{28,20},{20,12},{12,4},{4,0},{1,9},{9... | collective-permute-start | bytes 1572872 | tf_op jit(solution)/shard_map/ppermute | solution.py:586
  (237 other events, 2660.6 us)

commit v3 on v2

--- a/solution.py
+++ b/solution.py
@@ -424,7 +424,7 @@
         dlogit_ref[...] += grad_logit
 
 
-HEADS_AT_ONCE = 2
+HEADS_AT_ONCE = 4
 
 
 def _specs(heads, rows):
@@ -457,9 +457,9 @@
     )
 
 
-def _params():
+def _params(mebibytes=48):
     return pltpu.CompilerParams(
-        dimension_semantics=("arbitrary",), vmem_limit_bytes=48 * 1024 * 1024
+        dimension_semantics=("arbitrary",), vmem_limit_bytes=mebibytes * 1024 * 1024
     )
 
 
@@ -485,8 +485,8 @@
             jax.ShapeDtypeStruct((total, DK, DK), jnp.bfloat16),
         ],
         scratch_shapes=[pltpu.VMEM((3 * heads, rows + 8, DK), jnp.float32)],
-        compiler_params=_params(),
-        cost_estimate=_cost(11),
+        compiler_params=_params(60),
+        cost_estimate=_cost(8),
         name="delta_local",
     )(scal, *pre, halo, halo, halo, taps, logits)
 
@@ -508,8 +508,8 @@
             low,
             jax.ShapeDtypeStruct((total, rows // SPAN, DK, DK), jnp.bfloat16),
         ],
-        compiler_params=_params(),
-        cost_estimate=_cost(7),
+        compiler_params=_params(60),
+        cost_estimate=_cost(5),
         name="delta_apply",
     )(scal, q, k, w, uv, state_in, gate, gain)
 
@@ -533,7 +533,7 @@
             jax.ShapeDtypeStruct((total, DK, DK), jnp.float32),
         ],
         compiler_params=_params(),
-        cost_estimate=_cost(9),
+        cost_estimate=_cost(8),
         name="delta_back_local",
     )(scal, dn, gate, gain, o, q, k, w)
 
@@ -566,7 +566,7 @@
             pltpu.VMEM((3 * heads, rows + 16, DK), jnp.float32),
         ],
         compiler_params=_params(),
-        cost_estimate=_cost(17),
+        cost_estimate=_cost(15),
         name="delta_back",
     )(
         scal, *pre, halo, halo, halo, taps, logits, q, k, w, t, u, s, do, p, above
@@ -742,23 +742,34 @@
 
 
 class Flow:
-    def __init__(self):
+    def __init__(self, token):
         self.flying = []
+        self.token = token
 
     def step(self, ring, stage, values=()):
         each = lax.axis_size("seq") // 8
         for slot in range(stage * each, (stage + 1) * each):
-            keys = self.flying.pop(0) if len(self.flying) > 1 else []
-            arrived = [held[key] for held, key in keys]
             fresh = ring.fresh(slot)
-            arrived, first, values = lax.optimization_barrier(
-                (arrived, [held[0] for held in fresh], values)
+            new = 1 if slot // 2 == ring.half - 1 else 2
+            keys = []
+            while self.flying and (
+                sum(len(sent) for _, _, sent in self.flying) + new > 4
+                or any(other is ring and was <= slot - 2 for other, was, _ in self.flying)
+            ):
+                keys += self.flying.pop(0)[2]
+            arrived, first, values, self.token = lax.optimization_barrier(
+                (
+                    [held[key] for held, key in keys],
+                    [held[0] for held in fresh],
+                    values,
+                    self.token,
+                )
             )
             for held, value in zip(fresh, first):
                 held[0] = value
             for (held, key), value in zip(keys, arrived):
                 held[key] = value
-            self.flying.append(ring.send(slot))
+            self.flying.append((ring, slot, ring.send(slot)))
         return values
 
 
@@ -807,7 +818,7 @@
         out_specs=[vmem] * (len(shapes) + len(whole)),
         out_shape=list(shapes) + whole,
         scratch_shapes=[pltpu.SemaphoreType.DMA((len(operands), count))],
-        compiler_params=pltpu.CompilerParams(vmem_limit_bytes=48 * 1024 * 1024),
+        compiler_params=pltpu.CompilerParams(vmem_limit_bytes=60 * 1024 * 1024),
         cost_estimate=_cost(12),
         name="rows_dot",
     )(value, *[pieces[place] for pieces, _, _ in operands for place in range(count)])
@@ -855,7 +866,7 @@
         out_shape=[jax.ShapeDtypeStruct((value.shape[0], columns), jnp.float32)] * 2
         + [jax.ShapeDtypeStruct((value.shape[1], columns), jnp.bfloat16)] * 2,
         scratch_shapes=[pltpu.SemaphoreType.DMA((2, count))],
-        compiler_params=pltpu.CompilerParams(vmem_limit_bytes=52 * 1024 * 1024),
+        compiler_params=pltpu.CompilerParams(vmem_limit_bytes=60 * 1024 * 1024),
         cost_estimate=_cost(14),
         name="glu_early",
     )(
@@ -922,13 +933,6 @@
     )
 
 
-def scatter_round(held, bit):
-    low_rows, high_rows = held[: held.shape[0] // 2], held[held.shape[0] // 2 :]
-    upper = (lax.axis_index("seq") & bit) != 0
-    got = swap(jnp.where(upper, low_rows, high_rows), "seq", bit)
-    return jnp.where(upper, high_rows, low_rows) + got
-
-
 def bits_of(axis):
     return [1 << bit for bit in range(lax.axis_size(axis).bit_length() - 1)]
 
@@ -957,6 +961,15 @@
         other_half(low(partial_rows)), "head", 1
     ).astype(jnp.float32)
     return pair
+
+
+def summed_over_head(value):
+    if lax.axis_size("head") == 4:
+        one, two, three = (swap(value, "head", bits) for bits in (1, 2, 3))
+        return (value + one) + (two + three)
+    for bit in bits_of("head"):
+        value = value + swap(value, "head", bit)
+    return value
 
 
 def asked(total):
@@ -1039,7 +1052,7 @@
     shard = proj_master.shape[1]
     heads = width // DK
     scal = jnp.stack([lengths[0] - seq_index * rows, seq_index * rows]).astype(jnp.int32)
-    flow = Flow()
+    flow = Flow(lengths)
     sizes = [conv_master.size, beta_master.size, gains_master.size]
     packed = low(
         jnp.concatenate(
@@ -1158,7 +1171,7 @@
     )
     sums, w_mlp_g, w_mlp_u, h_two = flow.step(ring_m, 7, (sums, w_mlp_g, w_mlp_u, h_two))
     late = (half - 1, half, half + 1)
-    shard = gates[half].shape[0]
+    shard = proj_master.shape[1]
     act_low, grad_gate_u, grad_up_u = glu_late(
         h_two[:, late[0] * shard : (late[-1] + 1) * shard],
         [gates[one] for one in late],
@@ -1166,18 +1179,20 @@
         sums,
         grad_act,
     )
+    def rows_of(value):
+        piece = value.shape[0] // count
+        return lambda one: value[one * piece : (one + 1) * piece]
+
+    back_m = Scatter(
+        rows_of(low(dot_tn(h_two, grad_gate_u))), rows_of(low(dot_tn(h_two, grad_up_u)))
+    )
+    flow.step(back_m, 0)
+    grad_gate_u, grad_up_u, act_low, w_mlp_g, w_mlp_u = flow.step(
+        back_m, 1, (grad_gate_u, grad_up_u, act_low, w_mlp_g, w_mlp_u)
+    )
     for one in late:
         w_mlp_g = lax.dynamic_update_slice_in_dim(w_mlp_g, gates[one], one * shard, 0)
         w_mlp_u = lax.dynamic_update_slice_in_dim(w_mlp_u, ups[one], one * shard, 0)
-    def rows_of(value):
-        piece = value.shape[0] // count
-        return lambda one: value[one * piece : (one + 1) * piece]
-
-    back_m = Scatter(
-        rows_of(low(dot_tn(h_two, grad_gate_u))), rows_of(low(dot_tn(h_two, grad_up_u)))
-    )
-    flow.step(back_m, 0)
-    grad_gate_u, grad_up_u, act_low = flow.step(back_m, 1, (grad_gate_u, grad_up_u, act_low))
     part = low(dot_nt(grad_gate_u, w_mlp_g) + dot_nt(grad_up_u, w_mlp_u))
     part = flow.step(back_m, 2, part)
     pair, act_low = flow.step(back_m, 3, (summed_pair(part), act_low))
@@ -1198,8 +1213,9 @@
     grad_gate, grad_gain_o, grad_out, through, carry = delta_back_local(
         scal, grad_normed, gate, gain_o, out_rows, q, k, w
     )
-    grad_gate, carry, act_low = flow.step(back_m, 7, (grad_gate, carry, act_low))
-    above = passed_along(low(carry), -1)
+    grad_gate, carry, grad_attn, act_low = flow.step(
+        back_m, 7, (grad_gate, carry, grad_attn, act_low)
+    )
     grad_do_a = low(dot_tn(dy_ring, act_low[:, :cut]))
     grad_do_b = jnp.concatenate(
         [low(dot_tn(dy_ring, act_low[:, cut:])), low(dot_tn(grad_attn, normed))], axis=1
@@ -1210,71 +1226,78 @@
         moved = jnp.einsum("hji,hjk->hik", state_map, state, preferred_element_type=f32)
         return passed_along(low(moved + carry), -1)
 
-    above = flow.step(back_do, 0, above)
-    for _ in range(third):
-        above = hop_back(above)
+    grad_gate, carry = flow.step(back_do, 0, (grad_gate, carry))
+    above = passed_along(low(carry), -1)
     above, mlp_parts = flow.step(back_do, 1, (above, mlp_parts))
     for _ in range(third):
         above = hop_back(above)
     above = flow.step(back_do, 2, above)
+    for _ in range(third):
+        above = hop_back(above)
+    above = flow.step(back_do, 3, above)
     for _ in range(hops - 1 - 2 * third):
         above = hop_back(above)
-    above = flow.step(back_do, 3, above)
+    above, mlp_sum = flow.step(back_do, 4, (above, summed(mlp_parts)))
     grad_pre, tail, back_halo, grad_taps, grad_logits = delta_back(
         scal, pre, halo, taps, logits, q, k, w, t, change, states, grad_out, through, above
     )
-    mlp_sum = flow.step(back_do, 4, summed(mlp_parts))
-    result = join_columns(x_one + mlp_sum, targets)
-    grad_pre, back_halo, tail, grad_logits, result = flow.step(
-        back_do, 5, (grad_pre, back_halo, tail, grad_logits, result)
-    )
     fixed = low(tail + passed_along(back_halo, -1))
+    grad_logits = low(grad_logits)
     grad_pre = lax.dynamic_update_slice_in_dim(grad_pre, fixed, rows - 8, 1)
     grad_qk = jnp.concatenate([grad_pre[0], grad_pre[1]], axis=1)
     grad_vg = jnp.concatenate([grad_pre[2], grad_gate], axis=1)
-    grad_qk, grad_vg = flow.step(back_do, 6, (grad_qk, grad_vg))
-    back_p = Scatter(
-        rows_of(low(dot_tn(hidden, grad_qk))), rows_of(low(dot_tn(hidden, grad_vg)))
-    )
-    flow.step(back_do, 7)
-    grad_qk, grad_vg, grad_logits = flow.step(back_p, 0, (grad_qk, grad_vg, grad_logits))
-    grad_logits = low(grad_logits)
+    grad_w_qk = low(dot_tn(hidden, grad_qk))
+    grad_w_qk, grad_qk, grad_vg, grad_logits, grad_taps = flow.step(
+        back_do, 5, (grad_w_qk, grad_qk, grad_vg, grad_logits, grad_taps)
+    )
+    grad_beta = dot_tn(grad_logits, hidden)
+    grad_conv = jnp.transpose(
+        grad_taps.reshape(3, CONV, count, width // count), (2, 0, 1, 3)
+    ).reshape(count, -1)
     grad_hidden = low(
         dot_nt(grad_qk, w_qk) + dot_nt(grad_vg, w_vg) + dot(grad_logits, w_beta)
     )
-    grad_beta = dot_tn(grad_logits, hidden)
-    grad_hidden, grad_beta = flow.step(back_p, 1, (grad_hidden, grad_beta))
-    pair = summed_pair(grad_hidden)
     grad_gain_a = jnp.sum(grad_hidden.astype(f32) * x_rows * x_inv, axis=0, keepdims=True)
+    grad_hidden, grad_gain_a, grad_vg = flow.step(
+        back_do, 6, (grad_hidden, grad_gain_a, grad_vg)
+    )
     stacked = jnp.concatenate([grad_gain_a, grad_gain_m, grad_beta], axis=0)
     stacked = jnp.take(stacked.reshape(2 + heads, count, -1), targets, axis=1).reshape(-1, D)
     grad_gains = jnp.concatenate(
         [stacked[:2].reshape(-1), jnp.sum(grad_gain_o[:, 0], axis=0)]
     ).reshape(count, -1)
-    grad_conv = jnp.transpose(
-        grad_taps.reshape(3, CONV, count, width // count), (2, 0, 1, 3)
-    ).reshape(count, -1)
     grad_beta = jnp.transpose(stacked[2:]).reshape(count, -1)
-    small_sum = jnp.concatenate([grad_conv, grad_beta, grad_gains], axis=1)
-    small_sum, pair = flow.step(back_p, 2, (small_sum, pair))
+    small = jnp.stack(
+        [
+            jnp.pad(low(one), ((0, 0), (0, 2 * width - one.shape[1])))
+            for one in (grad_conv, grad_beta, grad_gains)
+        ],
+        axis=1,
+    )
+    small = jnp.pad(jnp.take(small, sources, axis=0), ((0, 0), (0, 13), (0, 0)))
+    grad_w_vg = low(dot_tn(hidden, grad_vg)).reshape(count, -1, 2 * width)
+    grad_w_vg = jnp.concatenate([grad_w_vg, small], axis=1)
+    grad_w_vg = flow.step(back_do, 7, grad_w_vg)
+    back_p = Scatter(rows_of(grad_w_qk), lambda one: grad_w_vg[one])
+    flow.step(back_p, 0)
+    flow.step(back_p, 1)
+    grad_hidden, mlp_master, mlp_sum = flow.step(
+        back_p, 2, (grad_hidden, mlp_master, mlp_sum)
+    )
+    pair = summed_pair(grad_hidden)
+    result = join_columns(x_one + mlp_sum, targets)
+    pair, result, down_master, out_master = flow.step(
+        back_p, 3, (pair, result, down_master, out_master)
+    )
     parts = asked(pair)
-    flow.step(back_p, 3)
-    small_sum, parts = flow.step(back_p, 4, (small_sum, parts))
-    small_sum = scatter_round(small_sum, seq_bits[-1])
     mlp_g_sum, mlp_u_sum = back_m.sums()
     mlp_new, mlp_first_new, mlp_second_new = adam_update(
         mlp_master, mlp_first, mlp_second, jnp.stack([mlp_g_sum, mlp_u_sum]),
         rate_matrix, decay_matrix,
     )
-    small_sum, mlp_new, mlp_first_new, mlp_second_new = flow.step(
-        back_p, 5, (small_sum, mlp_new, mlp_first_new, mlp_second_new)
-    )
-    for bit in seq_bits[-2:0:-1]:
-        small_sum = scatter_round(small_sum, bit)
-    grad_x_rest = norm_back(own_half(x_rows), own_half(x_inv), gain_a, summed(parts))
-    input_half = grad_x_one + grad_x_rest
-    small_sum, input_half = flow.step(back_p, 6, (small_sum, input_half))
-    small_sum = scatter_round(small_sum, seq_bits[0])[0]
+    mlp_new, mlp_first_new, mlp_second_new = flow.step(
+        back_p, 4, (mlp_new, mlp_first_new, mlp_second_new)
+    )
     do_a_sum, do_b_sum = back_do.sums()
     summed_down = jnp.transpose(jnp.concatenate([do_a_sum, do_b_sum[:, :rest]], axis=1))
     out_sum = jnp.transpose(do_b_sum[:, rest:])
@@ -1284,16 +1307,22 @@
     out_new, out_first_new, out_second_new = adam_update(
         out_master, out_first, out_second, out_sum, rate_matrix, decay_matrix
     )
-    input_grad = join_columns(input_half, targets)
-    small_sum, input_grad, down_new, down_first_new, down_second_new = flow.step(
-        back_p, 7, (small_sum, input_grad, down_new, down_first_new, down_second_new)
-    )
-    gains_sum = small_sum[sizes[0] + sizes[1] :]
-    for bit in bits_of("head"):
-        gains_sum = gains_sum + swap(gains_sum, "head", bit)
-    summed_conv = small_sum[: sizes[0]].reshape(conv_master.shape)
-    summed_beta = small_sum[sizes[0] : sizes[0] + sizes[1]].reshape(beta_master.shape)
+    parts, down_new, down_first_new, down_second_new = flow.step(
+        back_p, 5, (parts, down_new, down_first_new, down_second_new)
+    )
+    grad_x_rest = norm_back(own_half(x_rows), own_half(x_inv), gain_a, summed(parts))
+    input_half = grad_x_one + grad_x_rest
+    input_half, out_new, out_first_new, out_second_new = flow.step(
+        back_p, 6, (input_half, out_new, out_first_new, out_second_new)
+    )
+    input_grad = flow.step(back_p, 7, join_columns(input_half, targets))
     qk_sum, vg_sum = back_p.sums()
+    small_sum = [vg_sum[shard + one, : sizes[one]] for one in range(3)]
+    vg_sum = vg_sum[:shard]
+    gains_sum = small_sum[2]
+    gains_sum = summed_over_head(gains_sum)
+    summed_conv = small_sum[0].reshape(conv_master.shape)
+    summed_beta = small_sum[1].reshape(beta_master.shape)
     summed_proj = jnp.stack(
         [qk_sum[:, :width], qk_sum[:, width:], vg_sum[:, :width], vg_sum[:, width:]]
     )

time: 716 us -> 688 us (0.961)
  waiting for transfers between devices: 277 us -> 251 us
  local copies, waits for them, and re-layouts: 66.2 us -> 49 us
  matrix products: 43.1 us -> 55.5 us
  other arithmetic: 76.8 us -> 85 us
  Pallas kernels: 96.6 us -> 89.2 us
    unnamed x309 -> x273, local copies, waits for them, and re-layouts: 39.6 us -> 19.3 us
    ppermute x42, starting transfers between devices: 43.5 us -> 30.2 us  [send_down(): lax.ppermute(value, 'seq', [(b, a) for a, b in ring_pairs(lax.axis_size('...]
    ppermute x10, waiting for transfers between devices: 47.8 us -> 35.4 us  [passed_along(): lax.ppermute(value, 'seq', [(source, source + steps) for source in range(...]
    ppermute x42, waiting for transfers between devices: 145 us -> 134 us  [send_up(): return lax.ppermute(value, 'seq', ring_pairs(lax.axis_size('seq')))]
    ppermute x42, starting transfers between devices: 64.8 us -> 75.8 us  [send_up(): return lax.ppermute(value, 'seq', ring_pairs(lax.axis_size('seq')))]
    ppermute x20 -> x18, waiting for transfers between devices: 34.9 us -> 29.3 us  [swap(): return lax.ppermute(value, axis, [(one, one ^ bit) for one in range(count)])]
    convert_element_type x28 -> x30, other arithmetic: 27.8 us -> 29.3 us  [low(): return value.astype(jnp.bfloat16)]
  transfers between devices with their start and end apart: 114 -> 112, of which waited for: 53 -> 53; matrix products, arithmetic and copies ran while one was open for 16% -> 21% of each run, Pallas kernels for 13% -> 12%
where the time goes in v3:
time: 688 us; the launch traced here: 678 us
  waiting for transfers between devices  251 us (36%)
  starting transfers between devices  145 us (21%)
  Pallas kernels  89.2 us (13%)
  other arithmetic  85 us (12%)
  matrix products  55.5 us (8%)
  local copies, waits for them, and re-layouts  49 us (7%)
    ppermute x42, waiting for transfers between devices, send_up(): return lax.ppermute(value, 'seq', ring_pairs(lax.axis_size('seq')))  134 us
    ppermute x42, starting transfers between devices, send_up(): return lax.ppermute(value, 'seq', ring_pairs(lax.axis_size('seq')))  75.8 us
    ppermute x42, waiting for transfers between devices, send_down(): lax.ppermute(value, 'seq', [(b, a) for a, b in ring_pairs(lax.axis_size('...  52.2 us
    ppermute x10, waiting for transfers between devices, passed_along(): lax.ppermute(value, 'seq', [(source, source + steps) for source in range(...  35.4 us
    ppermute x42, starting transfers between devices, send_down(): lax.ppermute(value, 'seq', [(b, a) for a, b in ring_pairs(lax.axis_size('...  30.2 us
    ppermute x18, waiting for transfers between devices, swap(): return lax.ppermute(value, axis, [(one, one ^ bit) for one in range(count)])  29.3 us
    convert_element_type x30, other arithmetic, low(): return value.astype(jnp.bfloat16)  29.3 us
    ppermute x10, starting transfers between devices, passed_along(): lax.ppermute(value, 'seq', [(source, source + steps) for source in range(...  25.7 us
  transfers between devices with their start and end apart: 112, of which 53 were waited for; matrix products, arithmetic and copies ran while one was open for 21% of the time, Pallas kernels for 12%

profile of v3, /device:TPU:0, one launch (start us, length us, event | category | flops | bytes accessed | tf_op | source)
XLA Modules:
  0.0 678.4 jit_solution(11965515708994956499)
XLA Ops:
  38.1 10.5 %collective-permute-done.7 = bf16[2,4096]{1,0:T(2,128)(2,1)S(1)} collective-permute-done((bf16[2,4096]{1,0:T(2,128)(2,1)S(1)}, bf16[2,4096]{1,0:T(2,128)(2,1)S(1)}, u32[]{:S(2)}, u32[]{:S(2)}) %collective-permute-start.7) | collective-permute-done | bytes 16416 | tf_op jit(solution)/shard_map/ppermute | solution.py:924
  50.8 7.2 %collective-permute-done.5.refs_15_ = bf16[256,1024]{1,0:T(8,128)(2,1)} collective-permute-done((bf16[256,1024]{1,0:T(8,128)(2,1)}, bf16[256,1024]{1,0:T(8,128)(2,1)}, u32[]{:S(2)}, u32[]{:S(2)}) %collective-permute-start.5) | collective-permute-done | bytes 524320 | tf_op jit(solution)/shard_map/ppermute | solution.py:586
  66.4 7.2 %collective-permute-done.12 = bf16[4,4096]{1,0:T(4,128)(2,1)S(1)} collective-permute-done((bf16[4,4096]{1,0:T(4,128)(2,1)S(1)}, bf16[4,4096]{1,0:T(4,128)(2,1)S(1)}, u32[]{:S(2)}, u32[]{:S(2)}) %collective-permute-start.12) | collective-permute-done | bytes 32800 | tf_op jit(solution)/shard_map/ppermute | solution.py:924
  89.5 9.3 %collective-permute-done.18.refs_13_ = bf16[256,1024]{1,0:T(8,128)(2,1)S(1)} collective-permute-done((bf16[256,1024]{1,0:T(8,128)(2,1)}, bf16[256,1024]{1,0:T(8,128)(2,1)S(1)}, u32[]{:S(2)}, u32[]{:S(2)}) %collective-permute-start.18) | collective-permute-done | bytes 524320 | tf_op jit(solution)/shard_map/ppermute | solution.py:590
  101.8 10.9 %rows_dot.2 = (bf16[512,512]{1,0:T(8,128)(2,1)}, bf16[512,512]{1,0:T(8,128)(2,1)}, bf16[512,512]{1,0:T(8,128)(2,1)}, f32[512,512]{1,0:T(8,128)}, bf16[2048,1024]{1,0:T(8,128)(2,1)}, /*index=5*/bf16[2048,1024]{1,0:T(8,128)(2,1)}) custom-call(bf16[512,2048]{1,0:T(8,128)(2,1)} %copy-done.30, bf16[256,1024]{1,0:T(8,128)(2,1)} %get-tuple-element.295.refs_1_, ...), custom_call_target="tpu_custom_call" | custom-call | flops 13200000000 | bytes 43200000 | tf_op jit(solution)/shard_map/rows_dot/pallas_call | solution.py:815
  124.7 9.2 %delta_local.1 = (bf16[512,512]{1,0:T(8,128)(2,1)}, bf16[512,512]{1,0:T(8,128)(2,1)}, bf16[512,512]{1,0:T(8,128)(2,1)}, f32[512,512]{1,0:T(8,128)}, bf16[512,512...) custom-call(s32[2]{0:T(128)} %pad_add_fusion.scal_ref, ...), custom_call_target="tpu_custom_call" | custom-call | flops 8800000000 | bytes 28800000 | tf_op jit(solution)/shard_map/delta_local/pallas_call | solution.py:473
  155.4 7.9 %collective-permute-done.29 = bf16[4,128,128]{2,1,0:T(8,128)(2,1)S(1)} collective-permute-done((bf16[4,128,128]{2,1,0:T(8,128)(2,1)S(1)}, bf16[4,128,128]{2,1,0:T(8,128)(2,1)S(1)}, u32[]{:S(2)}, u32[]{:S(2)}) %collective-permute-start.29) | collective-permute-done | bytes 131104 | tf_op jit(solution)/shard_map/ppermute | solution.py:1010
  188.0 6.5 delta_apply.1
  195.3 11.5 %rows_dot.3 = (f32[512,1408]{1,0:T(8,128)}, bf16[2048,896]{1,0:T(8,128)(2,1)}, bf16[2048,512]{1,0:T(8,128)(2,1)}, bf16[2048,512]{1,0:T(8,128)(2,1)}) custom-call(bf16[512,2048]{1,0:T(8,128)(2,1)} %copy-done, bf16[256,896]{1,0:T(8,128)(2,1)} %slice.377.refs_1_, bf16[256,896]{1,0:T(8,128)(2,1)} %collective-permute-done.16.refs_2_, ...), custom_call_target="tpu_custom_call" | custom-call | flops 13200000000 | bytes 43200000 | tf_op jit(solution)/shard_map/rows_dot/pallas_call | solution.py:815
  216.9 14.4 %collective-permute-done.36.refs_16_ = bf16[256,1408]{1,0:T(8,128)(2,1)} collective-permute-done((bf16[256,1408]{1,0:T(8,128)(2,1)}, bf16[256,1408]{1,0:T(8,128)(2,1)}, u32[]{:S(2)}, u32[]{:S(2)}) %collective-permute-start.36) | collective-permute-done | bytes 720928 | tf_op jit(solution)/shard_map/ppermute | solution.py:586
  239.4 14.6 %collective-permute-done.41.refs_15_ = bf16[256,1408]{1,0:T(8,128)(2,1)S(1)} collective-permute-done((bf16[256,1408]{1,0:T(8,128)(2,1)}, bf16[256,1408]{1,0:T(8,128)(2,1)S(1)}, u32[]{:S(2)}, u32[]{:S(2)}) %collective-permute-start.41) | collective-permute-done | bytes 720928 | tf_op jit(solution)/shard_map/ppermute | solution.py:586
  259.8 7.9 %collective-permute-done.44.refs_7_ = bf16[256,1408]{1,0:T(8,128)(2,1)} collective-permute-done((bf16[256,1408]{1,0:T(8,128)(2,1)S(1)}, bf16[256,1408]{1,0:T(8,128)(2,1)}, u32[]{:S(2)}, u32[]{:S(2)}) %collective-permute-start.44) | collective-permute-done | bytes 720928 | tf_op jit(solution)/shard_map/ppermute | solution.py:586
  277.4 10.6 %collective-permute-done.48.refs_2_ = bf16[256,1408]{1,0:T(8,128)(2,1)S(1)} collective-permute-done((bf16[256,1408]{1,0:T(8,128)(2,1)}, bf16[256,1408]{1,0:T(8,128)(2,1)S(1)}, u32[]{:S(2)}, u32[]{:S(2)}) %collective-permute-start.48) | collective-permute-done | bytes 720928 | tf_op jit(solution)/shard_map/ppermute | solution.py:586
  289.7 12.1 %glu_early.1 = (f32[512,1408]{1,0:T(8,128)}, f32[512,1408]{1,0:T(8,128)}, bf16[2048,1408]{1,0:T(8,128)(2,1)}, bf16[2048,1408]{1,0:T(8,128)(2,1)}) custom-call(bf16[512,2048]{1,0:T(8,128)(2,1)} %maximum_select_fusion.refs_0_, bf16[256,1408]{1,0:T(8,128)(2,1)} %get-tuple-element.375.refs_1_.refs_4_.refs_5_.refs_6_, ...), custom_call_target="tpu_custom_call" | custom-call | flops 15399999488 | bytes 50400000 | tf_op jit(solution)/shard_map/glu_early/pallas_call | solution.py:862
  305.5 12.0 %collective-permute-done.52.refs_4_ = bf16[256,1408]{1,0:T(8,128)(2,1)S(1)} collective-permute-done((bf16[256,1408]{1,0:T(8,128)(2,1)}, bf16[256,1408]{1,0:T(8,128)(2,1)S(1)}, u32[]{:S(2)}, u32[]{:S(2)}) %collective-permute-start.52) | collective-permute-done | bytes 720928 | tf_op jit(solution)/shard_map/ppermute | solution.py:590
  317.5 8.0 %glu_late.1 = (bf16[512,1408]{1,0:T(8,128)(2,1)}, bf16[512,1408]{1,0:T(8,128)(2,1)}, bf16[512,1408]{1,0:T(8,128)(2,1)}) custom-call(bf16[512,768]{1,0:T(8,128)(2,1)S(1)} %slice.297.value_ref, bf16[256,1408]{1,0:T(8,128)(2,1)} %collective-permute-done.49.refs_0_, bf16[256,1408]{1,0:T(8,128)(2,1)S(1)} %collective-permute-done.51.refs_1_, ...), custom_call_target="tpu_custom_call" | custom-call | flops 8800000000 | bytes 28800000 | tf_op jit(solution)/shard_map/glu_late/pallas_call | solution.py:910
  325.5 5.2 convolution_convert_fusion.1
  346.3 6.3 add_convert_fusion.2
  362.3 14.1 %collective-permute-done.53 = bf16[256,1408]{1,0:T(8,128)(2,1)S(1)} collective-permute-done((bf16[256,1408]{1,0:T(8,128)(2,1)S(1)}, bf16[256,1408]{1,0:T(8,128)(2,1)S(1)}, u32[]{:S(2)}, u32[]{:S(2)}) %collective-permute-start.53) | collective-permute-done | bytes 720928 | tf_op jit(solution)/shard_map/ppermute | solution.py:586
  384.6 7.2 %collective-permute-done.61 = bf16[256,1408]{1,0:T(8,128)(2,1)S(1)} collective-permute-done((bf16[256,1408]{1,0:T(8,128)(2,1)S(1)}, bf16[256,1408]{1,0:T(8,128)(2,1)S(1)}, u32[]{:S(2)}, u32[]{:S(2)}) %collective-permute-start.61) | collective-permute-done | bytes 720928 | tf_op jit(solution)/shard_map/ppermute | solution.py:586
  396.0 11.3 %collective-permute-done.58 = bf16[256,1408]{1,0:T(8,128)(2,1)S(1)} collective-permute-done((bf16[256,1408]{1,0:T(8,128)(2,1)S(1)}, bf16[256,1408]{1,0:T(8,128)(2,1)S(1)}, u32[]{:S(2)}, u32[]{:S(2)}) %collective-permute-start.58) | collective-permute-done | bytes 720928 | tf_op jit(solution)/shard_map/ppermute | solution.py:586
  424.0 7.4 %delta_back_local.1 = (bf16[512,512]{1,0:T(8,128)(2,1)S(1)}, f32[4,8,128]{2,1,0:T(8,128)S(1)}, bf16[512,512]{1,0:T(8,128)(2,1)S(1)}, f32[512,512]{1,0:T(8,128)S(1)}, f32[4,128,128]{2,1,0:T(8,128)S(1)}) custom-call(s32[2]{0:T(128)S(1)} %copy-done.11, f32[512,512]{1,0:T(8,128)S(1)} %fusion.63.dn_ref, f32[512,512]{1,0:T(8,128)S(1)} %copy-done.13, ...), custom_call_target="tpu_custom_call" | custom-call | flops 8800000000 | bytes 28800000 | tf_op jit(solution)/shard_map/delta_back_local/pallas_call | solution.py:523
  431.4 6.4 collective-permute-done.63
  454.9 9.8 %collective-permute-done.73 = bf16[4,128,128]{2,1,0:T(8,128)(2,1)S(1)} collective-permute-done((bf16[4,128,128]{2,1,0:T(8,128)(2,1)S(1)}, bf16[4,128,128]{2,1,0:T(8,128)(2,1)S(1)}, u32[]{:S(2)}, u32[]{:S(2)}) %collective-permute-start.73) | collective-permute-done | bytes 131104 | tf_op jit(solution)/shard_map/ppermute | solution.py:1010
  485.8 6.9 %collective-permute-done.80 = bf16[4,128,128]{2,1,0:T(8,128)(2,1)S(1)} collective-permute-done((bf16[4,128,128]{2,1,0:T(8,128)(2,1)S(1)}, bf16[4,128,128]{2,1,0:T(8,128)(2,1)S(1)}, u32[]{:S(2)}, u32[]{:S(2)}) %collective-permute-start.80) | collective-permute-done | bytes 131104 | tf_op jit(solution)/shard_map/ppermute | solution.py:1010
  505.3 15.4 %delta_back.1 = (bf16[3,512,512]{2,1,0:T(8,128)(2,1)}, f32[3,8,512]{2,1,0:T(8,128)S(1)}, f32[3,8,512]{2,1,0:T(8,128)S(1)}, f32[3,4,512]{2,1,0:T(4,128)S(1)}, f32[512,4]{1,0:T(8,128)S(1)}) custom-call(s32[2]{0:T(128)S(1)} %copy-done.11, bf16[512,512]{1,0:T(8,128)(2,1)S(1)} %copy-done.4, bf16[512,512]{1,0:T(8,128)(2,1)S(1)} %copy-done.5, ...), custom_call_target="tpu_custom_call" | custom-call | flops 16499999744 | bytes 54000000 | tf_op jit(solution)/shard_map/delta_back/pallas_call | solution.py:548
  558.2 6.3 convolution_convert_fusion.2
  621.4 7.7 %collective-permute-done.97 = bf16[272,1024]{1,0:T(8,128)(2,1)S(1)} collective-permute-done((bf16[272,1024]{1,0:T(8,128)(2,1)S(1)}, bf16[272,1024]{1,0:T(8,128)(2,1)S(1)}, u32[]{:S(2)}, u32[]{:S(2)}) %collective-permute-start.97) | collective-permute-done | bytes 557088 | tf_op jit(solution)/shard_map/ppermute | solution.py:586
  629.1 5.3 collective-permute-done.98
  644.7 8.0 %collective-permute-done.100 = bf16[272,1024]{1,0:T(8,128)(2,1)S(1)} collective-permute-done((bf16[272,1024]{1,0:T(8,128)(2,1)S(1)}, bf16[272,1024]{1,0:T(8,128)(2,1)S(1)}, u32[]{:S(2)}, u32[]{:S(2)}) %collective-permute-start.100) | collective-permute-done | bytes 557088 | tf_op jit(solution)/shard_map/ppermute | solution.py:586
  657.2 6.3 collective-permute-done.107
  671.3 5.6 fusion.51
  (671 shorter events, 386.1 us)
Async XLA Ops:
  3.7 27.7 %collective-permute-start = (bf16[256,1024]{1,0:T(8,128)(2,1)}, bf16[256,1024]{1,0:T(8,128)(2,1)}, u32[]{:S(2)}, u32[]{:S(2)}) collective-permute-start(bf16[256,1024]{1,0:T(8,128)(2,1)} %get-tuple-element.295.refs_1_), channel_id=1, source_target_pairs={{0,8},{8,16},{16,24},{24,28},{28,20},{20,12},{12,4},{4,0},{1,9},{9... | collective-permute-start | bytes 1572872 | tf_op jit(solution)/shard_map/ppermute | solution.py:586
  6.7 24.7 %collective-permute-start.1 = (bf16[256,1024]{1,0:T(8,128)(2,1)}, bf16[256,1024]{1,0:T(8,128)(2,1)}, u32[]{:S(2)}, u32[]{:S(2)}) collective-permute-start(bf16[256,1024]{1,0:T(8,128)(2,1)} %get-tuple-element.295.refs_1_), channel_id=1, source_target_pairs={{8,0},{16,8},{24,16},{28,24},{20,28},{12,20},{4,12},{0,4},{9,1},{1... | collective-permute-start | bytes 1572872 | tf_op jit(solution)/shard_map/ppermute | solution.py:590
  6.7 24.7 %collective-permute-start.2 = (bf16[256,1024]{1,0:T(8,128)(2,1)}, bf16[256,1024]{1,0:T(8,128)(2,1)}, u32[]{:S(2)}, u32[]{:S(2)}) collective-permute-start(bf16[256,1024]{1,0:T(8,128)(2,1)} %get-tuple-element.299.refs_9_), channel_id=1, source_target_pairs={{0,8},{8,16},{16,24},{24,28},{28,20},{20,12},{12,4},{4,0},{1,9},{9... | collective-permute-start | bytes 1572872 | tf_op jit(solution)/shard_map/ppermute | solution.py:586
  48.7 25.0 %collective-permute-start.13 = (bf16[256,1024]{1,0:T(8,128)(2,1)}, bf16[256,1024]{1,0:T(8,128)(2,1)}, u32[]{:S(2)}, u32[]{:S(2)}) collective-permute-start(bf16[256,1024]{1,0:T(8,128)(2,1)} %collective-permute-done.8.refs_7_), channel_id=1, source_target_pairs={{0,8},{8,16},{16,24},{24,28},{28,20},{20,12},{12,4},{4,0},{1,9},{9... | collective-permute-start | bytes 1572872 | tf_op jit(solution)/shard_map/ppermute | solution.py:586
  86.9 25.8 %collective-permute-start.15 = (bf16[256,896]{1,0:T(8,128)(2,1)S(1)}, bf16[256,896]{1,0:T(8,128)(2,1)}, u32[]{:S(2)}, u32[]{:S(2)}) collective-permute-start(bf16[256,896]{1,0:T(8,128)(2,1)S(1)} %copy-done.79), channel_id=1, source_target_pairs={{0,8},{8,16},{16,24},{24,28},{28,20},{20,12},{12,4},{4,0},{1,9},{9... | collective-permute-start | bytes 1376264 | tf_op jit(solution)/shard_map/ppermute | solution.py:586
  145.5 27.3 %collective-permute-start.31 = (bf16[256,1024]{1,0:T(8,128)(2,1)}, bf16[256,1024]{1,0:T(8,128)(2,1)}, u32[]{:S(2)}, u32[]{:S(2)}) collective-permute-start(bf16[256,1024]{1,0:T(8,128)(2,1)} %collective-permute-done.26.refs_15_.refs_23_), channel_id=1, source_target_pairs={{0,8},{8,16},{16,24},{24,28},{28,20},{20,12},{12,4},{4,0},{1,9},{9... | collective-permute-start | bytes 1572872 | tf_op jit(solution)/shard_map/ppermute | solution.py:586
  233.2 24.5 %collective-permute-start.43 = (bf16[256,2048]{1,0:T(8,128)(2,1)S(1)}, bf16[256,2048]{1,0:T(8,128)(2,1)S(1)}, u32[]{:S(2)}, u32[]{:S(2)}) collective-permute-start(bf16[256,2048]{1,0:T(8,128)(2,1)S(1)} %convert_element_type.598), channel_id=1, source_target_pairs={{0,2},{1,3},{2,0},{3,1},{4,6},{5,7},{6,4},{7,5},{8,10},{9,11},{10,... | collective-permute-start | bytes 3145736 | tf_op jit(solution)/shard_map/ppermute | solution.py:924
  237.4 30.4 %collective-permute-start.44 = (bf16[256,1408]{1,0:T(8,128)(2,1)S(1)}, bf16[256,1408]{1,0:T(8,128)(2,1)}, u32[]{:S(2)}, u32[]{:S(2)}) collective-permute-start(bf16[256,1408]{1,0:T(8,128)(2,1)S(1)} %copy-done.115), channel_id=1, source_target_pairs={{0,8},{8,16},{16,24},{24,28},{28,20},{20,12},{12,4},{4,0},{1,9},{9... | collective-permute-start | bytes 2162696 | tf_op jit(solution)/shard_map/ppermute | solution.py:586
  238.8 30.0 %collective-permute-start.45 = (bf16[256,1408]{1,0:T(8,128)(2,1)}, bf16[256,1408]{1,0:T(8,128)(2,1)}, u32[]{:S(2)}, u32[]{:S(2)}) collective-permute-start(bf16[256,1408]{1,0:T(8,128)(2,1)} %collective-permute-done.39.refs_2_), channel_id=1, source_target_pairs={{8,0},{16,8},{24,16},{28,24},{20,28},{12,20},{4,12},{0,4},{9,1},{1... | collective-permute-start | bytes 2162696 | tf_op jit(solution)/shard_map/ppermute | solution.py:590
  270.8 31.1 %collective-permute-start.46 = (bf16[256,1408]{1,0:T(8,128)(2,1)}, bf16[256,1408]{1,0:T(8,128)(2,1)S(1)}, u32[]{:S(2)}, u32[]{:S(2)}) collective-permute-start(bf16[256,1408]{1,0:T(8,128)(2,1)} %copy-done.116), channel_id=1, source_target_pairs={{0,8},{8,16},{16,24},{24,28},{28,20},{20,12},{12,4},{4,0},{1,9},{9... | collective-permute-start | bytes 2162696 | tf_op jit(solution)/shard_map/ppermute | solution.py:586
  272.4 29.7 %collective-permute-start.47 = (bf16[256,1408]{1,0:T(8,128)(2,1)}, bf16[256,1408]{1,0:T(8,128)(2,1)}, u32[]{:S(2)}, u32[]{:S(2)}) collective-permute-start(bf16[256,1408]{1,0:T(8,128)(2,1)} %copy-done.117), channel_id=1, source_target_pairs={{8,0},{16,8},{24,16},{28,24},{20,28},{12,20},{4,12},{0,4},{9,1},{1... | collective-permute-start | bytes 2162696 | tf_op jit(solution)/shard_map/ppermute | solution.py:590
  359.8 32.0 %collective-permute-start.61 = (bf16[256,1408]{1,0:T(8,128)(2,1)S(1)}, bf16[256,1408]{1,0:T(8,128)(2,1)S(1)}, u32[]{:S(2)}, u32[]{:S(2)}) collective-permute-start(bf16[256,1408]{1,0:T(8,128)(2,1)S(1)} %get-tuple-element.691), channel_id=1, source_target_pairs={{0,8},{8,16},{16,24},{24,28},{28,20},{20,12},{12,4},{4,0},{1,9},{9... | collective-permute-start | bytes 2162696 | tf_op jit(solution)/shard_map/ppermute | solution.py:586
  360.2 32.0 %collective-permute-start.62 = (bf16[256,1408]{1,0:T(8,128)(2,1)S(1)}, bf16[256,1408]{1,0:T(8,128)(2,1)S(1)}, u32[]{:S(2)}, u32[]{:S(2)}) collective-permute-start(bf16[256,1408]{1,0:T(8,128)(2,1)S(1)} %get-tuple-element.690), channel_id=1, source_target_pairs={{8,0},{16,8},{24,16},{28,24},{20,28},{12,20},{4,12},{0,4},{9,1},{1... | collective-permute-start | bytes 2162696 | tf_op jit(solution)/shard_map/ppermute | solution.py:590
  377.2 30.2 %collective-permute-start.58 = (bf16[256,1408]{1,0:T(8,128)(2,1)S(1)}, bf16[256,1408]{1,0:T(8,128)(2,1)S(1)}, u32[]{:S(2)}, u32[]{:S(2)}) collective-permute-start(bf16[256,1408]{1,0:T(8,128)(2,1)S(1)} %get-tuple-element.693), channel_id=1, source_target_pairs={{0,8},{8,16},{16,24},{24,28},{28,20},{20,12},{12,4},{4,0},{1,9},{9... | collective-permute-start | bytes 2162696 | tf_op jit(solution)/shard_map/ppermute | solution.py:586
  377.7 30.0 %collective-permute-start.59 = (bf16[256,1408]{1,0:T(8,128)(2,1)S(1)}, bf16[256,1408]{1,0:T(8,128)(2,1)S(1)}, u32[]{:S(2)}, u32[]{:S(2)}) collective-permute-start(bf16[256,1408]{1,0:T(8,128)(2,1)S(1)} %get-tuple-element.692), channel_id=1, source_target_pairs={{8,0},{16,8},{24,16},{28,24},{20,28},{12,20},{4,12},{0,4},{9,1},{1... | collective-permute-start | bytes 2162696 | tf_op jit(solution)/shard_map/ppermute | solution.py:590
  379.6 28.1 %collective-permute-start.60 = (bf16[256,2048]{1,0:T(8,128)(2,1)S(1)}, bf16[256,2048]{1,0:T(8,128)(2,1)S(1)}, u32[]{:S(2)}, u32[]{:S(2)}) collective-permute-start(bf16[256,2048]{1,0:T(8,128)(2,1)S(1)} %convert_element_type.615), channel_id=1, source_target_pairs={{0,2},{1,3},{2,0},{3,1},{4,6},{5,7},{6,4},{7,5},{8,10},{9,11},{10,... | collective-permute-start | bytes 3145736 | tf_op jit(solution)/shard_map/ppermute | solution.py:924
  393.9 28.8 %collective-permute-start.65 = (bf16[256,1408]{1,0:T(8,128)(2,1)S(1)}, bf16[256,1408]{1,0:T(8,128)(2,1)S(1)}, u32[]{:S(2)}, u32[]{:S(2)}) collective-permute-start(bf16[256,1408]{1,0:T(8,128)(2,1)S(1)} %get-tuple-element.687), channel_id=1, source_target_pairs={{0,8},{8,16},{16,24},{24,28},{28,20},{20,12},{12,4},{4,0},{1,9},{9... | collective-permute-start | bytes 2162696 | tf_op jit(solution)/shard_map/ppermute | solution.py:586
  394.5 28.6 %collective-permute-start.66 = (bf16[256,1408]{1,0:T(8,128)(2,1)S(1)}, bf16[256,1408]{1,0:T(8,128)(2,1)S(1)}, u32[]{:S(2)}, u32[]{:S(2)}) collective-permute-start(bf16[256,1408]{1,0:T(8,128)(2,1)S(1)} %get-tuple-element.686), channel_id=1, source_target_pairs={{8,0},{16,8},{24,16},{28,24},{20,28},{12,20},{4,12},{0,4},{9,1},{1... | collective-permute-start | bytes 2162696 | tf_op jit(solution)/shard_map/ppermute | solution.py:590
  412.7 25.1 %collective-permute-start.63 = (bf16[256,1408]{1,0:T(8,128)(2,1)}, bf16[256,1408]{1,0:T(8,128)(2,1)S(1)}, u32[]{:S(2)}, u32[]{:S(2)}) collective-permute-start(bf16[256,1408]{1,0:T(8,128)(2,1)} %get-tuple-element.689), channel_id=1, source_target_pairs={{0,8},{8,16},{16,24},{24,28},{28,20},{20,12},{12,4},{4,0},{1,9},{9... | collective-permute-start | bytes 2162696 | tf_op jit(solution)/shard_map/ppermute | solution.py:586
  439.4 25.3 %collective-permute-start.72 = (bf16[256,1408]{1,0:T(8,128)(2,1)S(1)}, bf16[256,1408]{1,0:T(8,128)(2,1)S(1)}, u32[]{:S(2)}, u32[]{:S(2)}) collective-permute-start(bf16[256,1408]{1,0:T(8,128)(2,1)S(1)} %add_convert_fusion.3), channel_id=1, source_target_pairs={{8,0},{16,8},{24,16},{28,24},{20,28},{12,20},{4,12},{0,4},{9,1},{1... | collective-permute-start | bytes 2162696 | tf_op jit(solution)/shard_map/ppermute | solution.py:590
  447.6 32.8 %collective-permute-start.69 = (bf16[256,896]{0,1:T(8,128)(2,1)S(1)}, bf16[256,896]{0,1:T(8,128)(2,1)S(1)}, u32[]{:S(2)}, u32[]{:S(2)}) collective-permute-start(bf16[256,896]{0,1:T(8,128)(2,1)S(1)} %get-tuple-element.467), channel_id=1, source_target_pairs={{0,8},{8,16},{16,24},{24,28},{28,20},{20,12},{12,4},{4,0},{1,9},{9... | collective-permute-start | bytes 1376264 | tf_op jit(solution)/shard_map/ppermute | solution.py:586
  494.9 40.9 %collective-permute-start.84 = (bf16[256,1024]{0,1:T(8,128)(2,1)S(1)}, bf16[256,1024]{0,1:T(8,128)(2,1)S(1)}, u32[]{:S(2)}, u32[]{:S(2)}) collective-permute-start(bf16[256,1024]{0,1:T(8,128)(2,1)S(1)} %get-tuple-element.713), channel_id=1, source_target_pairs={{0,8},{8,16},{16,24},{24,28},{28,20},{20,12},{12,4},{4,0},{1,9},{9... | collective-permute-start | bytes 1572872 | tf_op jit(solution)/shard_map/ppermute | solution.py:586
  499.1 36.7 %collective-permute-start.85 = (bf16[256,1024]{0,1:T(8,128)(2,1)S(1)}, bf16[256,1024]{0,1:T(8,128)(2,1)S(1)}, u32[]{:S(2)}, u32[]{:S(2)}) collective-permute-start(bf16[256,1024]{0,1:T(8,128)(2,1)S(1)} %get-tuple-element.712), channel_id=1, source_target_pairs={{8,0},{16,8},{24,16},{28,24},{20,28},{12,20},{4,12},{0,4},{9,1},{1... | collective-permute-start | bytes 1572872 | tf_op jit(solution)/shard_map/ppermute | solution.py:590
  524.6 32.3 %collective-permute-start.82 = (bf16[256,896]{0,1:T(8,128)(2,1)}, bf16[256,896]{0,1:T(8,128)(2,1)}, u32[]{:S(2)}, u32[]{:S(2)}) collective-permute-start(bf16[256,896]{0,1:T(8,128)(2,1)} %get-tuple-element.717), channel_id=1, source_target_pairs={{0,8},{8,16},{16,24},{24,28},{28,20},{20,12},{12,4},{4,0},{1,9},{9... | collective-permute-start | bytes 1376264 | tf_op jit(solution)/shard_map/ppermute | solution.py:586
  528.8 28.5 %collective-permute-start.83 = (bf16[256,896]{0,1:T(8,128)(2,1)}, bf16[256,896]{0,1:T(8,128)(2,1)}, u32[]{:S(2)}, u32[]{:S(2)}) collective-permute-start(bf16[256,896]{0,1:T(8,128)(2,1)} %get-tuple-element.716), channel_id=1, source_target_pairs={{8,0},{16,8},{24,16},{28,24},{20,28},{12,20},{4,12},{0,4},{9,1},{1... | collective-permute-start | bytes 1376264 | tf_op jit(solution)/shard_map/ppermute | solution.py:590
  543.3 30.4 %collective-permute-start.88 = (bf16[256,1024]{0,1:T(8,128)(2,1)}, bf16[256,1024]{0,1:T(8,128)(2,1)}, u32[]{:S(2)}, u32[]{:S(2)}) collective-permute-start(bf16[256,1024]{0,1:T(8,128)(2,1)} %get-tuple-element.711), channel_id=1, source_target_pairs={{0,8},{8,16},{16,24},{24,28},{28,20},{20,12},{12,4},{4,0},{1,9},{9... | collective-permute-start | bytes 1572872 | tf_op jit(solution)/shard_map/ppermute | solution.py:586
  545.3 28.4 %collective-permute-start.89 = (bf16[256,1024]{0,1:T(8,128)(2,1)}, bf16[256,1024]{0,1:T(8,128)(2,1)}, u32[]{:S(2)}, u32[]{:S(2)}) collective-permute-start(bf16[256,1024]{0,1:T(8,128)(2,1)} %get-tuple-element.710), channel_id=1, source_target_pairs={{8,0},{16,8},{24,16},{28,24},{20,28},{12,20},{4,12},{0,4},{9,1},{1... | collective-permute-start | bytes 1572872 | tf_op jit(solution)/shard_map/ppermute | solution.py:590
  547.6 28.6 %collective-permute-start.93 = (bf16[256,1024]{1,0:T(8,128)(2,1)}, bf16[256,1024]{1,0:T(8,128)(2,1)}, u32[]{:S(2)}, u32[]{:S(2)}) collective-permute-start(bf16[256,1024]{1,0:T(8,128)(2,1)} %get-tuple-element.517), channel_id=1, source_target_pairs={{0,8},{8,16},{16,24},{24,28},{28,20},{20,12},{12,4},{4,0},{1,9},{9... | collective-permute-start | bytes 1572872 | tf_op jit(solution)/shard_map/ppermute | solution.py:586
  576.6 31.3 %collective-permute-start.96 = (f32[256,2048]{1,0:T(8,128)S(1)}, f32[256,2048]{1,0:T(8,128)S(1)}, u32[]{:S(2)}, u32[]{:S(2)}) collective-permute-start(f32[256,2048]{1,0:T(8,128)S(1)} %add.531.own_ref), channel_id=1, source_target_pairs={{0,1},{1,0},{2,3},{3,2},{4,5},{5,4},{6,7},{7,6},{8,9},{9,8},{10,11... | collective-permute-start | bytes 6291464 | tf_op jit(solution)/shard_map/ppermute | solution.py:924
  577.9 28.3 %collective-permute-start.95 = (bf16[256,2048]{1,0:T(8,128)(2,1)S(1)}, bf16[256,2048]{1,0:T(8,128)(2,1)S(1)}, u32[]{:S(2)}, u32[]{:S(2)}) collective-permute-start(bf16[256,2048]{1,0:T(8,128)(2,1)S(1)} %constant_dynamic-slice_fusion.1), channel_id=1, source_target_pairs={{0,1},{1,0},{2,3},{3,2},{4,5},{5,4},{6,7},{7,6},{8,9},{9,8},{10,11... | collective-permute-start | bytes 3145736 | tf_op jit(solution)/shard_map/ppermute | solution.py:924
  603.3 33.4 %collective-permute-start.104 = (bf16[256,1024]{1,0:T(8,128)(2,1)}, bf16[256,1024]{1,0:T(8,128)(2,1)}, u32[]{:S(2)}, u32[]{:S(2)}) collective-permute-start(bf16[256,1024]{1,0:T(8,128)(2,1)} %get-tuple-element.705), channel_id=1, source_target_pairs={{0,8},{8,16},{16,24},{24,28},{28,20},{20,12},{12,4},{4,0},{1,9},{9... | collective-permute-start | bytes 1572872 | tf_op jit(solution)/shard_map/ppermute | solution.py:586
  606.2 30.5 %collective-permute-start.105 = (bf16[256,1024]{1,0:T(8,128)(2,1)}, bf16[256,1024]{1,0:T(8,128)(2,1)}, u32[]{:S(2)}, u32[]{:S(2)}) collective-permute-start(bf16[256,1024]{1,0:T(8,128)(2,1)} %get-tuple-element.704), channel_id=1, source_target_pairs={{8,0},{16,8},{24,16},{28,24},{20,28},{12,20},{4,12},{0,4},{9,1},{1... | collective-permute-start | bytes 1572872 | tf_op jit(solution)/shard_map/ppermute | solution.py:590
  (215 other events, 2573.1 us)

commit v4 on v3

--- a/solution.py
+++ b/solution.py
@@ -746,14 +746,24 @@
         self.flying = []
         self.token = token
 
-    def step(self, ring, stage, values=()):
+    def wait(self, values):
+        keys = [one for _, _, sent in self.flying for one in sent]
+        self.flying = []
+        arrived, values, self.token = lax.optimization_barrier(
+            ([held[key] for held, key in keys], values, self.token)
+        )
+        for (held, key), value in zip(keys, arrived):
+            held[key] = value
+        return values
+
+    def step(self, ring, stage, values=(), most=4):
         each = lax.axis_size("seq") // 8
         for slot in range(stage * each, (stage + 1) * each):
             fresh = ring.fresh(slot)
             new = 1 if slot // 2 == ring.half - 1 else 2
             keys = []
             while self.flying and (
-                sum(len(sent) for _, _, sent in self.flying) + new > 4
+                sum(len(sent) for _, _, sent in self.flying) + new > most
                 or any(other is ring and was <= slot - 2 for other, was, _ in self.flying)
             ):
                 keys += self.flying.pop(0)[2]
@@ -1152,7 +1162,7 @@
         [(0, 0, cut, 0, 0), (1, 0, rest, 0, cut)],
         [jax.ShapeDtypeStruct((rows, units), f32)],
     )
-    w_out, normed, grad_act = flow.step(ring_m, 2, (w_out, normed, grad_act))
+    w_out, normed, grad_act = flow.step(ring_m, 2, (w_out, normed, grad_act), most=2)
     pair = summed_pair(low(dot_nt(normed, w_out)))
     pair = flow.step(ring_m, 3, pair)
     parts = asked(pair)
@@ -1241,6 +1251,11 @@
     grad_pre, tail, back_halo, grad_taps, grad_logits = delta_back(
         scal, pre, halo, taps, logits, q, k, w, t, change, states, grad_out, through, above
     )
+    grad_pre, tail, back_halo, grad_taps, grad_logits = flow.wait(
+        (grad_pre, tail, back_halo, grad_taps, grad_logits)
+    )
+    flow.step(back_do, 5)
+    flow.step(back_do, 6)
     fixed = low(tail + passed_along(back_halo, -1))
     grad_logits = low(grad_logits)
     grad_pre = lax.dynamic_update_slice_in_dim(grad_pre, fixed, rows - 8, 1)
@@ -1248,7 +1263,7 @@
     grad_vg = jnp.concatenate([grad_pre[2], grad_gate], axis=1)
     grad_w_qk = low(dot_tn(hidden, grad_qk))
     grad_w_qk, grad_qk, grad_vg, grad_logits, grad_taps = flow.step(
-        back_do, 5, (grad_w_qk, grad_qk, grad_vg, grad_logits, grad_taps)
+        back_do, 7, (grad_w_qk, grad_qk, grad_vg, grad_logits, grad_taps)
     )
     grad_beta = dot_tn(grad_logits, hidden)
     grad_conv = jnp.transpose(
@@ -1258,9 +1273,6 @@
         dot_nt(grad_qk, w_qk) + dot_nt(grad_vg, w_vg) + dot(grad_logits, w_beta)
     )
     grad_gain_a = jnp.sum(grad_hidden.astype(f32) * x_rows * x_inv, axis=0, keepdims=True)
-    grad_hidden, grad_gain_a, grad_vg = flow.step(
-        back_do, 6, (grad_hidden, grad_gain_a, grad_vg)
-    )
     stacked = jnp.concatenate([grad_gain_a, grad_gain_m, grad_beta], axis=0)
     stacked = jnp.take(stacked.reshape(2 + heads, count, -1), targets, axis=1).reshape(-1, D)
     grad_gains = jnp.concatenate(
@@ -1277,18 +1289,12 @@
     small = jnp.pad(jnp.take(small, sources, axis=0), ((0, 0), (0, 13), (0, 0)))
     grad_w_vg = low(dot_tn(hidden, grad_vg)).reshape(count, -1, 2 * width)
     grad_w_vg = jnp.concatenate([grad_w_vg, small], axis=1)
-    grad_w_vg = flow.step(back_do, 7, grad_w_vg)
     back_p = Scatter(rows_of(grad_w_qk), lambda one: grad_w_vg[one])
     flow.step(back_p, 0)
     flow.step(back_p, 1)
-    grad_hidden, mlp_master, mlp_sum = flow.step(
-        back_p, 2, (grad_hidden, mlp_master, mlp_sum)
-    )
+    grad_hidden, mlp_master = flow.step(back_p, 2, (grad_hidden, mlp_master))
     pair = summed_pair(grad_hidden)
-    result = join_columns(x_one + mlp_sum, targets)
-    pair, result, down_master, out_master = flow.step(
-        back_p, 3, (pair, result, down_master, out_master)
-    )
+    pair, down_master, out_master = flow.step(back_p, 3, (pair, down_master, out_master))
     parts = asked(pair)
     mlp_g_sum, mlp_u_sum = back_m.sums()
     mlp_new, mlp_first_new, mlp_second_new = adam_update(
@@ -1307,14 +1313,15 @@
     out_new, out_first_new, out_second_new = adam_update(
         out_master, out_first, out_second, out_sum, rate_matrix, decay_matrix
     )
-    parts, down_new, down_first_new, down_second_new = flow.step(
-        back_p, 5, (parts, down_new, down_first_new, down_second_new)
+    mlp_sum, down_new, down_first_new, down_second_new = flow.step(
+        back_p, 5, (mlp_sum, down_new, down_first_new, down_second_new)
+    )
+    result = join_columns(x_one + mlp_sum, targets)
+    parts, result, out_new, out_first_new, out_second_new = flow.step(
+        back_p, 6, (parts, result, out_new, out_first_new, out_second_new)
     )
     grad_x_rest = norm_back(own_half(x_rows), own_half(x_inv), gain_a, summed(parts))
     input_half = grad_x_one + grad_x_rest
-    input_half, out_new, out_first_new, out_second_new = flow.step(
-        back_p, 6, (input_half, out_new, out_first_new, out_second_new)
-    )
     input_grad = flow.step(back_p, 7, join_columns(input_half, targets))
     qk_sum, vg_sum = back_p.sums()
     small_sum = [vg_sum[shard + one, : sizes[one]] for one in range(3)]

time: 688 us -> 688 us (level)
  waiting for transfers between devices: 251 us -> 271 us
  local copies, waits for them, and re-layouts: 49 us -> 39.2 us
  other arithmetic: 85 us -> 75.9 us
    ppermute x42, waiting for transfers between devices: 134 us -> 152 us  [send_up(): return lax.ppermute(value, 'seq', ring_pairs(lax.axis_size('seq')))]
    ppermute x42, starting transfers between devices: 30.2 us -> 40.9 us  [send_down(): lax.ppermute(value, 'seq', [(b, a) for a, b in ring_pairs(lax.axis_size('...]
    ppermute x42, waiting for transfers between devices: 52.2 us -> 62.5 us  [send_down(): lax.ppermute(value, 'seq', [(b, a) for a, b in ring_pairs(lax.axis_size('...]
    ppermute x10, waiting for transfers between devices: 35.4 us -> 25.4 us  [passed_along(): lax.ppermute(value, 'seq', [(source, source + steps) for source in range(...]
    ppermute x42, starting transfers between devices: 75.8 us -> 68.4 us  [send_up(): return lax.ppermute(value, 'seq', ring_pairs(lax.axis_size('seq')))]
    unnamed x273 -> x269, local copies, waits for them, and re-layouts: 19.3 us -> 16.7 us
  transfers between devices with their start and end apart: 112 -> 112, of which waited for: 53 -> 60; matrix products, arithmetic and copies ran while one was open for 21% -> 17% of each run, Pallas kernels for 12% -> 12%
where the time goes in v4:
time: 688 us; the launch traced here: 679 us
  waiting for transfers between devices  271 us (39%)
  starting transfers between devices  147 us (21%)
  Pallas kernels  89.2 us (13%)
  other arithmetic  75.9 us (11%)
  matrix products  53.1 us (8%)
  local copies, waits for them, and re-layouts  39.2 us (6%)
    ppermute x42, waiting for transfers between devices, send_up(): return lax.ppermute(value, 'seq', ring_pairs(lax.axis_size('seq')))  152 us
    ppermute x42, starting transfers between devices, send_up(): return lax.ppermute(value, 'seq', ring_pairs(lax.axis_size('seq')))  68.4 us
    ppermute x42, waiting for transfers between devices, send_down(): lax.ppermute(value, 'seq', [(b, a) for a, b in ring_pairs(lax.axis_size('...  62.5 us
    ppermute x42, starting transfers between devices, send_down(): lax.ppermute(value, 'seq', [(b, a) for a, b in ring_pairs(lax.axis_size('...  40.9 us
    ppermute x18, waiting for transfers between devices, swap(): return lax.ppermute(value, axis, [(one, one ^ bit) for one in range(count)])  31.1 us
    ppermute x10, waiting for transfers between devices, passed_along(): lax.ppermute(value, 'seq', [(source, source + steps) for source in range(...  25.4 us
    ppermute x10, starting transfers between devices, passed_along(): lax.ppermute(value, 'seq', [(source, source + steps) for source in range(...  24.6 us
    dot_general x8, matrix products, dot_tn(): lax.dot_general(a, b, (((0,), (0,)), ((), ())), preferred_element_type=jn...  23.3 us
  transfers between devices with their start and end apart: 112, of which 60 were waited for; matrix products, arithmetic and copies ran while one was open for 17% of the time, Pallas kernels for 12%

profile of v4, /device:TPU:0, one launch (start us, length us, event | category | flops | bytes accessed | tf_op | source)
XLA Modules:
  0.0 678.8 jit_solution(4998813829685377479)
XLA Ops:
  35.7 11.2 %collective-permute-done.7 = bf16[2,4096]{1,0:T(2,128)(2,1)S(1)} collective-permute-done((bf16[2,4096]{1,0:T(2,128)(2,1)S(1)}, bf16[2,4096]{1,0:T(2,128)(2,1)S(1)}, u32[]{:S(2)}, u32[]{:S(2)}) %collective-permute-start.7) | collective-permute-done | bytes 16416 | tf_op jit(solution)/shard_map/ppermute | solution.py:934
  50.7 7.1 %collective-permute-done.5.refs_15_ = bf16[256,1024]{1,0:T(8,128)(2,1)} collective-permute-done((bf16[256,1024]{1,0:T(8,128)(2,1)}, bf16[256,1024]{1,0:T(8,128)(2,1)}, u32[]{:S(2)}, u32[]{:S(2)}) %collective-permute-start.5) | collective-permute-done | bytes 524320 | tf_op jit(solution)/shard_map/ppermute | solution.py:586
  66.4 7.2 %collective-permute-done.12 = bf16[4,4096]{1,0:T(4,128)(2,1)S(1)} collective-permute-done((bf16[4,4096]{1,0:T(4,128)(2,1)S(1)}, bf16[4,4096]{1,0:T(4,128)(2,1)S(1)}, u32[]{:S(2)}, u32[]{:S(2)}) %collective-permute-start.12) | collective-permute-done | bytes 32800 | tf_op jit(solution)/shard_map/ppermute | solution.py:934
  89.2 9.6 %collective-permute-done.18.refs_13_ = bf16[256,1024]{1,0:T(8,128)(2,1)S(1)} collective-permute-done((bf16[256,1024]{1,0:T(8,128)(2,1)}, bf16[256,1024]{1,0:T(8,128)(2,1)S(1)}, u32[]{:S(2)}, u32[]{:S(2)}) %collective-permute-start.18) | collective-permute-done | bytes 524320 | tf_op jit(solution)/shard_map/ppermute | solution.py:590
  101.8 10.9 %rows_dot.2 = (bf16[512,512]{1,0:T(8,128)(2,1)}, bf16[512,512]{1,0:T(8,128)(2,1)}, bf16[512,512]{1,0:T(8,128)(2,1)}, f32[512,512]{1,0:T(8,128)}, bf16[2048,1024]{1,0:T(8,128)(2,1)}, /*index=5*/bf16[2048,1024]{1,0:T(8,128)(2,1)}) custom-call(bf16[512,2048]{1,0:T(8,128)(2,1)} %copy-done.30, bf16[256,1024]{1,0:T(8,128)(2,1)} %get-tuple-element.294.refs_1_, ...), custom_call_target="tpu_custom_call" | custom-call | flops 13200000000 | bytes 43200000 | tf_op jit(solution)/shard_map/rows_dot/pallas_call | solution.py:825
  124.7 9.2 %delta_local.1 = (bf16[512,512]{1,0:T(8,128)(2,1)}, bf16[512,512]{1,0:T(8,128)(2,1)}, bf16[512,512]{1,0:T(8,128)(2,1)}, f32[512,512]{1,0:T(8,128)}, bf16[512,512...) custom-call(s32[2]{0:T(128)} %pad_add_fusion.scal_ref, ...), custom_call_target="tpu_custom_call" | custom-call | flops 8800000000 | bytes 28800000 | tf_op jit(solution)/shard_map/delta_local/pallas_call | solution.py:473
  155.4 8.0 %collective-permute-done.31 = bf16[4,128,128]{2,1,0:T(8,128)(2,1)S(1)} collective-permute-done((bf16[4,128,128]{2,1,0:T(8,128)(2,1)S(1)}, bf16[4,128,128]{2,1,0:T(8,128)(2,1)S(1)}, u32[]{:S(2)}, u32[]{:S(2)}) %collective-permute-start.31) | collective-permute-done | bytes 131104 | tf_op jit(solution)/shard_map/ppermute | solution.py:1020
  187.4 6.6 delta_apply.1
  199.1 11.5 %rows_dot.3 = (f32[512,1408]{1,0:T(8,128)}, bf16[2048,896]{1,0:T(8,128)(2,1)}, bf16[2048,512]{1,0:T(8,128)(2,1)}, bf16[2048,512]{1,0:T(8,128)(2,1)}) custom-call(bf16[512,2048]{1,0:T(8,128)(2,1)} %copy-done, bf16[256,896]{1,0:T(8,128)(2,1)} %copy-done.80, bf16[256,896]{1,0:T(8,128)(2,1)} %collective-permute-done.16.refs_2_, ...), custom_call_target="tpu_custom_call" | custom-call | flops 13200000000 | bytes 43200000 | tf_op jit(solution)/shard_map/rows_dot/pallas_call | solution.py:825
  210.6 6.4 collective-permute-done.38.refs_16_
  233.7 14.2 %collective-permute-done.40.refs_15_ = bf16[256,1408]{1,0:T(8,128)(2,1)S(1)} collective-permute-done((bf16[256,1408]{1,0:T(8,128)(2,1)}, bf16[256,1408]{1,0:T(8,128)(2,1)S(1)}, u32[]{:S(2)}, u32[]{:S(2)}) %collective-permute-start.40) | collective-permute-done | bytes 720928 | tf_op jit(solution)/shard_map/ppermute | solution.py:586
  254.8 7.7 %collective-permute-done.44.refs_7_ = bf16[256,1408]{1,0:T(8,128)(2,1)} collective-permute-done((bf16[256,1408]{1,0:T(8,128)(2,1)}, bf16[256,1408]{1,0:T(8,128)(2,1)}, u32[]{:S(2)}, u32[]{:S(2)}) %collective-permute-start.44) | collective-permute-done | bytes 720928 | tf_op jit(solution)/shard_map/ppermute | solution.py:586
  273.4 10.3 %collective-permute-done.48.refs_2_ = bf16[256,1408]{1,0:T(8,128)(2,1)S(1)} collective-permute-done((bf16[256,1408]{1,0:T(8,128)(2,1)}, bf16[256,1408]{1,0:T(8,128)(2,1)S(1)}, u32[]{:S(2)}, u32[]{:S(2)}) %collective-permute-start.48) | collective-permute-done | bytes 720928 | tf_op jit(solution)/shard_map/ppermute | solution.py:586
  286.1 12.1 %glu_early.1 = (f32[512,1408]{1,0:T(8,128)}, f32[512,1408]{1,0:T(8,128)}, bf16[2048,1408]{1,0:T(8,128)(2,1)}, bf16[2048,1408]{1,0:T(8,128)(2,1)}) custom-call(bf16[512,2048]{1,0:T(8,128)(2,1)} %maximum_select_fusion.refs_0_, bf16[256,1408]{1,0:T(8,128)(2,1)} %get-tuple-element.362.refs_1_.refs_4_.refs_5_.refs_6_, ...), custom_call_target="tpu_custom_call" | custom-call | flops 15399999488 | bytes 50400000 | tf_op jit(solution)/shard_map/glu_early/pallas_call | solution.py:872
  302.6 12.7 %collective-permute-done.52.refs_4_ = bf16[256,1408]{1,0:T(8,128)(2,1)S(1)} collective-permute-done((bf16[256,1408]{1,0:T(8,128)(2,1)}, bf16[256,1408]{1,0:T(8,128)(2,1)S(1)}, u32[]{:S(2)}, u32[]{:S(2)}) %collective-permute-start.52) | collective-permute-done | bytes 720928 | tf_op jit(solution)/shard_map/ppermute | solution.py:590
  315.5 8.0 %glu_late.1 = (bf16[512,1408]{1,0:T(8,128)(2,1)}, bf16[512,1408]{1,0:T(8,128)(2,1)}, bf16[512,1408]{1,0:T(8,128)(2,1)}) custom-call(bf16[512,768]{1,0:T(8,128)(2,1)S(1)} %slice.297.value_ref, bf16[256,1408]{1,0:T(8,128)(2,1)} %collective-permute-done.49.refs_0_, bf16[256,1408]{1,0:T(8,128)(2,1)S(1)} %collective-permute-done.51.refs_1_, ...), custom_call_target="tpu_custom_call" | custom-call | flops 8800000000 | bytes 28800000 | tf_op jit(solution)/shard_map/glu_late/pallas_call | solution.py:920
  344.3 6.3 add_convert_fusion.2
  360.3 14.1 %collective-permute-done.53 = bf16[256,1408]{1,0:T(8,128)(2,1)S(1)} collective-permute-done((bf16[256,1408]{1,0:T(8,128)(2,1)S(1)}, bf16[256,1408]{1,0:T(8,128)(2,1)S(1)}, u32[]{:S(2)}, u32[]{:S(2)}) %collective-permute-start.53) | collective-permute-done | bytes 720928 | tf_op jit(solution)/shard_map/ppermute | solution.py:586
  382.9 7.0 %collective-permute-done.61 = bf16[256,1408]{1,0:T(8,128)(2,1)S(1)} collective-permute-done((bf16[256,1408]{1,0:T(8,128)(2,1)S(1)}, bf16[256,1408]{1,0:T(8,128)(2,1)S(1)}, u32[]{:S(2)}, u32[]{:S(2)}) %collective-permute-start.61) | collective-permute-done | bytes 720928 | tf_op jit(solution)/shard_map/ppermute | solution.py:586
  394.5 10.9 %collective-permute-done.58 = bf16[256,1408]{1,0:T(8,128)(2,1)S(1)} collective-permute-done((bf16[256,1408]{1,0:T(8,128)(2,1)S(1)}, bf16[256,1408]{1,0:T(8,128)(2,1)S(1)}, u32[]{:S(2)}, u32[]{:S(2)}) %collective-permute-start.58) | collective-permute-done | bytes 720928 | tf_op jit(solution)/shard_map/ppermute | solution.py:586
  421.6 7.4 %delta_back_local.1 = (bf16[512,512]{1,0:T(8,128)(2,1)S(1)}, f32[4,8,128]{2,1,0:T(8,128)S(1)}, bf16[512,512]{1,0:T(8,128)(2,1)S(1)}, f32[512,512]{1,0:T(8,128)S(1)}, f32[4,128,128]{2,1,0:T(8,128)S(1)}) custom-call(s32[2]{0:T(128)S(1)} %copy-done.11, f32[512,512]{1,0:T(8,128)S(1)} %fusion.63.dn_ref, f32[512,512]{1,0:T(8,128)S(1)} %copy-done.13, ...), custom_call_target="tpu_custom_call" | custom-call | flops 8800000000 | bytes 28800000 | tf_op jit(solution)/shard_map/delta_back_local/pallas_call | solution.py:523
  429.1 6.8 collective-permute-done.63
  454.0 10.2 %collective-permute-done.70 = bf16[256,1408]{1,0:T(8,128)(2,1)S(1)} collective-permute-done((bf16[256,1408]{1,0:T(8,128)(2,1)S(1)}, bf16[256,1408]{1,0:T(8,128)(2,1)S(1)}, u32[]{:S(2)}, u32[]{:S(2)}) %collective-permute-start.70) | collective-permute-done | bytes 720928 | tf_op jit(solution)/shard_map/ppermute | solution.py:590
  486.1 6.1 collective-permute-done.78
  507.2 15.4 %delta_back.1 = (bf16[3,512,512]{2,1,0:T(8,128)(2,1)}, f32[3,8,512]{2,1,0:T(8,128)S(1)}, f32[3,8,512]{2,1,0:T(8,128)S(1)}, f32[3,4,512]{2,1,0:T(4,128)S(1)}, f32[512,4]{1,0:T(8,128)S(1)}) custom-call(s32[2]{0:T(128)S(1)} %copy-done.11, bf16[512,512]{1,0:T(8,128)(2,1)S(1)} %copy-done.4, bf16[512,512]{1,0:T(8,128)(2,1)S(1)} %copy-done.5, ...), custom_call_target="tpu_custom_call" | custom-call | flops 16499999744 | bytes 54000000 | tf_op jit(solution)/shard_map/delta_back/pallas_call | solution.py:548
  565.2 5.9 collective-permute-done.90
  571.9 6.3 collective-permute-done.96
  582.8 6.3 collective-permute-done.97
  611.1 5.7 collective-permute-done.91
  624.9 7.3 %collective-permute-done.93 = bf16[256,1024]{1,0:T(8,128)(2,1)} collective-permute-done((bf16[256,1024]{1,0:T(8,128)(2,1)}, bf16[256,1024]{1,0:T(8,128)(2,1)}, u32[]{:S(2)}, u32[]{:S(2)}) %collective-permute-start.93) | collective-permute-done | bytes 524320 | tf_op jit(solution)/shard_map/ppermute | solution.py:586
  644.9 7.4 %collective-permute-done.104 = bf16[272,1024]{1,0:T(8,128)(2,1)S(1)} collective-permute-done((bf16[272,1024]{1,0:T(8,128)(2,1)S(1)}, bf16[272,1024]{1,0:T(8,128)(2,1)S(1)}, u32[]{:S(2)}, u32[]{:S(2)}) %collective-permute-start.104) | collective-permute-done | bytes 557088 | tf_op jit(solution)/shard_map/ppermute | solution.py:586
  657.4 5.7 collective-permute-done.107
  (668 shorter events, 394.0 us)
Async XLA Ops:
  3.7 27.7 %collective-permute-start = (bf16[256,1024]{1,0:T(8,128)(2,1)}, bf16[256,1024]{1,0:T(8,128)(2,1)}, u32[]{:S(2)}, u32[]{:S(2)}) collective-permute-start(bf16[256,1024]{1,0:T(8,128)(2,1)} %get-tuple-element.294.refs_1_), channel_id=1, source_target_pairs={{0,8},{8,16},{16,24},{24,28},{28,20},{20,12},{12,4},{4,0},{1,9},{9... | collective-permute-start | bytes 1572872 | tf_op jit(solution)/shard_map/ppermute | solution.py:586
  6.7 24.7 %collective-permute-start.1 = (bf16[256,1024]{1,0:T(8,128)(2,1)}, bf16[256,1024]{1,0:T(8,128)(2,1)}, u32[]{:S(2)}, u32[]{:S(2)}) collective-permute-start(bf16[256,1024]{1,0:T(8,128)(2,1)} %get-tuple-element.294.refs_1_), channel_id=1, source_target_pairs={{8,0},{16,8},{24,16},{28,24},{20,28},{12,20},{4,12},{0,4},{9,1},{1... | collective-permute-start | bytes 1572872 | tf_op jit(solution)/shard_map/ppermute | solution.py:590
  6.7 26.7 %collective-permute-start.2 = (bf16[256,1024]{1,0:T(8,128)(2,1)}, bf16[256,1024]{1,0:T(8,128)(2,1)}, u32[]{:S(2)}, u32[]{:S(2)}) collective-permute-start(bf16[256,1024]{1,0:T(8,128)(2,1)} %get-tuple-element.298.refs_9_), channel_id=1, source_target_pairs={{0,8},{8,16},{16,24},{24,28},{28,20},{20,12},{12,4},{4,0},{1,9},{9... | collective-permute-start | bytes 1572872 | tf_op jit(solution)/shard_map/ppermute | solution.py:586
  8.7 24.7 %collective-permute-start.3 = (bf16[256,1024]{1,0:T(8,128)(2,1)}, bf16[256,1024]{1,0:T(8,128)(2,1)}, u32[]{:S(2)}, u32[]{:S(2)}) collective-permute-start(bf16[256,1024]{1,0:T(8,128)(2,1)} %get-tuple-element.298.refs_9_), channel_id=1, source_target_pairs={{8,0},{16,8},{24,16},{28,24},{20,28},{12,20},{4,12},{0,4},{9,1},{1... | collective-permute-start | bytes 1572872 | tf_op jit(solution)/shard_map/ppermute | solution.py:590
  33.5 24.3 %collective-permute-start.5 = (bf16[256,1024]{1,0:T(8,128)(2,1)}, bf16[256,1024]{1,0:T(8,128)(2,1)}, u32[]{:S(2)}, u32[]{:S(2)}) collective-permute-start(bf16[256,1024]{1,0:T(8,128)(2,1)} %collective-permute-done.2.refs_16_), channel_id=1, source_target_pairs={{0,8},{8,16},{16,24},{24,28},{28,20},{20,12},{12,4},{4,0},{1,9},{9... | collective-permute-start | bytes 1572872 | tf_op jit(solution)/shard_map/ppermute | solution.py:586
  47.0 26.7 %collective-permute-start.13 = (bf16[256,1024]{1,0:T(8,128)(2,1)}, bf16[256,1024]{1,0:T(8,128)(2,1)S(1)}, u32[]{:S(2)}, u32[]{:S(2)}) collective-permute-start(bf16[256,1024]{1,0:T(8,128)(2,1)} %collective-permute-done.8.refs_7_), channel_id=1, source_target_pairs={{0,8},{8,16},{16,24},{24,28},{28,20},{20,12},{12,4},{4,0},{1,9},{9... | collective-permute-start | bytes 1572872 | tf_op jit(solution)/shard_map/ppermute | solution.py:586
  86.5 26.2 %collective-permute-start.15 = (bf16[256,896]{1,0:T(8,128)(2,1)S(1)}, bf16[256,896]{1,0:T(8,128)(2,1)}, u32[]{:S(2)}, u32[]{:S(2)}) collective-permute-start(bf16[256,896]{1,0:T(8,128)(2,1)S(1)} %slice.377.refs_1_), channel_id=1, source_target_pairs={{0,8},{8,16},{16,24},{24,28},{28,20},{20,12},{12,4},{4,0},{1,9},{9... | collective-permute-start | bytes 1376264 | tf_op jit(solution)/shard_map/ppermute | solution.py:586
  88.5 24.2 %collective-permute-start.16 = (bf16[256,896]{1,0:T(8,128)(2,1)S(1)}, bf16[256,896]{1,0:T(8,128)(2,1)}, u32[]{:S(2)}, u32[]{:S(2)}) collective-permute-start(bf16[256,896]{1,0:T(8,128)(2,1)S(1)} %slice.377.refs_1_), channel_id=1, source_target_pairs={{8,0},{16,8},{24,16},{28,24},{20,28},{12,20},{4,12},{0,4},{9,1},{1... | collective-permute-start | bytes 1376264 | tf_op jit(solution)/shard_map/ppermute | solution.py:590
  122.0 23.5 %collective-permute-start.24 = (bf16[256,1024]{1,0:T(8,128)(2,1)}, bf16[256,1024]{1,0:T(8,128)(2,1)}, u32[]{:S(2)}, u32[]{:S(2)}) collective-permute-start(bf16[256,1024]{1,0:T(8,128)(2,1)} %collective-permute-done.21.refs_16_.refs_24_), channel_id=1, source_target_pairs={{0,8},{8,16},{16,24},{24,28},{28,20},{20,12},{12,4},{4,0},{1,9},{9... | collective-permute-start | bytes 1572872 | tf_op jit(solution)/shard_map/ppermute | solution.py:586
  145.5 27.3 %collective-permute-start.27 = (bf16[256,1024]{1,0:T(8,128)(2,1)}, bf16[256,1024]{1,0:T(8,128)(2,1)}, u32[]{:S(2)}, u32[]{:S(2)}) collective-permute-start(bf16[256,1024]{1,0:T(8,128)(2,1)} %collective-permute-done.24.refs_15_.refs_23_), channel_id=1, source_target_pairs={{0,8},{8,16},{16,24},{24,28},{28,20},{20,12},{12,4},{4,0},{1,9},{9... | collective-permute-start | bytes 1572872 | tf_op jit(solution)/shard_map/ppermute | solution.py:586
  182.8 27.8 %collective-permute-start.34 = (bf16[256,1408]{1,0:T(8,128)(2,1)S(1)}, bf16[256,1408]{1,0:T(8,128)(2,1)}, u32[]{:S(2)}, u32[]{:S(2)}) collective-permute-start(bf16[256,1408]{1,0:T(8,128)(2,1)S(1)} %copy-done.66), channel_id=1, source_target_pairs={{0,8},{8,16},{16,24},{24,28},{28,20},{20,12},{12,4},{4,0},{1,9},{9... | collective-permute-start | bytes 2162696 | tf_op jit(solution)/shard_map/ppermute | solution.py:586
  227.1 25.3 %collective-permute-start.43 = (bf16[256,2048]{1,0:T(8,128)(2,1)S(1)}, bf16[256,2048]{1,0:T(8,128)(2,1)S(1)}, u32[]{:S(2)}, u32[]{:S(2)}) collective-permute-start(bf16[256,2048]{1,0:T(8,128)(2,1)S(1)} %convert_element_type.598), channel_id=1, source_target_pairs={{0,2},{1,3},{2,0},{3,1},{4,6},{5,7},{6,4},{7,5},{8,10},{9,11},{10,... | collective-permute-start | bytes 3145736 | tf_op jit(solution)/shard_map/ppermute | solution.py:934
  231.2 31.3 %collective-permute-start.44 = (bf16[256,1408]{1,0:T(8,128)(2,1)}, bf16[256,1408]{1,0:T(8,128)(2,1)}, u32[]{:S(2)}, u32[]{:S(2)}) collective-permute-start(bf16[256,1408]{1,0:T(8,128)(2,1)} %collective-permute-done.34.refs_8_), channel_id=1, source_target_pairs={{0,8},{8,16},{16,24},{24,28},{28,20},{20,12},{12,4},{4,0},{1,9},{9... | collective-permute-start | bytes 2162696 | tf_op jit(solution)/shard_map/ppermute | solution.py:586
  231.6 31.1 %collective-permute-start.45 = (bf16[256,1408]{1,0:T(8,128)(2,1)}, bf16[256,1408]{1,0:T(8,128)(2,1)}, u32[]{:S(2)}, u32[]{:S(2)}) collective-permute-start(bf16[256,1408]{1,0:T(8,128)(2,1)} %collective-permute-done.35.refs_2_), channel_id=1, source_target_pairs={{8,0},{16,8},{24,16},{28,24},{20,28},{12,20},{4,12},{0,4},{9,1},{1... | collective-permute-start | bytes 2162696 | tf_op jit(solution)/shard_map/ppermute | solution.py:590
  266.7 31.5 %collective-permute-start.46 = (bf16[256,1408]{1,0:T(8,128)(2,1)}, bf16[256,1408]{1,0:T(8,128)(2,1)S(1)}, u32[]{:S(2)}, u32[]{:S(2)}) collective-permute-start(bf16[256,1408]{1,0:T(8,128)(2,1)} %copy-done.113), channel_id=1, source_target_pairs={{0,8},{8,16},{16,24},{24,28},{28,20},{20,12},{12,4},{4,0},{1,9},{9... | collective-permute-start | bytes 2162696 | tf_op jit(solution)/shard_map/ppermute | solution.py:586
  268.8 30.5 %collective-permute-start.47 = (bf16[256,1408]{1,0:T(8,128)(2,1)}, bf16[256,1408]{1,0:T(8,128)(2,1)}, u32[]{:S(2)}, u32[]{:S(2)}) collective-permute-start(bf16[256,1408]{1,0:T(8,128)(2,1)} %copy-done.114), channel_id=1, source_target_pairs={{8,0},{16,8},{24,16},{28,24},{20,28},{12,20},{4,12},{0,4},{9,1},{1... | collective-permute-start | bytes 2162696 | tf_op jit(solution)/shard_map/ppermute | solution.py:590
  357.9 32.0 %collective-permute-start.61 = (bf16[256,1408]{1,0:T(8,128)(2,1)S(1)}, bf16[256,1408]{1,0:T(8,128)(2,1)S(1)}, u32[]{:S(2)}, u32[]{:S(2)}) collective-permute-start(bf16[256,1408]{1,0:T(8,128)(2,1)S(1)} %get-tuple-element.691), channel_id=1, source_target_pairs={{0,8},{8,16},{16,24},{24,28},{28,20},{20,12},{12,4},{4,0},{1,9},{9... | collective-permute-start | bytes 2162696 | tf_op jit(solution)/shard_map/ppermute | solution.py:586
  358.7 32.0 %collective-permute-start.62 = (bf16[256,1408]{1,0:T(8,128)(2,1)S(1)}, bf16[256,1408]{1,0:T(8,128)(2,1)S(1)}, u32[]{:S(2)}, u32[]{:S(2)}) collective-permute-start(bf16[256,1408]{1,0:T(8,128)(2,1)S(1)} %get-tuple-element.690), channel_id=1, source_target_pairs={{8,0},{16,8},{24,16},{28,24},{20,28},{12,20},{4,12},{0,4},{9,1},{1... | collective-permute-start | bytes 2162696 | tf_op jit(solution)/shard_map/ppermute | solution.py:590
  375.6 29.7 %collective-permute-start.58 = (bf16[256,1408]{1,0:T(8,128)(2,1)S(1)}, bf16[256,1408]{1,0:T(8,128)(2,1)S(1)}, u32[]{:S(2)}, u32[]{:S(2)}) collective-permute-start(bf16[256,1408]{1,0:T(8,128)(2,1)S(1)} %get-tuple-element.687), channel_id=1, source_target_pairs={{0,8},{8,16},{16,24},{24,28},{28,20},{20,12},{12,4},{4,0},{1,9},{9... | collective-permute-start | bytes 2162696 | tf_op jit(solution)/shard_map/ppermute | solution.py:586
  376.4 29.8 %collective-permute-start.59 = (bf16[256,1408]{1,0:T(8,128)(2,1)S(1)}, bf16[256,1408]{1,0:T(8,128)(2,1)S(1)}, u32[]{:S(2)}, u32[]{:S(2)}) collective-permute-start(bf16[256,1408]{1,0:T(8,128)(2,1)S(1)} %get-tuple-element.686), channel_id=1, source_target_pairs={{8,0},{16,8},{24,16},{28,24},{20,28},{12,20},{4,12},{0,4},{9,1},{1... | collective-permute-start | bytes 2162696 | tf_op jit(solution)/shard_map/ppermute | solution.py:590
  377.8 28.3 %collective-permute-start.60 = (bf16[256,2048]{1,0:T(8,128)(2,1)S(1)}, bf16[256,2048]{1,0:T(8,128)(2,1)S(1)}, u32[]{:S(2)}, u32[]{:S(2)}) collective-permute-start(bf16[256,2048]{1,0:T(8,128)(2,1)S(1)} %convert_element_type.615), channel_id=1, source_target_pairs={{0,2},{1,3},{2,0},{3,1},{4,6},{5,7},{6,4},{7,5},{8,10},{9,11},{10,... | collective-permute-start | bytes 3145736 | tf_op jit(solution)/shard_map/ppermute | solution.py:934
  392.4 28.4 %collective-permute-start.65 = (bf16[256,1408]{1,0:T(8,128)(2,1)S(1)}, bf16[256,1408]{1,0:T(8,128)(2,1)S(1)}, u32[]{:S(2)}, u32[]{:S(2)}) collective-permute-start(bf16[256,1408]{1,0:T(8,128)(2,1)S(1)} %get-tuple-element.689), channel_id=1, source_target_pairs={{0,8},{8,16},{16,24},{24,28},{28,20},{20,12},{12,4},{4,0},{1,9},{9... | collective-permute-start | bytes 2162696 | tf_op jit(solution)/shard_map/ppermute | solution.py:586
  393.1 28.5 %collective-permute-start.66 = (bf16[256,1408]{1,0:T(8,128)(2,1)S(1)}, bf16[256,1408]{1,0:T(8,128)(2,1)S(1)}, u32[]{:S(2)}, u32[]{:S(2)}) collective-permute-start(bf16[256,1408]{1,0:T(8,128)(2,1)S(1)} %get-tuple-element.688), channel_id=1, source_target_pairs={{8,0},{16,8},{24,16},{28,24},{20,28},{12,20},{4,12},{0,4},{9,1},{1... | collective-permute-start | bytes 2162696 | tf_op jit(solution)/shard_map/ppermute | solution.py:590
  411.3 24.6 %collective-permute-start.63 = (bf16[256,1408]{1,0:T(8,128)(2,1)}, bf16[256,1408]{1,0:T(8,128)(2,1)S(1)}, u32[]{:S(2)}, u32[]{:S(2)}) collective-permute-start(bf16[256,1408]{1,0:T(8,128)(2,1)} %get-tuple-element.685), channel_id=1, source_target_pairs={{0,8},{8,16},{16,24},{24,28},{28,20},{20,12},{12,4},{4,0},{1,9},{9... | collective-permute-start | bytes 2162696 | tf_op jit(solution)/shard_map/ppermute | solution.py:586
  411.9 24.4 %collective-permute-start.64 = (bf16[256,1408]{1,0:T(8,128)(2,1)}, bf16[256,1408]{1,0:T(8,128)(2,1)S(1)}, u32[]{:S(2)}, u32[]{:S(2)}) collective-permute-start(bf16[256,1408]{1,0:T(8,128)(2,1)} %get-tuple-element.684), channel_id=1, source_target_pairs={{8,0},{16,8},{24,16},{28,24},{20,28},{12,20},{4,12},{0,4},{9,1},{1... | collective-permute-start | bytes 2162696 | tf_op jit(solution)/shard_map/ppermute | solution.py:590
  445.3 23.9 %collective-permute-start.72 = (bf16[256,2048]{1,0:T(8,128)(2,1)S(1)}, bf16[256,2048]{1,0:T(8,128)(2,1)S(1)}, u32[]{:S(2)}, u32[]{:S(2)}) collective-permute-start(bf16[256,2048]{1,0:T(8,128)(2,1)S(1)} %convert_element_type.651), channel_id=1, source_target_pairs={{0,2},{1,3},{2,0},{3,1},{4,6},{5,7},{6,4},{7,5},{8,10},{9,11},{10,... | collective-permute-start | bytes 3145736 | tf_op jit(solution)/shard_map/ppermute | solution.py:934
  447.9 32.3 %collective-permute-start.75 = (bf16[256,896]{0,1:T(8,128)(2,1)S(1)}, bf16[256,896]{0,1:T(8,128)(2,1)S(1)}, u32[]{:S(2)}, u32[]{:S(2)}) collective-permute-start(bf16[256,896]{0,1:T(8,128)(2,1)S(1)} %get-tuple-element.473), channel_id=1, source_target_pairs={{0,8},{8,16},{16,24},{24,28},{28,20},{20,12},{12,4},{4,0},{1,9},{9... | collective-permute-start | bytes 1376264 | tf_op jit(solution)/shard_map/ppermute | solution.py:586
  454.0 26.3 %collective-permute-start.76 = (bf16[256,896]{0,1:T(8,128)(2,1)S(1)}, bf16[256,896]{0,1:T(8,128)(2,1)S(1)}, u32[]{:S(2)}, u32[]{:S(2)}) collective-permute-start(bf16[256,896]{0,1:T(8,128)(2,1)S(1)} %get-tuple-element.474), channel_id=1, source_target_pairs={{8,0},{16,8},{24,16},{28,24},{20,28},{12,20},{4,12},{0,4},{9,1},{1... | collective-permute-start | bytes 1376264 | tf_op jit(solution)/shard_map/ppermute | solution.py:590
  494.2 28.5 %collective-permute-start.79 = (bf16[256,1024]{0,1:T(8,128)(2,1)S(1)}, bf16[256,1024]{0,1:T(8,128)(2,1)S(1)}, u32[]{:S(2)}, u32[]{:S(2)}) collective-permute-start(bf16[256,1024]{0,1:T(8,128)(2,1)S(1)} %get-tuple-element.711), channel_id=1, source_target_pairs={{0,8},{8,16},{16,24},{24,28},{28,20},{20,12},{12,4},{4,0},{1,9},{9... | collective-permute-start | bytes 1572872 | tf_op jit(solution)/shard_map/ppermute | solution.py:586
  497.5 25.2 %collective-permute-start.80 = (bf16[256,1024]{0,1:T(8,128)(2,1)S(1)}, bf16[256,1024]{0,1:T(8,128)(2,1)S(1)}, u32[]{:S(2)}, u32[]{:S(2)}) collective-permute-start(bf16[256,1024]{0,1:T(8,128)(2,1)S(1)} %get-tuple-element.710), channel_id=1, source_target_pairs={{8,0},{16,8},{24,16},{28,24},{20,28},{12,20},{4,12},{0,4},{9,1},{1... | collective-permute-start | bytes 1572872 | tf_op jit(solution)/shard_map/ppermute | solution.py:590
  530.7 41.3 %collective-permute-start.95 = (bf16[256,896]{0,1:T(8,128)(2,1)}, bf16[256,896]{0,1:T(8,128)(2,1)}, u32[]{:S(2)}, u32[]{:S(2)}) collective-permute-start(bf16[256,896]{0,1:T(8,128)(2,1)} %add_convert_fusion.23), channel_id=1, source_target_pairs={{0,8},{8,16},{16,24},{24,28},{28,20},{20,12},{12,4},{4,0},{1,9},{9... | collective-permute-start | bytes 1376264 | tf_op jit(solution)/shard_map/ppermute | solution.py:586
  605.7 26.7 %collective-permute-start.100 = (bf16[256,2048]{1,0:T(8,128)(2,1)}, bf16[256,2048]{1,0:T(8,128)(2,1)}, u32[]{:S(2)}, u32[]{:S(2)}) collective-permute-start(bf16[256,2048]{1,0:T(8,128)(2,1)} %convert_element_type.718), channel_id=1, source_target_pairs={{0,2},{1,3},{2,0},{3,1},{4,6},{5,7},{6,4},{7,5},{8,10},{9,11},{10,... | collective-permute-start | bytes 3145736 | tf_op jit(solution)/shard_map/ppermute | solution.py:934
  (214 other events, 2739.4 us)
